TPU v7x, 128 devices: a whole 4x4x4 slice. The times are simulated.
128 devices in a mesh: patch: 64 (over x, y_hi, z, core), head: 2 (over y_lo).
Axes of the slice: x: 4, y: 4 (y_hi: 2, y_lo: 2; y = y_hi * 2 + y_lo), z: 4, core: 2. Of those that a mesh axis runs over, the one named last changes fastest.
Arguments:
- image: bfloat16 [8192, 3072], P(('patch', 'head')), may hold values from -6 to 6
- w_qkv: bfloat16 [3072, 3, 1792], P(None, None, 'head'), may hold values from -0.109375 to 0.109375
- qk_gain: float32 [2, 128], replicated, may hold values from 0.1 to 1.9
- stale_kv: bfloat16 [2, 8192, 1792], P(None, 'patch', 'head')
- text_kv: bfloat16 [2, 512, 1792], P(None, None, 'head'), may hold values from -6 to 6
- text_count: int32 [1], replicated, may hold values from 128 to 512
- row_offset: int32 [64], P('patch'), may hold values from 0 to 63, as said below
- w_out: bfloat16 [1792, 3072], P('head'), may hold values from -0.125 to 0.125
Outputs:
- mixed: bfloat16 [8192, 3072], P(('patch', 'head'))
- fresh_kv: bfloat16 [2, 8192, 1792], P(None, 'patch', 'head')
Inputs may be any that keep to these rules, and one draw needn't show every extreme that they name: `row_offset`: A permutation of 0, 1, 2, ...: each patch starts at a different multiple of 1.
All inputs are finite; a program needn't handle non-finite values.
Results may differ from a plain program's by a relative error of at most 0.015.
Values may be sent and summed in bfloat16 or wider, within the bound.
No kernel may reach another device: no remote copies, remote signals or barrier semaphores. Data moves between devices by JAX's collectives and lax.ppermute only.
A program may use at most 192 MiB of HBM per device.

v0:
```python
import jax
import jax.numpy as jnp
from jax import lax
from jax.sharding import PartitionSpec as P

D = 3072
HD = 128
COLS = 128


def rope_angles(rows, cols):
    first = HD // 8
    band = (HD - first) // 2
    omega = 10000.0 ** (-2.0 * jnp.arange(band // 2, dtype=jnp.float32) / band)
    zeros = jnp.zeros((rows.shape[0], first // 2), jnp.float32)
    return jnp.concatenate(
        [zeros, rows[:, None] * omega[None, :], cols[:, None] * omega[None, :]], axis=1
    )


def rotate(vectors, angles):
    count, heads = (vectors.shape[0], vectors.shape[1])
    pairs = vectors.reshape(count, heads, HD // 2, 2)
    cosine = jnp.cos(angles)[:, None, :]
    sine = jnp.sin(angles)[:, None, :]
    first = pairs[..., 0]
    second = pairs[..., 1]
    turned = jnp.stack([first * cosine - second * sine, first * sine + second * cosine], axis=-1)
    return turned.reshape(count, heads, HD)


def normalize(vectors, gain):
    return vectors * lax.rsqrt(jnp.mean(vectors * vectors, axis=-1, keepdims=True) + 1e-06) * gain


def attend_block(carry, queries, key_rows, value_rows, keep, scale):
    peak, total, weighted = carry
    scores = (
        jnp.einsum("qhd,khd->hqk", queries, key_rows, preferred_element_type=jnp.float32) * scale
    )
    scores = jnp.where(keep[None, None, :], scores, -jnp.inf)
    new_peak = jnp.maximum(peak, jnp.max(scores, axis=-1))
    factor = jnp.exp(peak - new_peak)
    raw = jnp.exp(scores - new_peak[..., None])
    total = total * factor + jnp.sum(raw, axis=-1)
    update = jnp.einsum(
        "hqk,khd->hqd", raw.astype(jnp.bfloat16), value_rows, preferred_element_type=jnp.float32
    )
    return (new_peak, total, weighted * factor[..., None] + update)


def body(image, w_qkv, qk_gain, stale_kv, text_kv, text_count, row_offset, w_out):
    patch_rows = lax.all_gather(image, "head", axis=0, tiled=True)
    tok_count = patch_rows.shape[0]
    feature_cols = w_qkv.shape[2]
    local_heads = feature_cols // HD
    projected = jnp.dot(
        patch_rows, w_qkv.reshape(D, 3 * feature_cols), preferred_element_type=jnp.float32
    )
    projected = projected.reshape(tok_count, 3, local_heads, HD)
    within = jnp.arange(tok_count, dtype=jnp.int32)
    rows = (row_offset[0] + within // COLS).astype(jnp.float32)
    cols = (within % COLS).astype(jnp.float32)
    angles = rope_angles(rows, cols)
    queries = rotate(normalize(projected[:, 0], qk_gain[0]), angles).astype(jnp.bfloat16)
    keys_new = rotate(normalize(projected[:, 1], qk_gain[1]), angles).astype(jnp.bfloat16)
    values_new = projected[:, 2].astype(jnp.bfloat16)
    fresh_kv = jnp.stack(
        [keys_new.reshape(tok_count, feature_cols), values_new.reshape(tok_count, feature_cols)]
    )
    scale = 1.0 / jnp.sqrt(jnp.float32(HD))
    text_slots = text_kv.shape[1]
    text_keys = text_kv[0].reshape(text_slots, local_heads, HD)
    text_values = text_kv[1].reshape(text_slots, local_heads, HD)
    first_keys = jnp.concatenate([text_keys, keys_new], axis=0)
    first_values = jnp.concatenate([text_values, values_new], axis=0)
    first_keep = jnp.concatenate(
        [jnp.arange(text_slots, dtype=jnp.int32) < text_count[0], jnp.ones((tok_count,), bool)]
    )
    start_carry = (
        jnp.full((local_heads, tok_count), -jnp.inf, jnp.float32),
        jnp.zeros((local_heads, tok_count), jnp.float32),
        jnp.zeros((local_heads, tok_count, HD), jnp.float32),
    )
    carry = attend_block(start_carry, queries, first_keys, first_values, first_keep, scale)
    own_start = lax.axis_index("patch") * tok_count
    gathered = lax.all_gather(stale_kv, "patch", axis=1, tiled=True)
    piece_rows = gathered.shape[1]
    row_ids = jnp.arange(piece_rows, dtype=jnp.int32)
    keep = jnp.logical_or(row_ids < own_start, row_ids >= own_start + tok_count)
    key_rows = gathered[0].reshape(piece_rows, local_heads, HD)
    value_rows = gathered[1].reshape(piece_rows, local_heads, HD)
    carry = attend_block(carry, queries, key_rows, value_rows, keep, scale)
    peak, total, weighted = carry
    attended = (
        jnp.transpose(weighted / total[..., None], (1, 0, 2))
        .reshape(tok_count, feature_cols)
        .astype(jnp.bfloat16)
    )
    mixed = lax.psum_scatter(
        jnp.dot(attended, w_out, preferred_element_type=jnp.float32).astype(jnp.bfloat16),
        "head",
        scatter_dimension=0,
        tiled=True,
    )
    return (mixed, fresh_kv)


def solution(mesh):
    placed = (
        P(("patch", "head"), None),
        P(None, None, "head"),
        P(),
        P(None, "patch", "head"),
        P(None, None, "head"),
        P(),
        P("patch"),
        P("head", None),
    )
    return jax.shard_map(
        body,
        mesh=mesh,
        in_specs=placed,
        out_specs=(P(("patch", "head"), None), P(None, "patch", "head")),
        check_vma=False,
    )
```

profile of v0, /device:TPU:1, one launch (start us, length us, event | category | flops | bytes accessed | tf_op | source)
XLA Modules:
  0.0 265.0 jit_solution(4090153903534855158)
XLA Ops:
  7.2 2.0 copy.22
  9.3 22.4 %copy.16 = bf16[3072,3,896]{0,2,1:T(8,128)(2,1)} copy(bf16[3072,3,896]{2,0,1:T(8,128)(2,1)} %param.9) | data formatting | bytes 33030144 | tf_op args[1]
  31.7 0.1 mul.182
  33.2 0.1 mul.199
  33.3 11.2 %all_gather.6 = bf16[128,3072]{1,0:T(8,128)(2,1)S(1)} all-gather(bf16[64,3072]{1,0:T(8,128)(2,1)S(1)} %copy-done.2), channel_id=1, replica_groups=mesh['patch'=64,'head'=2] {'head'}, dimensions={0}, use_global_device_ids=true | all-gather | bytes 1179648 | tf_op jit(solution)/shard_map/all_gather | solution.py:53
  44.6 8.0 %fusion.32 = f32[128,3,7,128]{0,3,2,1:T(8,128)S(1)} fusion(bf16[3,7,128,3072]{3,2,1,0:T(8,128)(2,1)} %bitcast.70, bf16[128,3072]{1,0:T(8,128)(2,1)S(1)} %all_gather.6), kind=kOutput, calls=%fused_computation.34 | convolution fusion | flops 2113929216 | bytes 18677760 | tf_op jit(solution)/shard_map/dot_general | solution.py:57
  52.6 0.9 multiply_reduce_fusion
  53.5 0.1 broadcast_multiply_fusion.1
  53.5 0.2 fusion.36
  53.8 0.2 multiply_multiply_fusion
  54.0 0.6 multiply_subtract_fusion
  54.6 0.5 maximum_convert_fusion
  55.1 0.8 copy.19
  56.0 1.6 fusion.52
  57.6 1.3 copy.30
  58.9 2.3 copy.18
  61.2 0.5 copy.21
  61.7 1.2 multiply_multiply_fusion.1
  63.0 0.6 subtract_convert_fusion
  63.6 0.5 pad_maximum_fusion.1
  64.2 2.0 fusion.9
  66.2 1.4 copy-done
  67.6 0.6 fusion.10
  68.2 99.7 %all-gather.2.cloned.1.call-done = bf16[2,8192,896]{1,2,0:T(8,128)(2,1)} async-done(((bf16[2,128,896]{1,2,0:T(8,128)(2,1)}), bf16[2,8192,896]{1,2,0:T(8,128)(2,1)}) %all-gather.2.cloned.1.call-update) | async-done | bytes 29360144 | tf_op jit(solution)/shard_map/all_gather | solution.py:87
  167.9 21.6 %fusion.51 = (bf16[1,8192,896]{1,2,0:T(8,128)(2,1)}, bf16[1,8192,896]{1,2,0:T(8,128)(2,1)}) fusion(bf16[2,8192,896]{1,2,0:T(8,128)(2,1)} %all-gather.2.cloned.1.call-done), kind=kLoop, calls=%fused_computation.84 | loop fusion | bytes 58720256 | tf_op jit(solution)/shard_map/slice | solution.py:91
  189.5 15.0 %fusion = (f32[7,128]{1,0:T(8,128)S(1)}, f32[7,128,8192]{2,1,0:T(8,128)}) fusion(pred[8192]{0:T(1024)(128)(4,1)S(1)} %fusion.34, bf16[128,7,128]{0,2,1:T(8,128)(2,1)S(1)} %bitcast.80, bf16[8192,7,128]{0,2,1:T(8,128)(2,1)} %bitcast.69), kind=kOutput, calls=%fused_computation.2 | convolution fusion | flops 1901067392 | bytes 44281344 | tf_op jit(solution)/shard_map/qhd,khd->hqk/dot_general | solution.py:39
  204.6 13.4 %fusion.1 = f32[7,128]{1,0:T(8,128)S(1)} fusion(f32[7,128,8192]{2,1,0:T(8,128)} %get-tuple-element.28, f32[7,128]{1,0:T(8,128)S(1)} %max.18, pred[8192]{0:T(1024)(128)(4,1)S(1)} %fusion.34), kind=kLoop, calls=%fused_computation.3 | loop fusion | flops 29359232 | bytes 29375488 | tf_op jit(solution)/shard_map/reduce_sum | solution.py:45
  218.0 16.7 %fusion.16 = f32[128,7,128]{0,2,1:T(8,128)S(1)} fusion(bf16[8192,7,128]{0,2,1:T(8,128)(2,1)} %bitcast.71, f32[7,128,8192]{2,1,0:T(8,128)} %get-tuple-element.28, f32[7,128]{1,0:T(8,128)S(1)} %max.18, pred[8192]{0:T(1024)(128)(4,1)S(1)} %fusion.34), kind=kOutput, calls=%fused_computation.21 | convolution fusion | flops 1908408320 | bytes 44510720 | tf_op jit(solution)/shard_map/hqk,khd->hqd/dot_general | solution.py:46
  234.7 0.8 fusion.19
  235.6 1.9 convolution_convert_fusion
  237.6 1.0 copy.25
  238.5 19.6 %reduce-scatter.2.cloned.1.call-done = bf16[64,3072]{1,0:T(8,128)(2,1)} async-done(((bf16[128,3072]{1,0:T(8,128)(2,1)}), bf16[64,3072]{1,0:T(8,128)(2,1)}) %reduce-scatter.2.cloned.1.call-update) | async-done | bytes 393232 | tf_op jit(solution)/shard_map/reduce_scatter | solution.py:100
  (30 shorter events, 0.3 us)
Async XLA Ops:
  7.2 160.7 %all-gather.2.cloned.1.call-start = ((), (), s32[]{:S(2)}) async-start(), calls=%async_computation.1 | async-start | bytes 29818880 | tf_op jit(solution)/shard_map/all_gather | solution.py:87
  9.2 248.9 %reduce-scatter.2.cloned.1.call-start = ((), (), s32[]{:S(2)}) async-start(), calls=%async_computation.2 | async-start | bytes 1179648 | tf_op jit(solution)/shard_map/reduce_scatter | solution.py:100
  9.3 22.4 %copy-start.3 = (f32[2,128]{1,0:T(2,128)S(1)}, f32[2,128]{1,0:T(2,128)}, u32[]{:S(2)}) copy-start(f32[2,128]{1,0:T(2,128)} %param.10) | copy-start | bytes 3076
  9.3 24.0 %copy-start.2 = (bf16[64,3072]{1,0:T(8,128)(2,1)S(1)}, bf16[64,3072]{1,0:T(8,128)(2,1)}, u32[]{:S(2)}) copy-start(bf16[64,3072]{1,0:T(8,128)(2,1)} %param.8) | copy-start | bytes 1179652
  66.1 1.4 copy-start
  217.9 17.6 %slice-start = ((s8[5505024]{0:T(1024)(128)(4,1)}), s8[4194304]{0:T(1024)(128)(4,1)S(1)}, s32[]{:S(2)}) async-start(s8[5505024]{0:T(1024)(128)(4,1)} %bitcast.72), calls=%async_computation.3 | async-start | bytes 8388608
  217.9 16.8 %copy-start.1 = (f32[7,128,640]{2,1,0:T(8,128)S(1)}, f32[7,128,640]{2,1,0:T(8,128)}, u32[]{:S(2)}) copy-start(f32[7,128,640]{2,1,0:T(8,128)} %copy-done) | copy-start | bytes 6881284
  218.0 17.6 %slice-start.1 = ((s8[5505024]{0:T(1024)(128)(4,1)}), s8[1310720]{0:T(1024)(128)(4,1)S(1)}, s32[]{:S(2)}) async-start(s8[5505024]{0:T(1024)(128)(4,1)} %bitcast.72), calls=%async_computation.4 | async-start | bytes 2621440
Sparse Core Ops, SparseCore 0:
  11.7 156.1 all-gather.1
  237.6 20.4 reduce-scatter.1
where the time goes:
time: 266 us; the launch traced here: 265 us
  waiting for transfers between devices  119 us (45%)
  local copies, waits for them, and re-layouts  55.4 us (21%)
  matrix products  44.5 us (17%)
  other arithmetic  18.9 us (7%)
  between operations  15.6 us (6%)
  blocking collectives  11.2 us (4%)
    all_gather x1, waiting for transfers between devices, body(): gathered = lax.all_gather(stale_kv, 'patch', axis=1, tiled=True)  99.7 us
    unnamed x16, local copies, waits for them, and re-layouts  28.1 us
    slice x1, local copies, waits for them, and re-layouts, body(): key_rows = gathered[0].reshape(piece_rows, local_heads, HD)  21.6 us
    reduce_scatter x1, waiting for transfers between devices, body(): lax.psum_scatter(jnp.dot(attended, w_out, preferred_element_type=jnp.floa...  19.6 us
    dot_general x2, matrix products, attend_block(): jnp.einsum('hqk,khd->hqd', raw.astype(jnp.bfloat16), value_rows, preferre...  17.5 us
    dot_general x2, matrix products, attend_block(): jnp.einsum('qhd,khd->hqk', queries, key_rows, preferred_element_type=jnp....  17 us
    reduce_sum x2, other arithmetic, attend_block(): total = total * factor + jnp.sum(raw, axis=-1)  14 us
    all_gather x1, blocking collectives, body(): patch_rows = lax.all_gather(image, 'head', axis=0, tiled=True)  11.2 us
  transfers between devices with their start and end apart: 2, of which 2 were waited for; matrix products, arithmetic and copies ran while one was open for 17% of the time, Pallas kernels for 0%

commit v1 on v0

v1 whole, which is shorter than its diff:
```python
import functools
import math

import jax
import jax.numpy as jnp
import numpy as np
from jax import lax
from jax.experimental import pallas as pl
from jax.experimental.pallas import tpu as pltpu
from jax.sharding import PartitionSpec as P

D = 3072
HD = 128
COLS = 128
HEADS = 7
MINE = 3
UNITS = 7
TOK = 128
FEAT = HEADS * HD
STEP = 512
SCALE2 = math.log2(math.e) / math.sqrt(HD)
F32 = jnp.float32
BF16 = jnp.bfloat16
VMEM_LIMIT = 48 * 1024 * 1024


def _place(x, y, z, c):
    return ((x * 2 + y) * 4 + z) * 2 + c


def _perm(move):
    pairs = []
    for p in range(64):
        x, y, z, c = p // 16, (p // 8) % 2, (p // 2) % 4, p % 2
        pairs.append((p, _place(*move(x, y, z, c))))
    return pairs


def _key_move(d):
    return lambda x, y, z, c: ((x + d) % 4, y, z, c) if c == 0 else (x, y, (z + d) % 4, c)


def _query_move(d):
    return lambda x, y, z, c: (x, y, (z + d) % 4, c) if c == 0 else ((x + d) % 4, y, z, c)


def _core_move(x, y, z, c):
    return (x, y, z, 1 - c)


def _y_move(x, y, z, c):
    return (x, 1 - y, z, c)


def move(array, how):
    return lax.ppermute(array, "patch", _perm(how))


def swap_heads(array):
    return lax.ppermute(array, "head", [(0, 1), (1, 0)])


def _turn(v, gain, cosine, sine):
    v = v * lax.rsqrt(jnp.mean(v * v, axis=-1, keepdims=True) + 1e-06) * gain
    lane = lax.broadcasted_iota(jnp.int32, v.shape, 1)
    other = jnp.where(lane % 2 == 0, pltpu.roll(v, HD - 1, 1), pltpu.roll(v, 1, 1))
    return (v * cosine + other * sine).astype(BF16)


def _tokens(place, own_ref, oth_ref, x_ref):
    h = place[1]
    half = own_ref.shape[0]
    x_ref[pl.ds(pl.multiple_of(h * half, half), half), :] = own_ref[...]
    x_ref[pl.ds(pl.multiple_of((1 - h) * half, half), half), :] = oth_ref[...]


def _query_kernel(place, own_ref, oth_ref, w_ref, gain_ref, cos_ref, sin_ref, qa_ref, qb_ref, x_ref, acc_ref):
    k = pl.program_id(0)
    _tokens(place, own_ref, oth_ref, x_ref)

    @pl.when(k == 0)
    def _():
        acc_ref[...] = jnp.zeros_like(acc_ref)

    acc_ref[...] += jnp.dot(x_ref[...], w_ref[0], preferred_element_type=F32)

    @pl.when(k == pl.num_programs(0) - 1)
    def _():
        for head in range(HEADS):
            q = _turn(acc_ref[:, head * HD : (head + 1) * HD], gain_ref[0:1, :], cos_ref[...], sin_ref[...])
            if head == MINE:
                qa_ref[MINE] = q
                continue
            low = head < MINE

            @pl.when(place[0] == (0 if low else 1))
            def _():
                qa_ref[head if low else head - MINE - 1] = q

            @pl.when(place[0] == (1 if low else 0))
            def _():
                qb_ref[head if low else head - MINE - 1] = q


def _kv_kernel(place, own_ref, oth_ref, w_ref, gain_ref, cos_ref, sin_ref, out_ref, x_ref, acc_ref):
    j = pl.program_id(0)
    k = pl.program_id(1)
    _tokens(place, own_ref, oth_ref, x_ref)

    @pl.when(k == 0)
    def _():
        acc_ref[...] = jnp.zeros_like(acc_ref)

    acc_ref[...] += jnp.dot(x_ref[...], w_ref[0], preferred_element_type=F32)

    @pl.when(k == pl.num_programs(1) - 1)
    def _():
        @pl.when(j == 0)
        def _():
            for head in range(HEADS):
                at = slice(head * HD, (head + 1) * HD)
                out_ref[0, :, at] = _turn(acc_ref[:, at], gain_ref[1:2, :], cos_ref[...], sin_ref[...])

        @pl.when(j == 1)
        def _():
            out_ref[0] = acc_ref[...].astype(BF16)


def project_queries(place, own, oth, w, gain, cosine, sine):
    half = own.shape[0]
    steps = D // STEP
    return pl.pallas_call(
        _query_kernel,
        grid_spec=pltpu.PrefetchScalarGridSpec(
            num_scalar_prefetch=1,
            grid=(steps,),
            in_specs=[
                pl.BlockSpec((half, STEP), lambda k, s: (0, k)),
                pl.BlockSpec((half, STEP), lambda k, s: (0, k)),
                pl.BlockSpec((1, STEP, FEAT), lambda k, s: (0, k, 0)),
                pl.BlockSpec((2, HD), lambda k, s: (0, 0)),
                pl.BlockSpec((TOK, HD), lambda k, s: (0, 0)),
                pl.BlockSpec((TOK, HD), lambda k, s: (0, 0)),
            ],
            out_specs=[
                pl.BlockSpec((MINE + 1, TOK, HD), lambda k, s: (0, 0, 0)),
                pl.BlockSpec((MINE, TOK, HD), lambda k, s: (0, 0, 0)),
            ],
            scratch_shapes=[pltpu.VMEM((TOK, STEP), BF16), pltpu.VMEM((TOK, FEAT), F32)],
        ),
        out_shape=[
            jax.ShapeDtypeStruct((MINE + 1, TOK, HD), BF16),
            jax.ShapeDtypeStruct((MINE, TOK, HD), BF16),
        ],
        compiler_params=pltpu.CompilerParams(vmem_limit_bytes=VMEM_LIMIT),
        name="query_projection",
    )(place, own, oth, w, gain, cosine, sine)


def project_keys(place, own, oth, w, gain, cosine, sine):
    half = own.shape[0]
    steps = D // STEP
    return pl.pallas_call(
        _kv_kernel,
        grid_spec=pltpu.PrefetchScalarGridSpec(
            num_scalar_prefetch=1,
            grid=(2, steps),
            in_specs=[
                pl.BlockSpec((half, STEP), lambda j, k, s: (0, k)),
                pl.BlockSpec((half, STEP), lambda j, k, s: (0, k)),
                pl.BlockSpec((1, STEP, FEAT), lambda j, k, s: (j + 1, k, 0)),
                pl.BlockSpec((2, HD), lambda j, k, s: (0, 0)),
                pl.BlockSpec((TOK, HD), lambda j, k, s: (0, 0)),
                pl.BlockSpec((TOK, HD), lambda j, k, s: (0, 0)),
            ],
            out_specs=pl.BlockSpec((1, TOK, FEAT), lambda j, k, s: (j, 0, 0)),
            scratch_shapes=[pltpu.VMEM((TOK, STEP), BF16), pltpu.VMEM((TOK, FEAT), F32)],
        ),
        out_shape=jax.ShapeDtypeStruct((2, TOK, FEAT), BF16),
        compiler_params=pltpu.CompilerParams(vmem_limit_bytes=VMEM_LIMIT),
        name="key_value_projection",
    )(place, own, oth, w, gain, cosine, sine)


def _head_of(u, c):
    low = jnp.where(u > MINE, u - MINE - 1, u)
    return jnp.where(u == MINE, MINE, low + (MINE + 1) * c)


def _slot_of(u, c):
    low = jnp.where(u > MINE, u - MINE - 1, u)
    return jnp.where(u == MINE, MINE * (1 - c), low + c)


def _scores(q, k):
    return lax.dot_general(q, k, (((1,), (1,)), ((), ())), preferred_element_type=F32)


def _fold(state, scores, values):
    peak = jnp.max(scores[0], axis=1, keepdims=True)
    for s in scores[1:]:
        peak = jnp.maximum(peak, jnp.max(s, axis=1, keepdims=True))
    if state is not None:
        peak = jnp.maximum(peak, state[0])
    total = None
    out = None
    for s, v in zip(scores, values, strict=True):
        raw = jnp.exp2((s - peak) * SCALE2)
        part = jnp.sum(raw, axis=1, keepdims=True)
        total = part if total is None else total + part
        upd = jnp.dot(raw.astype(BF16), v, preferred_element_type=F32)
        out = upd if out is None else out + upd
    if state is not None:
        factor = jnp.exp2((state[0] - peak) * SCALE2)
        total = total + state[1] * factor
        out = out + state[2] * factor
    return peak, total, out


def _pack(peak, total):
    lane = lax.broadcasted_iota(jnp.int32, (peak.shape[0], HD), 1)
    return jnp.where(lane < HD // 2, peak, total)


def _home_kernel(place, count, q_ref, text_ref, fresh_ref, sib_ref, pair_ref, acc_ref, stat_ref):
    u = pl.program_id(0)
    q = q_ref[0]
    own = u <= MINE
    text = _scores(q, text_ref[0])
    slot = lax.broadcasted_iota(jnp.int32, text.shape, 1)
    text = jnp.where(slot < count[0], text, -jnp.inf)
    fresh = jnp.where(own, fresh_ref[...], sib_ref[...])
    stale = jnp.where(own, pair_ref[:, TOK:], pair_ref[:, :TOK])
    peak, total, out = _fold(
        None,
        [text, _scores(q, fresh[0]), _scores(q, stale[0])],
        [text_ref[1], fresh[1], stale[1]],
    )
    acc_ref[0] = out
    stat_ref[0] = _pack(peak, total)


def attend_home(place, count, queries, text_kv, fresh, sibling, pair):
    text_slots = text_kv.shape[1]
    return pl.pallas_call(
        _home_kernel,
        grid_spec=pltpu.PrefetchScalarGridSpec(
            num_scalar_prefetch=2,
            grid=(UNITS,),
            in_specs=[
                pl.BlockSpec((1, TOK, HD), lambda u, s, n: (u, 0, 0)),
                pl.BlockSpec((2, text_slots, HD), lambda u, s, n: (0, 0, _head_of(u, s[0]))),
                pl.BlockSpec((2, TOK, HD), lambda u, s, n: (0, 0, _head_of(u, s[0]))),
                pl.BlockSpec((2, TOK, HD), lambda u, s, n: (0, 0, jnp.maximum(u - MINE - 1, 0))),
                pl.BlockSpec((2, 2 * TOK, HD), lambda u, s, n: (0, 0, _slot_of(u, s[0]))),
            ],
            out_specs=[
                pl.BlockSpec((1, TOK, HD), lambda u, s, n: (u, 0, 0)),
                pl.BlockSpec((1, TOK, HD), lambda u, s, n: (u, 0, 0)),
            ],
        ),
        out_shape=[jax.ShapeDtypeStruct((UNITS, TOK, HD), F32)] * 2,
        compiler_params=pltpu.CompilerParams(vmem_limit_bytes=VMEM_LIMIT),
        name="home_attention",
    )(place, count, queries, text_kv, fresh, sibling, pair)


def _near_kernel(place, q0, q1, q2, q3, acc_in, stat_in, k0, k1, k2, k3, acc_ref, stat_ref, q_ref):
    q_ref[0:TOK] = q0[0]
    q_ref[TOK : 2 * TOK] = q1[0]
    q_ref[2 * TOK : 3 * TOK] = q2[0]
    q_ref[3 * TOK :] = q3[0]
    far = [k1, k2, k3]
    state = (stat_in[0, :, 0:1], stat_in[0, :, HD // 2 : HD // 2 + 1], acc_in[0])
    q = q_ref[0:TOK]
    peak, total, out = _fold(state, [_scores(q, k[0]) for k in far], [k[1] for k in far])
    acc_ref[0, 0:TOK] = out
    stat_ref[0, 0:TOK] = _pack(peak, total)
    q = q_ref[TOK:]
    blocks = [k0] + far
    peak, total, out = _fold(None, [_scores(q, k[0]) for k in blocks], [k[1] for k in blocks])
    acc_ref[0, TOK:] = out
    stat_ref[0, TOK:] = _pack(peak, total)


def _pair_spec():
    return pl.BlockSpec((2, 2 * TOK, HD), lambda u, s: (0, 0, _slot_of(u, s[0])))


def _unit_spec(rows=TOK):
    return pl.BlockSpec((1, rows, HD), lambda u, s: (u, 0, 0))


def attend_near(place, queries, acc, stat, pairs):
    rows = 4 * TOK
    return pl.pallas_call(
        _near_kernel,
        grid_spec=pltpu.PrefetchScalarGridSpec(
            num_scalar_prefetch=1,
            grid=(UNITS,),
            in_specs=[_unit_spec()] * 6 + [_pair_spec()] * 4,
            out_specs=[_unit_spec(rows)] * 2,
            scratch_shapes=[pltpu.VMEM((rows, HD), BF16)],
        ),
        out_shape=[jax.ShapeDtypeStruct((UNITS, rows, HD), F32)] * 2,
        compiler_params=pltpu.CompilerParams(vmem_limit_bytes=VMEM_LIMIT),
        name="near_attention",
    )(place, *queries, acc, stat, *pairs)


def _far_kernel(place, q0, q1, q2, q3, acc_in, stat_in, k0, k1, k2, k3, o0, o1, o2, o3, q_ref):
    u = pl.program_id(0)
    q_ref[0:TOK] = q0[0]
    q_ref[TOK : 2 * TOK] = q1[0]
    q_ref[2 * TOK : 3 * TOK] = q2[0]
    q_ref[3 * TOK :] = q3[0]
    blocks = [k0, k1, k2, k3]
    state = (stat_in[0, :, 0:1], stat_in[0, :, HD // 2 : HD // 2 + 1], acc_in[0])
    q = q_ref[...]
    peak, total, out = _fold(state, [_scores(q, k[0]) for k in blocks], [k[1] for k in blocks])
    out = (out / total).astype(BF16)
    level = peak * SCALE2 + jnp.log2(total)
    high = level.astype(BF16).astype(F32)
    middle = (level - high).astype(BF16).astype(F32)
    low = level - high - middle
    lane = lax.broadcasted_iota(jnp.int32, (4 * TOK, HD), 1)
    mark = jnp.where(
        lane == u, high, jnp.where(lane == u + 16, middle, jnp.where(lane == u + 32, low, 0.0))
    ).astype(BF16)
    for i, o in enumerate((o0, o1, o2, o3)):
        at = slice(i * TOK, (i + 1) * TOK)
        o[u] = out[at]

        @pl.when(u == 0)
        def _():
            o[UNITS] = mark[at]

        @pl.when(u > 0)
        def _():
            o[UNITS] += mark[at]


def attend_far(place, queries, acc, stat, pairs):
    rows = 4 * TOK
    return pl.pallas_call(
        _far_kernel,
        grid_spec=pltpu.PrefetchScalarGridSpec(
            num_scalar_prefetch=1,
            grid=(UNITS,),
            in_specs=[_unit_spec()] * 4 + [_unit_spec(rows)] * 2 + [_pair_spec()] * 4,
            out_specs=[pl.BlockSpec((UNITS + 1, TOK, HD), lambda u, s: (0, 0, 0))] * 4,
            scratch_shapes=[pltpu.VMEM((rows, HD), BF16)],
        ),
        out_shape=[jax.ShapeDtypeStruct((UNITS + 1, TOK, HD), BF16)] * 4,
        compiler_params=pltpu.CompilerParams(vmem_limit_bytes=VMEM_LIMIT),
        name="far_attention",
    )(place, *queries, acc, stat, *pairs)


def _merge_kernel(p0, p1, p2, p3, mine_ref, sib_ref):
    parts = (p0, p1, p2, p3)
    levels = []
    for p in parts:
        mark = p[UNITS].astype(F32)
        levels.append(mark + pltpu.roll(mark, HD - 16, 1) + pltpu.roll(mark, HD - 32, 1))
    top = jnp.maximum(jnp.maximum(levels[0], levels[1]), jnp.maximum(levels[2], levels[3]))
    weights = [jnp.exp2(v - top) for v in levels]
    total = weights[0] + weights[1] + weights[2] + weights[3]
    weights = [w / total for w in weights]
    for u in range(UNITS):
        out = None
        for p, w in zip(parts, weights, strict=True):
            term = p[u].astype(F32) * w[:, u : u + 1]
            out = term if out is None else out + term
        if u <= MINE:
            mine_ref[u] = out.astype(BF16)
        else:
            sib_ref[u - MINE - 1] = out.astype(BF16)


def merge(parts):
    return pl.pallas_call(
        _merge_kernel,
        out_shape=[
            jax.ShapeDtypeStruct((MINE + 1, TOK, HD), BF16),
            jax.ShapeDtypeStruct((MINE, TOK, HD), BF16),
        ],
        compiler_params=pltpu.CompilerParams(vmem_limit_bytes=VMEM_LIMIT),
        name="merge_parts",
    )(*parts)


def _out_kernel(place, mine_ref, got_ref, w_ref, keep_ref, send_ref, a_ref):
    half = keep_ref.shape[0]

    @pl.when(pl.program_id(0) == 0)
    def _():
        a_ref[:, MINE * HD : (MINE + 1) * HD] = mine_ref[MINE]
        for i in range(MINE):
            low = slice(i * HD, (i + 1) * HD)
            high = slice((MINE + 1 + i) * HD, (MINE + 2 + i) * HD)

            @pl.when(place[0] == 0)
            def _():
                a_ref[:, low] = mine_ref[i]
                a_ref[:, high] = got_ref[i]

            @pl.when(place[0] == 1)
            def _():
                a_ref[:, low] = got_ref[i]
                a_ref[:, high] = mine_ref[i]

    out = jnp.dot(a_ref[...], w_ref[...], preferred_element_type=F32)

    @pl.when(place[1] == 0)
    def _():
        keep_ref[...] = out[:half]
        send_ref[...] = out[half:].astype(BF16)

    @pl.when(place[1] == 1)
    def _():
        keep_ref[...] = out[half:]
        send_ref[...] = out[:half].astype(BF16)


def project_out(place, mine, got, w_out):
    half = TOK // 2
    cut = 768
    return pl.pallas_call(
        _out_kernel,
        grid_spec=pltpu.PrefetchScalarGridSpec(
            num_scalar_prefetch=1,
            grid=(D // cut,),
            in_specs=[
                pl.BlockSpec((MINE + 1, TOK, HD), lambda n, s: (0, 0, 0)),
                pl.BlockSpec((MINE, TOK, HD), lambda n, s: (0, 0, 0)),
                pl.BlockSpec((FEAT, cut), lambda n, s: (0, n)),
            ],
            out_specs=[
                pl.BlockSpec((half, cut), lambda n, s: (0, n)),
                pl.BlockSpec((half, cut), lambda n, s: (0, n)),
            ],
            scratch_shapes=[pltpu.VMEM((TOK, FEAT), BF16)],
        ),
        out_shape=[
            jax.ShapeDtypeStruct((half, D), F32),
            jax.ShapeDtypeStruct((half, D), BF16),
        ],
        compiler_params=pltpu.CompilerParams(vmem_limit_bytes=VMEM_LIMIT),
        name="output_projection",
    )(place, mine, got, w_out)


def _bands():
    first = HD // 8
    band = (HD - first) // 2
    omega = np.repeat(10000.0 ** (-2.0 * np.arange(band // 2) / band), 2)
    along_rows = np.zeros((HD,))
    along_cols = np.zeros((HD,))
    along_rows[first : first + band] = omega
    along_cols[first + band :] = omega
    sign = np.where(np.arange(HD) % 2 == 0, -1.0, 1.0)
    return (v.astype(np.float32)[None, :] for v in (along_rows, along_cols, sign))


def body(image, w_qkv, qk_gain, stale_kv, text_kv, text_count, row_offset, w_out):
    core = lax.axis_index("patch") % 2
    place = jnp.stack([core, lax.axis_index("head")]).astype(jnp.int32)
    other_image = swap_heads(image)

    wide = (2, TOK, (MINE + 1) * HD)
    given = lax.dynamic_slice(stale_kv, (0, 0, (1 - core) * MINE * HD), wide)
    kept = lax.dynamic_slice(stale_kv, (0, 0, core * MINE * HD), wide)
    pair = jnp.concatenate([kept, move(given, _core_move)], axis=1)
    far_pair = move(pair, _y_move)
    near = [pair] + [move(pair, _key_move(d)) for d in (1, 3, 2)]
    far = [far_pair] + [move(far_pair, _key_move(d)) for d in (1, 3, 2)]

    within = jnp.arange(TOK, dtype=jnp.int32)
    rows = (row_offset[0] + within // COLS).astype(F32)[:, None]
    cols = (within % COLS).astype(F32)[:, None]
    along_rows, along_cols, sign = _bands()
    angles = rows * along_rows + cols * along_cols
    cosine = jnp.cos(angles)
    sine = jnp.sin(angles) * sign

    w = jnp.transpose(w_qkv, (1, 0, 2))
    q_mine, q_given = project_queries(place, image, other_image, w, qk_gain, cosine, sine)
    units = jnp.concatenate([q_mine, move(q_given, _core_move)], axis=0)
    queries = [units] + [move(units, _query_move(d)) for d in (1, 3, 2)]
    fresh_kv = project_keys(place, image, other_image, w, qk_gain, cosine, sine)
    fresh_given = lax.dynamic_slice(
        fresh_kv, (0, 0, (1 - core) * (MINE + 1) * HD), (2, TOK, MINE * HD)
    )
    sibling = move(fresh_given, _core_move)

    acc, stat = attend_home(place, text_count, units, text_kv, fresh_kv, sibling, pair)
    acc, stat = attend_near(place, queries, acc, stat, near)
    parts = attend_far(place, queries, acc, stat, far)
    back = [parts[0]] + [move(parts[i], _query_move(d)) for i, d in ((1, 3), (2, 1), (3, 2))]
    mine, given_back = merge(back)
    keep, send = project_out(place, mine, move(given_back, _core_move), w_out)
    mixed = (keep + swap_heads(send).astype(F32)).astype(BF16)
    return (mixed, fresh_kv)


def solution(mesh):
    placed = (
        P(("patch", "head"), None),
        P(None, None, "head"),
        P(),
        P(None, "patch", "head"),
        P(None, None, "head"),
        P(),
        P("patch"),
        P("head", None),
    )
    return jax.shard_map(
        body,
        mesh=mesh,
        in_specs=placed,
        out_specs=(P(("patch", "head"), None), P(None, "patch", "head")),
        check_vma=False,
    )
```

time: 266 us -> 121 us (0.45)
  waiting for transfers between devices: 119 us -> 26.5 us
  Pallas kernels: 0 us -> 59 us
  local copies, waits for them, and re-layouts: 55.4 us -> 2.11 us
  matrix products: 44.5 us -> 0 us
  starting transfers between devices: 0.08 us -> 28.7 us
  other arithmetic: 18.9 us -> 1.95 us
  between operations: 15.6 us -> 2.11 us
  blocking collectives: 11.2 us -> 0 us
    all_gather x1 -> x0, waiting for transfers between devices: 99.7 us -> none  [body(): gathered = lax.all_gather(stale_kv, 'patch', axis=1, tiled=True)]
    pallas_call x0 -> x7, Pallas kernels: none -> 59 us  [the longest x1 16.8 us: attend_far(): pl.pallas_call(_far_kernel, grid_spec=pltpu.PrefetchScalarGridSpec(num_sc...]
    dot_general x6 -> x0, matrix products: 44.5 us -> none  [the longest x2 17.5 us: attend_block(): jnp.einsum('hqk,khd->hqd', raw.astype(jnp.bfloat16), value_rows, preferre...]
    ppermute x0 -> x19, starting transfers between devices: none -> 28.7 us  [the longest x17 25.9 us: move(): return lax.ppermute(array, 'patch', _perm(how))]
    unnamed x16 -> x9, local copies, waits for them, and re-layouts: 28.1 us -> 0.03 us
    ppermute x0 -> x19, waiting for transfers between devices: none -> 26.5 us  [the longest x17 14.2 us: move(): return lax.ppermute(array, 'patch', _perm(how))]
    slice x5 -> x0, local copies, waits for them, and re-layouts: 23.8 us -> none  [the longest x1 21.6 us: body(): key_rows = gathered[0].reshape(piece_rows, local_heads, HD)]
    reduce_scatter x1 -> x0, waiting for transfers between devices: 19.6 us -> none  [body(): lax.psum_scatter(jnp.dot(attended, w_out, preferred_element_type=jnp.floa...]
  transfers between devices with their start and end apart: 2 -> 19, of which waited for: 2 -> 8; matrix products, arithmetic and copies ran while one was open for 17% -> 2% of each run, Pallas kernels for 0% -> 31%
where the time goes in v1:
time: 121 us; the launch traced here: 120 us
  Pallas kernels  59 us (49%)
  starting transfers between devices  28.7 us (24%)
  waiting for transfers between devices  26.5 us (22%)
  local copies, waits for them, and re-layouts  2.11 us (2%)
  between operations  2.11 us (2%)
  other arithmetic  1.95 us (2%)
    ppermute x17, starting transfers between devices, move(): return lax.ppermute(array, 'patch', _perm(how))  25.9 us
    pallas_call x1, Pallas kernels, attend_far(): pl.pallas_call(_far_kernel, grid_spec=pltpu.PrefetchScalarGridSpec(num_sc...  16.8 us
    ppermute x17, waiting for transfers between devices, move(): return lax.ppermute(array, 'patch', _perm(how))  14.2 us
    pallas_call x1, Pallas kernels, attend_near(): pl.pallas_call(_near_kernel, grid_spec=pltpu.PrefetchScalarGridSpec(num_s...  12.8 us
    ppermute x2, waiting for transfers between devices, swap_heads(): return lax.ppermute(array, 'head', [(0, 1), (1, 0)])  12.4 us
    pallas_call x1, Pallas kernels, project_keys(): pl.pallas_call(_kv_kernel, grid_spec=pltpu.PrefetchScalarGridSpec(num_sca...  12.3 us
    pallas_call x1, Pallas kernels, project_queries(): pl.pallas_call(_query_kernel, grid_spec=pltpu.PrefetchScalarGridSpec(num_...  6.87 us
    pallas_call x1, Pallas kernels, attend_home(): pl.pallas_call(_home_kernel, grid_spec=pltpu.PrefetchScalarGridSpec(num_s...  4.91 us
  transfers between devices with their start and end apart: 19, of which 8 were waited for; matrix products, arithmetic and copies ran while one was open for 2% of the time, Pallas kernels for 31%

profile of v1, /device:TPU:1, one launch (start us, length us, event | category | flops | bytes accessed | tf_op | source)
XLA Modules:
  0.0 120.4 jit_solution(13235683113008726178)
XLA Ops:
  0.7 1.1 constant_dynamic-slice_fusion.1
  1.8 1.5 %collective-permute-start.6 = (bf16[2,128,512]{2,1,0:T(8,128)(2,1)S(1)}, bf16[2,128,512]{2,1,0:T(8,128)(2,1)S(1)}, u32[]{:S(2)}, u32[]{:S(2)}) collective-permute-start(bf16[2,128,512]{2,1,0:T(8,128)(2,1)S(1)} %get-tuple-element.31), channel_id=1, source_target_pairs={{0,2},{2,0},{4,6},{6,4},{8,10},{10,8},{12,14},{14,12},{16,18},{18,... | collective-permute-start | bytes 786440 | tf_op jit(solution)/shard_map/ppermute | solution.py:56
  3.3 1.4 %collective-permute-start = (bf16[64,3072]{1,0:T(8,128)(2,1)}, bf16[64,3072]{1,0:T(8,128)(2,1)S(1)}, u32[]{:S(2)}, u32[]{:S(2)}) collective-permute-start(bf16[64,3072]{1,0:T(8,128)(2,1)} %own_ref.3), channel_id=1, source_target_pairs={{0,1},{1,0},{2,3},{3,2},{4,5},{5,4},{6,7},{7,6},{8,9},{9,8},{10,11... | collective-permute-start | bytes 1179656 | tf_op jit(solution)/shard_map/ppermute | solution.py:60
  5.4 1.0 sine_multiply_fusion
  6.5 1.7 %collective-permute-start.7 = (bf16[2,256,512]{2,1,0:T(8,128)(2,1)S(1)}, bf16[2,256,512]{2,1,0:T(8,128)(2,1)S(1)}, u32[]{:S(2)}, u32[]{:S(2)}) collective-permute-start(bf16[2,256,512]{2,1,0:T(8,128)(2,1)S(1)} %pad_maximum_fusion.pair_ref.k0), channel_id=1, source_target_pairs={{0,32},{2,6},{4,36},{6,10},{8,40},{10,14},{12,44},{14,2},{16,48},{... | collective-permute-start | bytes 1572872 | tf_op jit(solution)/shard_map/ppermute | solution.py:56
  8.2 2.6 %collective-permute-start.10 = (bf16[2,256,512]{2,1,0:T(8,128)(2,1)S(1)}, bf16[2,256,512]{2,1,0:T(8,128)(2,1)S(1)}, u32[]{:S(2)}, u32[]{:S(2)}) collective-permute-start(bf16[2,256,512]{2,1,0:T(8,128)(2,1)S(1)} %pad_maximum_fusion.pair_ref.k0), channel_id=1, source_target_pairs={{0,16},{2,18},{4,20},{6,22},{8,24},{10,26},{12,28},{14,30},{16,0},... | collective-permute-start | bytes 1572872 | tf_op jit(solution)/shard_map/ppermute | solution.py:56
  10.8 3.3 %collective-permute-done.oth_ref = bf16[64,3072]{1,0:T(8,128)(2,1)S(1)} collective-permute-done((bf16[64,3072]{1,0:T(8,128)(2,1)}, bf16[64,3072]{1,0:T(8,128)(2,1)S(1)}, u32[]{:S(2)}, u32[]{:S(2)}) %collective-permute-start) | collective-permute-done | bytes 393248 | tf_op jit(solution)/shard_map/ppermute | solution.py:60
  14.2 12.3 %key_value_projection.1.fresh_ref = bf16[2,128,896]{2,1,0:T(8,128)(2,1)} custom-call(s32[2]{0:T(128)S(1)} %pad_add_fusion.place, bf16[64,3072]{1,0:T(8,128)(2,1)S(1)} %copy-done.2, bf16[64,3072]{1,0:T(8,128)(2,1)S(1)} %collective-permute-done.oth_ref, bf16[3,3072,896]{2,1,0:T(8,128)(2,1)} %bitcast.5, f32[2,128]{1,0:T(2,128)S(1)} %copy-done.3, ...), custom_call_target="tpu_custom_call" | custom-call | tf_op jit(solution)/shard_map/key_value_projection/pallas_call | solution.py:163
  26.5 0.9 constant_dynamic-slice_fusion.2
  27.4 1.4 %collective-permute-start.5 = (bf16[2,128,384]{2,1,0:T(8,128)(2,1)S(1)}, bf16[2,128,384]{2,1,0:T(8,128)(2,1)S(1)}, u32[]{:S(2)}, u32[]{:S(2)}) collective-permute-start(bf16[2,128,384]{2,1,0:T(8,128)(2,1)S(1)} %constant_dynamic-slice_fusion.2), channel_id=1, source_target_pairs={{0,2},{2,0},{4,6},{6,4},{8,10},{10,8},{12,14},{14,12},{16,18},{18,... | collective-permute-start | bytes 589832 | tf_op jit(solution)/shard_map/ppermute | solution.py:56
  28.9 6.9 %query_projection.1 = (bf16[4,128,128]{2,1,0:T(8,128)(2,1)S(1)}, bf16[3,128,128]{2,1,0:T(8,128)(2,1)S(1)}) custom-call(s32[2]{0:T(128)S(1)} %pad_add_fusion.place, bf16[64,3072]{1,0:T(8,128)(2,1)S(1)} %copy-done.2, bf16[64,3072]{1,0:T(8,128)(2,1)S(1)} %collective-permute-done.oth_ref, bf16[3,3072,896]{2,1,0:T(8,128)(2,1)} %bitcast.6, ...), custom_call_target="tpu_custom_call" | custom-call | tf_op jit(solution)/shard_map/query_projection/pallas_call | solution.py:132
  35.9 1.2 %collective-permute-done.1 = bf16[3,128,128]{2,1,0:T(8,128)(2,1)S(1)} collective-permute-done((bf16[3,128,128]{2,1,0:T(8,128)(2,1)S(1)}, bf16[3,128,128]{2,1,0:T(8,128)(2,1)S(1)}, u32[]{:S(2)}, u32[]{:S(2)}) %collective-permute-start.1) | collective-permute-done | bytes 98336 | tf_op jit(solution)/shard_map/ppermute | solution.py:56
  37.1 1.4 %collective-permute-start.2 = (bf16[7,128,128]{2,1,0:T(8,128)(2,1)S(1)}, bf16[7,128,128]{2,1,0:T(8,128)(2,1)S(1)}, u32[]{:S(2)}, u32[]{:S(2)}) collective-permute-start(bf16[7,128,128]{2,1,0:T(8,128)(2,1)S(1)} %constant_dynamic-update-slice_fusion.q_ref.q0), channel_id=1, source_target_pairs={{0,4},{2,34},{4,8},{6,38},{8,12},{10,42},{12,0},{14,46},{16,20},{1... | collective-permute-start | bytes 688136 | tf_op jit(solution)/shard_map/ppermute | solution.py:56
  38.5 1.4 %collective-permute-start.3 = (bf16[7,128,128]{2,1,0:T(8,128)(2,1)S(1)}, bf16[7,128,128]{2,1,0:T(8,128)(2,1)S(1)}, u32[]{:S(2)}, u32[]{:S(2)}) collective-permute-start(bf16[7,128,128]{2,1,0:T(8,128)(2,1)S(1)} %constant_dynamic-update-slice_fusion.q_ref.q0), channel_id=1, source_target_pairs={{0,12},{2,98},{4,0},{6,102},{8,4},{10,106},{12,8},{14,110},{16,28}... | collective-permute-start | bytes 688136 | tf_op jit(solution)/shard_map/ppermute | solution.py:56
  39.9 1.6 %collective-permute-start.4 = (bf16[7,128,128]{2,1,0:T(8,128)(2,1)S(1)}, bf16[7,128,128]{2,1,0:T(8,128)(2,1)S(1)}, u32[]{:S(2)}, u32[]{:S(2)}) collective-permute-start(bf16[7,128,128]{2,1,0:T(8,128)(2,1)S(1)} %constant_dynamic-update-slice_fusion.q_ref.q0), channel_id=1, source_target_pairs={{0,8},{2,66},{4,12},{6,70},{8,0},{10,74},{12,4},{14,78},{16,24},{1... | collective-permute-start | bytes 688136 | tf_op jit(solution)/shard_map/ppermute | solution.py:56
  41.5 2.1 %collective-permute-done.2.q1 = bf16[7,128,128]{2,1,0:T(8,128)(2,1)S(1)} collective-permute-done((bf16[7,128,128]{2,1,0:T(8,128)(2,1)S(1)}, bf16[7,128,128]{2,1,0:T(8,128)(2,1)S(1)}, u32[]{:S(2)}, u32[]{:S(2)}) %collective-permute-start.2) | collective-permute-done | bytes 229408 | tf_op jit(solution)/shard_map/ppermute | solution.py:56
  43.6 3.8 %collective-permute-start.8 = (bf16[2,256,512]{2,1,0:T(8,128)(2,1)S(1)}, bf16[2,256,512]{2,1,0:T(8,128)(2,1)S(1)}, u32[]{:S(2)}, u32[]{:S(2)}) collective-permute-start(bf16[2,256,512]{2,1,0:T(8,128)(2,1)S(1)} %pad_maximum_fusion.pair_ref.k0), channel_id=1, source_target_pairs={{0,96},{2,14},{4,100},{6,2},{8,104},{10,6},{12,108},{14,10},{16,11... | collective-permute-start | bytes 1572872 | tf_op jit(solution)/shard_map/ppermute | solution.py:56
  48.0 2.9 %collective-permute-start.12 = (bf16[2,256,512]{2,1,0:T(8,128)(2,1)S(1)}, bf16[2,256,512]{2,1,0:T(8,128)(2,1)S(1)}, u32[]{:S(2)}, u32[]{:S(2)}) collective-permute-start(bf16[2,256,512]{2,1,0:T(8,128)(2,1)S(1)} %collective-permute-done.10.k0), channel_id=1, source_target_pairs={{0,96},{2,14},{4,100},{6,2},{8,104},{10,6},{12,108},{14,10},{16,11... | collective-permute-start | bytes 1572872 | tf_op jit(solution)/shard_map/ppermute | solution.py:56
  50.9 1.0 collective-permute-start.13
  52.5 4.9 %home_attention.1 = (f32[7,128,128]{2,1,0:T(8,128)S(1)}, f32[7,128,128]{2,1,0:T(8,128)S(1)}) custom-call(s32[2]{0:T(128)S(1)} %pad_add_fusion.place, s32[1]{0:T(128)S(6)} %copy.14.count, bf16[7,128,128]{2,1,0:T(8,128)(2,1)S(1)} %constant_dynamic-update-slice_fusion.q_ref.q0, bf16[2,512,896]{2,1,0:T(8,128)(2,1)S(1)} %copy-done.1, ...), custom_call_target="tpu_custom_call" | custom-call | tf_op jit(solution)/shard_map/home_attention/pallas_call | solution.py:245
  57.5 2.1 %collective-permute-done.8.k2 = bf16[2,256,512]{2,1,0:T(8,128)(2,1)S(1)} collective-permute-done((bf16[2,256,512]{2,1,0:T(8,128)(2,1)S(1)}, bf16[2,256,512]{2,1,0:T(8,128)(2,1)S(1)}, u32[]{:S(2)}, u32[]{:S(2)}) %collective-permute-start.8) | collective-permute-done | bytes 524320 | tf_op jit(solution)/shard_map/ppermute | solution.py:56
  59.5 12.8 %near_attention.1 = (f32[7,512,128]{2,1,0:T(8,128)S(1)}, f32[7,512,128]{2,1,0:T(8,128)}) custom-call(s32[2]{0:T(128)S(1)} %pad_add_fusion.place, bf16[7,128,128]{2,1,0:T(8,128)(2,1)S(1)} %constant_dynamic-update-slice_fusion.q_ref.q0, bf16[7,128,128]{2,1,0:T(8,128)(2,1)S(1)} %collective-permute-done.2.q1, ...), custom_call_target="tpu_custom_call" | custom-call | tf_op jit(solution)/shard_map/near_attention/pallas_call | solution.py:296
  72.3 16.8 %far_attention.1 = (bf16[8,128,128]{2,1,0:T(8,128)(2,1)S(1)}, bf16[8,128,128]{2,1,0:T(8,128)(2,1)S(1)}, bf16[8,128,128]{2,1,0:T(8,128)(2,1)S(1)}, bf16[8,128,128]{2,1,0:T(8,128)(2,1)S(1)}) custom-call(s32[2]{0:T(128)S(1)} %pad_add_fusion.place, bf16[7,128,128]{2,1,0:T(8,128)(2,1)S(1)} %constant_dynamic-update-slice_fusion.q_ref.q0, ...), custom_call_target="tpu_custom_call" | custom-call | tf_op jit(solution)/shard_map/far_attention/pallas_call | solution.py:345
  89.1 2.3 %collective-permute-start.14 = (bf16[8,128,128]{2,1,0:T(8,128)(2,1)S(1)}, bf16[8,128,128]{2,1,0:T(8,128)(2,1)S(1)}, u32[]{:S(2)}, u32[]{:S(2)}) collective-permute-start(bf16[8,128,128]{2,1,0:T(8,128)(2,1)S(1)} %get-tuple-element.23), channel_id=1, source_target_pairs={{0,12},{2,98},{4,0},{6,102},{8,4},{10,106},{12,8},{14,110},{16,28}... | collective-permute-start | bytes 786440 | tf_op jit(solution)/shard_map/ppermute | solution.py:56
  91.5 1.7 %collective-permute-start.16 = (bf16[8,128,128]{2,1,0:T(8,128)(2,1)S(1)}, bf16[8,128,128]{2,1,0:T(8,128)(2,1)S(1)}, u32[]{:S(2)}, u32[]{:S(2)}) collective-permute-start(bf16[8,128,128]{2,1,0:T(8,128)(2,1)S(1)} %get-tuple-element.25), channel_id=1, source_target_pairs={{0,8},{2,66},{4,12},{6,70},{8,0},{10,74},{12,4},{14,78},{16,24},{1... | collective-permute-start | bytes 786440 | tf_op jit(solution)/shard_map/ppermute | solution.py:56
  93.2 1.6 %collective-permute-done.14.p1 = bf16[8,128,128]{2,1,0:T(8,128)(2,1)S(1)} collective-permute-done((bf16[8,128,128]{2,1,0:T(8,128)(2,1)S(1)}, bf16[8,128,128]{2,1,0:T(8,128)(2,1)S(1)}, u32[]{:S(2)}, u32[]{:S(2)}) %collective-permute-start.14) | collective-permute-done | bytes 262176 | tf_op jit(solution)/shard_map/ppermute | solution.py:56
  94.8 6.2 %collective-permute-done.15.p2 = bf16[8,128,128]{2,1,0:T(8,128)(2,1)S(1)} collective-permute-done((bf16[8,128,128]{2,1,0:T(8,128)(2,1)S(1)}, bf16[8,128,128]{2,1,0:T(8,128)(2,1)S(1)}, u32[]{:S(2)}, u32[]{:S(2)}) %collective-permute-start.15) | collective-permute-done | bytes 262176 | tf_op jit(solution)/shard_map/ppermute | solution.py:56
  101.7 1.8 %collective-permute-start.17 = (bf16[3,128,128]{2,1,0:T(8,128)(2,1)S(1)}, bf16[3,128,128]{2,1,0:T(8,128)(2,1)S(1)}, u32[]{:S(2)}, u32[]{:S(2)}) collective-permute-start(bf16[3,128,128]{2,1,0:T(8,128)(2,1)S(1)} %get-tuple-element.27), channel_id=1, source_target_pairs={{0,2},{2,0},{4,6},{6,4},{8,10},{10,8},{12,14},{14,12},{16,18},{18,... | collective-permute-start | bytes 294920 | tf_op jit(solution)/shard_map/ppermute | solution.py:56
  103.6 0.9 collective-permute-done.17.got_ref
  104.5 4.7 %output_projection.1 = (f32[64,3072]{1,0:T(8,128)S(1)}, bf16[64,3072]{1,0:T(8,128)(2,1)S(1)}) custom-call(s32[2]{0:T(128)S(1)} %pad_add_fusion.place, bf16[4,128,128]{2,1,0:T(8,128)(2,1)S(1)} %get-tuple-element.26.mine_ref, bf16[3,128,128]{2,1,0:T(8,128)(2,1)S(1)} %collective-permute-done.17.got_ref, bf16[896,3072]{1,0:T(8,128)(2,1)} %w_ref.1), custom_call_target="tpu_custom_call" | custom-call | tf_op jit(solution)/shard_map/output_projection/pallas_call | solution.py:429
  109.2 1.4 %collective-permute-start.18 = (bf16[64,3072]{1,0:T(8,128)(2,1)S(1)}, bf16[64,3072]{1,0:T(8,128)(2,1)S(1)}, u32[]{:S(2)}, u32[]{:S(2)}) collective-permute-start(bf16[64,3072]{1,0:T(8,128)(2,1)S(1)} %get-tuple-element.29), channel_id=1, source_target_pairs={{0,1},{1,0},{2,3},{3,2},{4,5},{5,4},{6,7},{7,6},{8,9},{9,8},{10,11... | collective-permute-start | bytes 1179656 | tf_op jit(solution)/shard_map/ppermute | solution.py:60
  110.6 9.0 %collective-permute-done.18 = bf16[64,3072]{1,0:T(8,128)(2,1)S(1)} collective-permute-done((bf16[64,3072]{1,0:T(8,128)(2,1)S(1)}, bf16[64,3072]{1,0:T(8,128)(2,1)S(1)}, u32[]{:S(2)}, u32[]{:S(2)}) %collective-permute-start.18) | collective-permute-done | bytes 393248 | tf_op jit(solution)/shard_map/ppermute | solution.py:60
  (30 shorter events, 2.4 us)
Async XLA Ops:
  0.6 13.5 %copy-start.2 = (bf16[64,3072]{1,0:T(8,128)(2,1)S(1)}, bf16[64,3072]{1,0:T(8,128)(2,1)}, u32[]{:S(2)}) copy-start(bf16[64,3072]{1,0:T(8,128)(2,1)} %own_ref.3) | copy-start | bytes 1179652
  0.6 13.5 %copy-start.3 = (f32[2,128]{1,0:T(2,128)S(1)}, f32[2,128]{1,0:T(2,128)}, u32[]{:S(2)}) copy-start(f32[2,128]{1,0:T(2,128)} %gain_ref.3) | copy-start | bytes 3076
  1.8 4.7 %collective-permute-start.6 = (bf16[2,128,512]{2,1,0:T(8,128)(2,1)S(1)}, bf16[2,128,512]{2,1,0:T(8,128)(2,1)S(1)}, u32[]{:S(2)}, u32[]{:S(2)}) collective-permute-start(bf16[2,128,512]{2,1,0:T(8,128)(2,1)S(1)} %get-tuple-element.31), channel_id=1, source_target_pairs={{0,2},{2,0},{4,6},{6,4},{8,10},{10,8},{12,14},{14,12},{16,18},{18,... | collective-permute-start | bytes 786440 | tf_op jit(solution)/shard_map/ppermute | solution.py:56
  3.3 10.9 %collective-permute-start = (bf16[64,3072]{1,0:T(8,128)(2,1)}, bf16[64,3072]{1,0:T(8,128)(2,1)S(1)}, u32[]{:S(2)}, u32[]{:S(2)}) collective-permute-start(bf16[64,3072]{1,0:T(8,128)(2,1)} %own_ref.3), channel_id=1, source_target_pairs={{0,1},{1,0},{2,3},{3,2},{4,5},{5,4},{6,7},{7,6},{8,9},{9,8},{10,11... | collective-permute-start | bytes 1179656 | tf_op jit(solution)/shard_map/ppermute | solution.py:60
  6.5 44.4 %collective-permute-start.7 = (bf16[2,256,512]{2,1,0:T(8,128)(2,1)S(1)}, bf16[2,256,512]{2,1,0:T(8,128)(2,1)S(1)}, u32[]{:S(2)}, u32[]{:S(2)}) collective-permute-start(bf16[2,256,512]{2,1,0:T(8,128)(2,1)S(1)} %pad_maximum_fusion.pair_ref.k0), channel_id=1, source_target_pairs={{0,32},{2,6},{4,36},{6,10},{8,40},{10,14},{12,44},{14,2},{16,48},{... | collective-permute-start | bytes 1572872 | tf_op jit(solution)/shard_map/ppermute | solution.py:56
  8.2 39.2 %collective-permute-start.10 = (bf16[2,256,512]{2,1,0:T(8,128)(2,1)S(1)}, bf16[2,256,512]{2,1,0:T(8,128)(2,1)S(1)}, u32[]{:S(2)}, u32[]{:S(2)}) collective-permute-start(bf16[2,256,512]{2,1,0:T(8,128)(2,1)S(1)} %pad_maximum_fusion.pair_ref.k0), channel_id=1, source_target_pairs={{0,16},{2,18},{4,20},{6,22},{8,24},{10,26},{12,28},{14,30},{16,0},... | collective-permute-start | bytes 1572872 | tf_op jit(solution)/shard_map/ppermute | solution.py:56
  27.4 25.1 %copy-start = (bf16[2,128,896]{2,1,0:T(8,128)(2,1)S(1)}, bf16[2,128,896]{2,1,0:T(8,128)(2,1)}, u32[]{:S(2)}) copy-start(bf16[2,128,896]{2,1,0:T(8,128)(2,1)} %key_value_projection.1.fresh_ref) | copy-start | bytes 1376260
  27.4 25.1 %copy-start.1 = (bf16[2,512,896]{2,1,0:T(8,128)(2,1)S(1)}, bf16[2,512,896]{2,1,0:T(8,128)(2,1)}, u32[]{:S(2)}) copy-start(bf16[2,512,896]{2,1,0:T(8,128)(2,1)} %text_ref.1) | copy-start | bytes 5505028
  27.4 12.5 %collective-permute-start.5 = (bf16[2,128,384]{2,1,0:T(8,128)(2,1)S(1)}, bf16[2,128,384]{2,1,0:T(8,128)(2,1)S(1)}, u32[]{:S(2)}, u32[]{:S(2)}) collective-permute-start(bf16[2,128,384]{2,1,0:T(8,128)(2,1)S(1)} %constant_dynamic-slice_fusion.2), channel_id=1, source_target_pairs={{0,2},{2,0},{4,6},{6,4},{8,10},{10,8},{12,14},{14,12},{16,18},{18,... | collective-permute-start | bytes 589832 | tf_op jit(solution)/shard_map/ppermute | solution.py:56
  35.7 1.4 %collective-permute-start.1 = (bf16[3,128,128]{2,1,0:T(8,128)(2,1)S(1)}, bf16[3,128,128]{2,1,0:T(8,128)(2,1)S(1)}, u32[]{:S(2)}, u32[]{:S(2)}) collective-permute-start(bf16[3,128,128]{2,1,0:T(8,128)(2,1)S(1)} %get-tuple-element.17), channel_id=1, source_target_pairs={{0,2},{2,0},{4,6},{6,4},{8,10},{10,8},{12,14},{14,12},{16,18},{18,... | collective-permute-start | bytes 294920 | tf_op jit(solution)/shard_map/ppermute | solution.py:56
  37.1 6.4 %collective-permute-start.2 = (bf16[7,128,128]{2,1,0:T(8,128)(2,1)S(1)}, bf16[7,128,128]{2,1,0:T(8,128)(2,1)S(1)}, u32[]{:S(2)}, u32[]{:S(2)}) collective-permute-start(bf16[7,128,128]{2,1,0:T(8,128)(2,1)S(1)} %constant_dynamic-update-slice_fusion.q_ref.q0), channel_id=1, source_target_pairs={{0,4},{2,34},{4,8},{6,38},{8,12},{10,42},{12,0},{14,46},{16,20},{1... | collective-permute-start | bytes 688136 | tf_op jit(solution)/shard_map/ppermute | solution.py:56
  38.5 8.9 %collective-permute-start.3 = (bf16[7,128,128]{2,1,0:T(8,128)(2,1)S(1)}, bf16[7,128,128]{2,1,0:T(8,128)(2,1)S(1)}, u32[]{:S(2)}, u32[]{:S(2)}) collective-permute-start(bf16[7,128,128]{2,1,0:T(8,128)(2,1)S(1)} %constant_dynamic-update-slice_fusion.q_ref.q0), channel_id=1, source_target_pairs={{0,12},{2,98},{4,0},{6,102},{8,4},{10,106},{12,8},{14,110},{16,28}... | collective-permute-start | bytes 688136 | tf_op jit(solution)/shard_map/ppermute | solution.py:56
  39.9 8.1 %collective-permute-start.4 = (bf16[7,128,128]{2,1,0:T(8,128)(2,1)S(1)}, bf16[7,128,128]{2,1,0:T(8,128)(2,1)S(1)}, u32[]{:S(2)}, u32[]{:S(2)}) collective-permute-start(bf16[7,128,128]{2,1,0:T(8,128)(2,1)S(1)} %constant_dynamic-update-slice_fusion.q_ref.q0), channel_id=1, source_target_pairs={{0,8},{2,66},{4,12},{6,70},{8,0},{10,74},{12,4},{14,78},{16,24},{1... | collective-permute-start | bytes 688136 | tf_op jit(solution)/shard_map/ppermute | solution.py:56
  43.6 15.9 %collective-permute-start.8 = (bf16[2,256,512]{2,1,0:T(8,128)(2,1)S(1)}, bf16[2,256,512]{2,1,0:T(8,128)(2,1)S(1)}, u32[]{:S(2)}, u32[]{:S(2)}) collective-permute-start(bf16[2,256,512]{2,1,0:T(8,128)(2,1)S(1)} %pad_maximum_fusion.pair_ref.k0), channel_id=1, source_target_pairs={{0,96},{2,14},{4,100},{6,2},{8,104},{10,6},{12,108},{14,10},{16,11... | collective-permute-start | bytes 1572872 | tf_op jit(solution)/shard_map/ppermute | solution.py:56
  47.4 12.1 %collective-permute-start.9 = (bf16[2,256,512]{2,1,0:T(8,128)(2,1)S(1)}, bf16[2,256,512]{2,1,0:T(8,128)(2,1)S(1)}, u32[]{:S(2)}, u32[]{:S(2)}) collective-permute-start(bf16[2,256,512]{2,1,0:T(8,128)(2,1)S(1)} %pad_maximum_fusion.pair_ref.k0), channel_id=1, source_target_pairs={{0,64},{2,10},{4,68},{6,14},{8,72},{10,2},{12,76},{14,6},{16,80},{... | collective-permute-start | bytes 1572872 | tf_op jit(solution)/shard_map/ppermute | solution.py:56
  47.4 24.9 %collective-permute-start.11 = (bf16[2,256,512]{2,1,0:T(8,128)(2,1)S(1)}, bf16[2,256,512]{2,1,0:T(8,128)(2,1)S(1)}, u32[]{:S(2)}, u32[]{:S(2)}) collective-permute-start(bf16[2,256,512]{2,1,0:T(8,128)(2,1)S(1)} %collective-permute-done.10.k0), channel_id=1, source_target_pairs={{0,32},{2,6},{4,36},{6,10},{8,40},{10,14},{12,44},{14,2},{16,48},{... | collective-permute-start | bytes 1572872 | tf_op jit(solution)/shard_map/ppermute | solution.py:56
  48.0 24.3 %collective-permute-start.12 = (bf16[2,256,512]{2,1,0:T(8,128)(2,1)S(1)}, bf16[2,256,512]{2,1,0:T(8,128)(2,1)S(1)}, u32[]{:S(2)}, u32[]{:S(2)}) collective-permute-start(bf16[2,256,512]{2,1,0:T(8,128)(2,1)S(1)} %collective-permute-done.10.k0), channel_id=1, source_target_pairs={{0,96},{2,14},{4,100},{6,2},{8,104},{10,6},{12,108},{14,10},{16,11... | collective-permute-start | bytes 1572872 | tf_op jit(solution)/shard_map/ppermute | solution.py:56
  50.9 21.5 %collective-permute-start.13 = (bf16[2,256,512]{2,1,0:T(8,128)(2,1)S(1)}, bf16[2,256,512]{2,1,0:T(8,128)(2,1)S(1)}, u32[]{:S(2)}, u32[]{:S(2)}) collective-permute-start(bf16[2,256,512]{2,1,0:T(8,128)(2,1)S(1)} %collective-permute-done.10.k0), channel_id=1, source_target_pairs={{0,64},{2,10},{4,68},{6,14},{8,72},{10,2},{12,76},{14,6},{16,80},{... | collective-permute-start | bytes 1572872 | tf_op jit(solution)/shard_map/ppermute | solution.py:56
  89.1 5.6 %collective-permute-start.14 = (bf16[8,128,128]{2,1,0:T(8,128)(2,1)S(1)}, bf16[8,128,128]{2,1,0:T(8,128)(2,1)S(1)}, u32[]{:S(2)}, u32[]{:S(2)}) collective-permute-start(bf16[8,128,128]{2,1,0:T(8,128)(2,1)S(1)} %get-tuple-element.23), channel_id=1, source_target_pairs={{0,12},{2,98},{4,0},{6,102},{8,4},{10,106},{12,8},{14,110},{16,28}... | collective-permute-start | bytes 786440 | tf_op jit(solution)/shard_map/ppermute | solution.py:56
  91.5 9.5 %collective-permute-start.15 = (bf16[8,128,128]{2,1,0:T(8,128)(2,1)S(1)}, bf16[8,128,128]{2,1,0:T(8,128)(2,1)S(1)}, u32[]{:S(2)}, u32[]{:S(2)}) collective-permute-start(bf16[8,128,128]{2,1,0:T(8,128)(2,1)S(1)} %get-tuple-element.24), channel_id=1, source_target_pairs={{0,4},{2,34},{4,8},{6,38},{8,12},{10,42},{12,0},{14,46},{16,20},{1... | collective-permute-start | bytes 786440 | tf_op jit(solution)/shard_map/ppermute | solution.py:56
  91.5 9.5 %collective-permute-start.16 = (bf16[8,128,128]{2,1,0:T(8,128)(2,1)S(1)}, bf16[8,128,128]{2,1,0:T(8,128)(2,1)S(1)}, u32[]{:S(2)}, u32[]{:S(2)}) collective-permute-start(bf16[8,128,128]{2,1,0:T(8,128)(2,1)S(1)} %get-tuple-element.25), channel_id=1, source_target_pairs={{0,8},{2,66},{4,12},{6,70},{8,0},{10,74},{12,4},{14,78},{16,24},{1... | collective-permute-start | bytes 786440 | tf_op jit(solution)/shard_map/ppermute | solution.py:56
  101.7 2.8 %collective-permute-start.17 = (bf16[3,128,128]{2,1,0:T(8,128)(2,1)S(1)}, bf16[3,128,128]{2,1,0:T(8,128)(2,1)S(1)}, u32[]{:S(2)}, u32[]{:S(2)}) collective-permute-start(bf16[3,128,128]{2,1,0:T(8,128)(2,1)S(1)} %get-tuple-element.27), channel_id=1, source_target_pairs={{0,2},{2,0},{4,6},{6,4},{8,10},{10,8},{12,14},{14,12},{16,18},{18,... | collective-permute-start | bytes 294920 | tf_op jit(solution)/shard_map/ppermute | solution.py:56
  109.2 10.4 %collective-permute-start.18 = (bf16[64,3072]{1,0:T(8,128)(2,1)S(1)}, bf16[64,3072]{1,0:T(8,128)(2,1)S(1)}, u32[]{:S(2)}, u32[]{:S(2)}) collective-permute-start(bf16[64,3072]{1,0:T(8,128)(2,1)S(1)} %get-tuple-element.29), channel_id=1, source_target_pairs={{0,1},{1,0},{2,3},{3,2},{4,5},{5,4},{6,7},{7,6},{8,9},{9,8},{10,11... | collective-permute-start | bytes 1179656 | tf_op jit(solution)/shard_map/ppermute | solution.py:60

commit v2 on v0

v2 whole, which is shorter than its diff:
```python
import functools
import math

import jax
import jax.numpy as jnp
import numpy as np
from jax import lax
from jax.experimental import pallas as pl
from jax.experimental.pallas import tpu as pltpu
from jax.sharding import PartitionSpec as P

D = 3072
HD = 128
COLS = 128
HEADS = 7
MINE = 3
UNITS = 7
TOK = 128
FEAT = HEADS * HD
HALF = TOK // 2
PIECES = 6
STEP = D // PIECES
SCALE2 = math.log2(math.e) / math.sqrt(HD)
F32 = jnp.float32
HBM = "hbm"
BF16 = jnp.bfloat16
MIB = 1024 * 1024
COST = pl.CostEstimate(flops=1, transcendentals=0, bytes_accessed=1)
SMEM = pl.BlockSpec(memory_space=pltpu.SMEM)
VMEM = pl.BlockSpec(memory_space=pltpu.VMEM)
ANY = pl.BlockSpec(memory_space=pl.ANY)


def _place(x, y, z, c):
    return ((x * 2 + y) * 4 + z) * 2 + c


def _perm(move):
    pairs = []
    for p in range(64):
        x, y, z, c = p // 16, (p // 8) % 2, (p // 2) % 4, p % 2
        pairs.append((p, _place(*move(x, y, z, c))))
    return pairs


def _key_move(d):
    return lambda x, y, z, c: ((x + d) % 4, y, z, c) if c == 0 else (x, y, (z + d) % 4, c)


def _query_move(d):
    return lambda x, y, z, c: (x, y, (z + d) % 4, c) if c == 0 else ((x + d) % 4, y, z, c)


def _core_move(x, y, z, c):
    return (x, y, z, 1 - c)


def _y_move(x, y, z, c):
    return (x, 1 - y, z, c)


def move(array, how):
    return lax.ppermute(array, "patch", _perm(how))


def swap_heads(array):
    return lax.ppermute(array, "head", [(0, 1), (1, 0)])


def kernel_call(kernel, name, out_shape, scratch_shapes, scalars, *arrays, after=(), outside=(), limit=12):
    first, count = len(scalars) + len(outside) + len(arrays), len(after)

    def run(*refs):
        kernel(*refs[:first], *refs[first + count :])

    return pl.pallas_call(
        run,
        in_specs=[SMEM] * len(scalars) + [ANY] * len(outside) + [VMEM] * len(arrays) + [ANY] * count,
        out_specs=[VMEM] * len(out_shape),
        out_shape=[pltpu.VMEM(*s) if len(s) == 2 else jax.ShapeDtypeStruct(*s[:2]) for s in out_shape],
        scratch_shapes=[pltpu.VMEM(*s) if isinstance(s, tuple) else s for s in scratch_shapes],
        compiler_params=pltpu.CompilerParams(vmem_limit_bytes=limit * MIB),
        cost_estimate=COST,
        name=name,
    )(*scalars, *(pltpu.with_memory_space_constraint(a, pltpu.HBM) for a in outside), *arrays, *after)


def _turn(v, table_ref, which):
    v = v * lax.rsqrt(jnp.mean(v * v, axis=-1, keepdims=True) + 1e-06)
    lane = lax.broadcasted_iota(jnp.int32, v.shape, 1)
    other = jnp.where(lane % 2 == 0, pltpu.roll(v, HD - 1, 1), pltpu.roll(v, 1, 1))
    return v * table_ref[2 * which] + other * table_ref[2 * which + 1]


def _bring(w_ref, which, out_ref, sems):
    groups = []
    for j, i in enumerate(which):
        copies = []
        for k in range(PIECES):
            rows = pl.ds(k * STEP, STEP)
            copies.append(pltpu.make_async_copy(w_ref.at[i, rows], out_ref.at[j, rows], sems.at[j * PIECES + k]))
        for copy in copies:
            copy.start()
        groups.append(copies)
    return groups


def _stage_kernel(w_ref, out_ref, sems):
    for copy in _bring(w_ref, (0,), out_ref, sems)[0]:
        copy.wait()


def stage(w, after):
    scratch = [pltpu.SemaphoreType.DMA((PIECES,))]
    outs = [((1, D, FEAT), BF16)]
    return kernel_call(_stage_kernel, "stage_weights", outs, scratch, [], outside=[w], after=after)[0]


def _query_kernel(place, w_ref, oth_ref, own_ref, table_ref, qa_ref, qb_ref, q_ref, x_ref):
    x = jnp.concatenate([oth_ref[...], own_ref[...]], axis=0)
    x_ref[...] = x
    projected = jnp.dot(x, w_ref[0], preferred_element_type=F32)
    queries = []
    for head in range(HEADS):
        at = slice(head * HD, (head + 1) * HD)
        queries.append((_turn(projected[:, at], table_ref, 0) * SCALE2).astype(BF16))
        q_ref[head] = queries[head]
    qa_ref[MINE] = queries[MINE]
    first = place[0] == 0
    for i in range(MINE):
        low, high = queries[i], queries[i + MINE + 1]
        qa_ref[i] = jnp.where(first, low, high)
        qb_ref[i] = jnp.where(first, high, low)


def project_queries(place, *arrays):
    outs = [
        ((MINE + 1, TOK, HD), BF16),
        ((MINE, TOK, HD), BF16),
        ((HEADS, TOK, HD), BF16),
        ((TOK, D), BF16),
    ]
    return kernel_call(_query_kernel, "query_projection", outs, [], [place], *arrays)


def _home_kernel(
    place, count, w_ref, text_ref, x_ref, table_ref, q_ref, out_ref, home_ref, stat_ref, buffer, text, part, sems
):
    bring_text = pltpu.make_async_copy(text_ref, text, sems.at[2 * PIECES])
    bring_text.start()
    groups = _bring(w_ref, (1, 2), buffer, sems)
    first = pl.ds(pl.multiple_of((1 - place[1]) * HALF, HALF), HALF)
    second = pl.ds(pl.multiple_of(place[1] * HALF, HALF), HALF)
    bring_text.wait()
    peaks = []
    for head in range(HEADS):
        at = slice(head * HD, (head + 1) * HD)
        s = _scores(q_ref[head], text[0, :, at])
        s = jnp.where(_lane(s.shape) < count[0], s, -jnp.inf)
        peak, part[head] = _fold(s, None, text[1, :, at])
        peaks.append(peak)
    for copy in groups[0]:
        copy.wait()
    projected = jnp.dot(x_ref[...], buffer[0], preferred_element_type=F32)
    keys = []
    for head in range(HEADS):
        at = slice(head * HD, (head + 1) * HD)
        k = _turn(projected[:, at], table_ref, 1).astype(BF16)
        out_ref[0, first, at] = k[:HALF]
        out_ref[0, second, at] = k[HALF:]
        keys.append(k)
    for copy in groups[1]:
        copy.wait()
    v = jnp.dot(x_ref[...], buffer[1], preferred_element_type=F32).astype(BF16)
    out_ref[1, first, :] = v[:HALF]
    out_ref[1, second, :] = v[HALF:]
    stat = jnp.zeros((TOK, HD), F32)
    for head in range(HEADS):
        at = slice(head * HD, (head + 1) * HD)
        peak, out = _fold(_scores(q_ref[head], keys[head]), peaks[head], v[:, at])
        out = out + part[head] * jnp.exp2(peaks[head] - peak)
        total = out[:, HD:]
        home_ref[head] = (out[:, :HD] / total).astype(BF16)
        stat = jnp.where(_lane(stat.shape) == head, peak + jnp.log2(total), stat)
    stat_ref[...] = stat


def attend_home(place, count, w, text_kv, *arrays, after):
    outs = [((2, TOK, FEAT), BF16, HBM), ((HEADS, TOK, HD), BF16), ((TOK, HD), F32)]
    scratch = [
        ((2, D, FEAT), BF16),
        (text_kv.shape, BF16),
        ((HEADS, TOK, 2 * HD), F32),
        pltpu.SemaphoreType.DMA((2 * PIECES + 1,)),
    ]
    outside = [w, text_kv]
    return kernel_call(
        _home_kernel,
        "home_attention",
        outs,
        scratch,
        [place, count],
        *arrays,
        outside=outside,
        after=after,
        limit=24,
    )


def _join_kernel(a_ref, b_ref, out_ref):
    out_ref[: MINE + 1] = a_ref[...]
    out_ref[MINE + 1 :] = b_ref[...]


def _gate_kernel(a_ref, *refs):
    del a_ref, refs


def gate(array, after):
    return pl.pallas_call(
        _gate_kernel,
        in_specs=[ANY] * (1 + len(after)),
        out_specs=ANY,
        out_shape=pltpu.VMEM(array.shape, array.dtype),
        input_output_aliases={0: 0},
        compiler_params=pltpu.CompilerParams(vmem_limit_bytes=MIB),
        cost_estimate=COST,
        name="gate",
    )(pltpu.with_memory_space_constraint(array, pltpu.VMEM), *after)


def join_units(a, b, after):
    outs = [((UNITS, TOK, HD), BF16)]
    return kernel_call(_join_kernel, "join_units", outs, [], [], a, b, after=after)[0]


def _scores(q, k):
    return lax.dot_general(q, k, (((1,), (1,)), ((), ())), preferred_element_type=F32)


def _fold(s, peak, values):
    top = s[:, :HD]
    for t in range(1, s.shape[1] // HD):
        top = jnp.maximum(top, s[:, t * HD : (t + 1) * HD])
    top = jnp.max(top, axis=1, keepdims=True)
    if peak is not None:
        top = jnp.maximum(top, peak)
    raw = jnp.exp2(s - top).astype(BF16)
    wide = jnp.concatenate([values, jnp.ones((values.shape[0], HD), BF16)], axis=1)
    return top, jnp.dot(raw, wide, preferred_element_type=F32)


def _lane(shape):
    return lax.broadcasted_iota(jnp.int32, shape, 1)


def _put(stat, u, peak, total):
    lane = _lane(stat.shape)
    return jnp.where(lane == u, peak, jnp.where(lane == u + 16, total, stat))


def _cols(index):
    return pl.ds(pl.multiple_of(index * HD, HD), HD)


def _slot_of(u, c):
    if u == MINE:
        return MINE * (1 - c)
    return (u if u < MINE else u - MINE - 1) + c


def _near_kernel(place, *refs):
    queries, keys = refs[:4], refs[4:8]
    acc_ref, stat_ref, s_ref = refs[8:]
    c = place[0]
    steps = [(u, g) for u in range(UNITS) for g in range(2)]

    def score(i):
        u, g = steps[i]
        q = jnp.concatenate([r[u, g * HALF : (g + 1) * HALF] for r in queries], axis=0)
        for b, k in enumerate(keys):
            s = _scores(q, k[0, :, _cols(_slot_of(u, c))])
            s_ref[i % 2, :, b * 2 * TOK : (b + 1) * 2 * TOK] = s
        patch = slice(0, TOK) if u <= MINE else slice(TOK, 2 * TOK)
        s_ref[i % 2, :HALF, patch] = jnp.full((HALF, TOK), -jnp.inf, F32)

    stats = [jnp.zeros((4 * HALF, HD), F32)] * 2
    score(0)
    for i, (u, g) in enumerate(steps):
        if i + 1 < len(steps):
            score(i + 1)
        values = jnp.concatenate([k[1, :, _cols(_slot_of(u, c))] for k in keys], axis=0)
        peak, out = _fold(s_ref[i % 2], None, values)
        acc_ref[u, g * 4 * HALF : (g + 1) * 4 * HALF] = out[:, :HD]
        stats[g] = _put(stats[g], u, peak, out[:, HD:])
    stat_ref[: 4 * HALF] = stats[0]
    stat_ref[4 * HALF :] = stats[1]


def attend_near(place, queries, pairs, after):
    outs = [((UNITS, 4 * TOK, HD), F32), ((4 * TOK, HD), F32)]
    scratch = [((2, 4 * HALF, 8 * TOK), F32)]
    return kernel_call(_near_kernel, "near_attention", outs, scratch, [place], *queries, *pairs, after=after)


def _far_kernel(g, place, *refs):
    queries, (acc_in, stat_in), keys = refs[:4], refs[4:6], refs[6:10]
    outs, s_ref = refs[10:14], refs[14]
    c = place[0]
    rows = slice(g * 4 * HALF, (g + 1) * 4 * HALF)

    def score(u):
        q = jnp.concatenate([r[u, g * HALF : (g + 1) * HALF] for r in queries], axis=0)
        for b, k in enumerate(keys):
            s = _scores(q, k[0, :, _cols(_slot_of(u, c))])
            s_ref[u % 2, :, b * 2 * TOK : (b + 1) * 2 * TOK] = s

    mark = jnp.zeros((4 * HALF, HD), F32)
    score(0)
    for u in range(UNITS):
        if u + 1 < UNITS:
            score(u + 1)
        before = stat_in[rows, u : u + 1]
        values = jnp.concatenate([k[1, :, _cols(_slot_of(u, c))] for k in keys], axis=0)
        peak, out = _fold(s_ref[u % 2], before, values)
        factor = jnp.exp2(before - peak)
        total = stat_in[rows, u + 16 : u + 17] * factor + out[:, HD:]
        out = ((acc_in[u, rows] * factor + out[:, :HD]) / total).astype(BF16)
        level = peak + jnp.log2(total)
        lane = _lane(level.shape)
        mark = jnp.where(lane % 16 == u, level, mark)
        for i, o in enumerate(outs):
            o[u] = out[i * HALF : (i + 1) * HALF]
    mark = _spread(mark)
    for i, o in enumerate(outs):
        o[UNITS] = mark[i * HALF : (i + 1) * HALF]


def attend_far(g, place, queries, acc, stat, pairs, after):
    outs = [((UNITS + 1, HALF, HD), BF16)] * 4
    scratch = [((2, 4 * HALF, 8 * TOK), F32)]
    kernel = functools.partial(_far_kernel, g)
    return kernel_call(kernel, f"far_attention_{g}", outs, scratch, [place], *queries, acc, stat, *pairs, after=after)


def _spread(level):
    high = level.astype(BF16).astype(F32)
    middle = (level - high).astype(BF16).astype(F32)
    lane = _lane(level.shape)
    low = level - high - middle
    return jnp.where(lane < 16, high, jnp.where(lane < 32, middle, low)).astype(BF16)


def _collect(mark):
    mark = mark.astype(F32)
    return mark + pltpu.roll(mark, HD - 16, 1) + pltpu.roll(mark, HD - 32, 1)


def _merge_kernel(p0, p1, p2, p3, mine_ref, stat_ref, sib_ref):
    parts = (p0, p1, p2, p3)
    levels = [_collect(p[UNITS]) for p in parts]
    top = functools.reduce(jnp.maximum, levels)
    weights = [jnp.exp2(v - top) for v in levels]
    total = functools.reduce(jnp.add, weights)
    weights = [w / total for w in weights]
    for u in range(UNITS):
        out = None
        for p, w in zip(parts, weights, strict=True):
            term = p[u].astype(F32) * w[:, u : u + 1]
            out = term if out is None else out + term
        if u <= MINE:
            mine_ref[u] = out.astype(BF16)
        else:
            sib_ref[u - MINE - 1] = out.astype(BF16)
    level = top + jnp.log2(total)
    stat_ref[...] = level
    lane = _lane(level.shape)
    level = jnp.where(lane < 16, level, 0.0)
    sib_ref[MINE] = _spread(level + pltpu.roll(level, 16, 1) + pltpu.roll(level, 32, 1))


def merge(parts, after):
    outs = [((MINE + 1, HALF, HD), BF16), ((HALF, HD), F32), ((MINE + 1, HALF, HD), BF16)]
    return kernel_call(_merge_kernel, "merge_parts", outs, [], [], *parts, after=after)


def _out_kernel(g, place, mine_ref, stat_ref, got_ref, home_ref, level_ref, w_ref, out_ref):
    rows = slice(g * HALF, (g + 1) * HALF)
    first = place[0] == 0
    mine = stat_ref[...]
    got = _collect(got_ref[MINE])
    attended = []
    for head in range(HEADS):
        slot = head % (MINE + 1)
        a, la = mine_ref[slot], mine[:, slot : slot + 1]
        if head != MINE:
            low = head < MINE
            b, lb = got_ref[slot], got[:, slot + MINE + 1 : slot + MINE + 2]
            a, b = (a, b) if low else (b, a)
            la, lb = (la, lb) if low else (lb, la)
            a, la = jnp.where(first, a, b), jnp.where(first, la, lb)
        h, lh = home_ref[head, rows], level_ref[rows, head : head + 1]
        top = jnp.maximum(la, lh)
        wa, wh = jnp.exp2(la - top), jnp.exp2(lh - top)
        total = wa + wh
        out = a.astype(F32) * (wa / total) + h.astype(F32) * (wh / total)
        attended.append(out.astype(BF16))
    out = jnp.dot(jnp.concatenate(attended, axis=1), w_ref[...], preferred_element_type=F32)
    out_ref[...] = out.astype(out_ref.dtype)


def project_out(g, place, kind, *arrays):
    outs = [((HALF, D), kind, HBM)]
    kernel = functools.partial(_out_kernel, g)
    return kernel_call(kernel, "output_projection", outs, [], [place], *arrays)[0]


def _bands():
    first = HD // 8
    band = (HD - first) // 2
    omega = np.repeat(10000.0 ** (-2.0 * np.arange(band // 2) / band), 2)
    along_rows = np.zeros((HD,))
    along_cols = np.zeros((HD,))
    along_rows[first : first + band] = omega
    along_cols[first + band :] = omega
    sign = np.where(np.arange(HD) % 2 == 0, -1.0, 1.0)
    return (v.astype(np.float32) for v in (along_rows, along_cols, sign))


def body(image, w_qkv, qk_gain, stale_kv, text_kv, text_count, row_offset, w_out):
    core = lax.axis_index("patch") % 2
    group = lax.axis_index("head")
    place = jnp.stack([core, group]).astype(jnp.int32)
    other_image = swap_heads(image)

    wide = (2, TOK, (MINE + 1) * HD)
    given = lax.dynamic_slice(stale_kv, (0, 0, (1 - core) * MINE * HD), wide)
    kept = lax.dynamic_slice(stale_kv, (0, 0, core * MINE * HD), wide)
    pair = jnp.concatenate([kept, move(given, _core_move)], axis=1)
    far_pair = move(pair, _y_move)
    near = [pair] + [move(pair, _key_move(d)) for d in (1, 3, 2)]

    within = jnp.arange(TOK, dtype=jnp.int32)
    within = jnp.where(within < HALF, within + (1 - group) * HALF, within - (1 - group) * HALF)
    rows = (row_offset[0] + within // COLS).astype(F32)[:, None]
    cols = (within % COLS).astype(F32)[:, None]
    along_rows, along_cols, sign = _bands()
    angles = rows * along_rows + cols * along_cols
    cosine = jnp.cos(angles)
    sine = jnp.sin(angles) * sign
    swapped = qk_gain.reshape(2, HD // 2, 2)[:, :, ::-1].reshape(2, HD)
    table = jnp.stack([qk_gain[0] * cosine, swapped[0] * sine, qk_gain[1] * cosine, swapped[1] * sine])

    w = jnp.transpose(w_qkv, (1, 0, 2))
    q_mine, q_given, q_own, x = project_queries(place, stage(w, [pair]), other_image, image, table)
    units = join_units(q_mine, move(q_given, _core_move), near[1:4])
    queries = [units] + [move(units, _query_move(d)) for d in (1, 3, 2)]
    far_pair = gate(far_pair, queries[1:4])
    far = [far_pair] + [move(far_pair, _key_move(d)) for d in (1, 3, 2)]
    acc, stat = attend_near(place, queries, near, [far_pair])
    fresh_kv, home, level = attend_home(place, text_count, w, text_kv, x, table, q_own, after=[acc])

    parts = [attend_far(g, place, queries, acc, stat, far, [home]) for g in (0, 1)]
    halves = []
    for g, kind in ((0, BF16), (1, F32)):
        back = [parts[g][0]] + [move(parts[g][i], _query_move(d)) for i, d in ((1, 3), (2, 1), (3, 2))]
        mine, mine_stat, given_back = merge(back, parts[1][:1] if g == 0 else [])
        got = move(given_back, _core_move)
        halves.append(project_out(g, place, kind, mine, mine_stat, got, home, level, w_out))
    mixed = (halves[1] + swap_heads(halves[0]).astype(F32)).astype(BF16)
    return (mixed, fresh_kv)


def solution(mesh):
    placed = (
        P(("patch", "head"), None),
        P(None, None, "head"),
        P(),
        P(None, "patch", "head"),
        P(None, None, "head"),
        P(),
        P("patch"),
        P("head", None),
    )
    return jax.shard_map(
        body,
        mesh=mesh,
        in_specs=placed,
        out_specs=(P(("patch", "head"), None), P(None, "patch", "head")),
        check_vma=False,
    )
```

time: 266 us -> 85 us (0.32)
  waiting for transfers between devices: 119 us -> 16.7 us
  local copies, waits for them, and re-layouts: 55.4 us -> 2.57 us
  matrix products: 44.5 us -> 0 us
  starting transfers between devices: 0.08 us -> 32 us
  Pallas kernels: 0 us -> 29.4 us
  other arithmetic: 18.9 us -> 2 us
  between operations: 15.6 us -> 2.2 us
  blocking collectives: 11.2 us -> 0 us
    all_gather x1 -> x0, waiting for transfers between devices: 99.7 us -> none  [body(): gathered = lax.all_gather(stale_kv, 'patch', axis=1, tiled=True)]
    dot_general x6 -> x0, matrix products: 44.5 us -> none  [the longest x2 17.5 us: attend_block(): jnp.einsum('hqk,khd->hqd', raw.astype(jnp.bfloat16), value_rows, preferre...]
    ppermute x0 -> x22, starting transfers between devices: none -> 32 us  [the longest x20 30.4 us: move(): return lax.ppermute(array, 'patch', _perm(how))]
    pallas_call x0 -> x12, Pallas kernels: none -> 29.4 us  [the longest x11 29.4 us: kernel_call(): pl.pallas_call(run, in_specs=[SMEM] * len(scalars) + [ANY] * len(outside)...]
    unnamed x16 -> x6, local copies, waits for them, and re-layouts: 28.1 us -> 0.02 us
    slice x5, local copies, waits for them, and re-layouts: 23.8 us -> 1.18 us  [the longest x1 0.77 us: body(): qk_gain[0] * cosine]
    reduce_scatter x1 -> x0, waiting for transfers between devices: 19.6 us -> none  [body(): lax.psum_scatter(jnp.dot(attended, w_out, preferred_element_type=jnp.floa...]
    ppermute x0 -> x22, waiting for transfers between devices: none -> 16.7 us  [the longest x20 16.7 us: move(): return lax.ppermute(array, 'patch', _perm(how))]
  transfers between devices with their start and end apart: 2 -> 22, of which waited for: 2 -> 9; matrix products, arithmetic and copies ran while one was open for 17% -> 3% of each run, Pallas kernels for 0% -> 27%
where the time goes in v2:
time: 85 us; the launch traced here: 84.8 us
  starting transfers between devices  32 us (38%)
  Pallas kernels  29.4 us (35%)
  waiting for transfers between devices  16.7 us (20%)
  local copies, waits for them, and re-layouts  2.57 us (3%)
  between operations  2.2 us (3%)
  other arithmetic  2 us (2%)
    ppermute x20, starting transfers between devices, move(): return lax.ppermute(array, 'patch', _perm(how))  30.4 us
    pallas_call x11, Pallas kernels, kernel_call(): pl.pallas_call(run, in_specs=[SMEM] * len(scalars) + [ANY] * len(outside)...  29.4 us
    ppermute x20, waiting for transfers between devices, move(): return lax.ppermute(array, 'patch', _perm(how))  16.7 us
  transfers between devices with their start and end apart: 22, of which 9 were waited for; matrix products, arithmetic and copies ran while one was open for 3% of the time, Pallas kernels for 27%

profile of v2, /device:TPU:1, one launch (start us, length us, event | category | flops | bytes accessed | tf_op | source)
XLA Modules:
  0.0 84.8 jit_solution(9807188464221051706)
XLA Ops:
  0.7 1.1 %constant_dynamic-slice_fusion.1 = (bf16[2,128,512]{2,1,0:T(8,128)(2,1)S(1)}, bf16[2,128,512]{2,1,0:T(8,128)(2,1)S(1)}) fusion(bf16[2,128,896]{2,1,0:T(8,128)(2,1)} %param.14, s32[]{:T(128)S(6)} %select_n.43, s32[]{:T(128)S(6)} %select_n.44), kind=kLoop, calls=%fused_computation.20 | loop fusion | bytes 1048584 | tf_op jit(solution)/shard_map/dynamic_slice | solution.py:438
  1.7 1.5 %collective-permute-start = (bf16[2,128,512]{2,1,0:T(8,128)(2,1)S(1)}, bf16[2,128,512]{2,1,0:T(8,128)(2,1)S(1)}, u32[]{:S(2)}, u32[]{:S(2)}) collective-permute-start(bf16[2,128,512]{2,1,0:T(8,128)(2,1)S(1)} %get-tuple-element.51), channel_id=1, source_target_pairs={{0,2},{2,0},{4,6},{6,4},{8,10},{10,8},{12,14},{14,12},{16,18},{18,... | collective-permute-start | bytes 786440 | tf_op jit(solution)/shard_map/ppermute | solution.py:63
  3.2 1.4 %collective-permute-start.1 = (bf16[64,3072]{1,0:T(8,128)(2,1)}, bf16[64,3072]{1,0:T(8,128)(2,1)S(1)}, u32[]{:S(2)}, u32[]{:S(2)}) collective-permute-start(bf16[64,3072]{1,0:T(8,128)(2,1)} %refs_3_.2), channel_id=1, source_target_pairs={{0,1},{1,0},{2,3},{3,2},{4,5},{5,4},{6,7},{7,6},{8,9},{9,8},{10,11... | collective-permute-start | bytes 1179656 | tf_op jit(solution)/shard_map/ppermute | solution.py:67
  6.9 1.7 %collective-permute-start.3 = (bf16[2,256,512]{2,1,0:T(8,128)(2,1)S(1)}, bf16[2,256,512]{2,1,0:T(8,128)(2,1)S(1)}, u32[]{:S(2)}, u32[]{:S(2)}) collective-permute-start(bf16[2,256,512]{2,1,0:T(8,128)(2,1)S(1)} %pad_maximum_fusion.refs_1_.refs_5_), channel_id=1, source_target_pairs={{0,32},{2,6},{4,36},{6,10},{8,40},{10,14},{12,44},{14,2},{16,48},{... | collective-permute-start | bytes 1572872 | tf_op jit(solution)/shard_map/ppermute | solution.py:63
  8.6 2.2 %collective-permute-start.4 = (bf16[2,256,512]{2,1,0:T(8,128)(2,1)S(1)}, bf16[2,256,512]{2,1,0:T(8,128)(2,1)S(1)}, u32[]{:S(2)}, u32[]{:S(2)}) collective-permute-start(bf16[2,256,512]{2,1,0:T(8,128)(2,1)S(1)} %pad_maximum_fusion.refs_1_.refs_5_), channel_id=1, source_target_pairs={{0,96},{2,14},{4,100},{6,2},{8,104},{10,6},{12,108},{14,10},{16,11... | collective-permute-start | bytes 1572872 | tf_op jit(solution)/shard_map/ppermute | solution.py:63
  10.8 1.2 %collective-permute-start.5 = (bf16[2,256,512]{2,1,0:T(8,128)(2,1)S(1)}, bf16[2,256,512]{2,1,0:T(8,128)(2,1)S(1)}, u32[]{:S(2)}, u32[]{:S(2)}) collective-permute-start(bf16[2,256,512]{2,1,0:T(8,128)(2,1)S(1)} %pad_maximum_fusion.refs_1_.refs_5_), channel_id=1, source_target_pairs={{0,64},{2,10},{4,68},{6,14},{8,72},{10,2},{12,76},{14,6},{16,80},{... | collective-permute-start | bytes 1572872 | tf_op jit(solution)/shard_map/ppermute | solution.py:63
  12.0 1.0 %fusion.4 = (f32[1,128,128]{2,1,0:T(8,128)S(1)}, f32[1,128,128]{2,1,0:T(8,128)S(1)}, f32[1,128,128]{2,1,0:T(8,128)S(1)}, f32[1,128,128]{2,1,0:T(8,128)S(1)}) fusion(f32[128]{0:T(128)} %constant.66.clone, f32[128]{0:T(128)S(1)} %mul.175, f32[128]{0:T(128)} %constant.65.clone, f32[128]{0:T(128)S(1)} %get-tuple-element.58, f32[128]{0:T(128)} %constant.64.clone, ...), kind=kLoop, calls=%fused_computation.9 | loop fusion | flops 131072 | bytes 266752 | tf_op jit(solution)/shard_map/mul | solution.py:452
  13.0 2.7 %collective-permute-start.9 = (bf16[2,256,512]{2,1,0:T(8,128)(2,1)S(1)}, bf16[2,256,512]{2,1,0:T(8,128)(2,1)S(1)}, u32[]{:S(2)}, u32[]{:S(2)}) collective-permute-start(bf16[2,256,512]{2,1,0:T(8,128)(2,1)S(1)} %pad_maximum_fusion.refs_1_.refs_5_), channel_id=1, source_target_pairs={{0,16},{2,18},{4,20},{6,22},{8,24},{10,26},{12,28},{14,30},{16,0},... | collective-permute-start | bytes 1572872 | tf_op jit(solution)/shard_map/ppermute | solution.py:63
  15.8 2.7 %stage_weights.1.refs_1_ = bf16[1,3072,896]{2,1,0:T(8,128)(2,1)S(1)} custom-call(bf16[3,3072,896]{2,1,0:T(8,128)(2,1)} %bitcast.11, bf16[2,256,512]{2,1,0:T(8,128)(2,1)S(1)} %pad_maximum_fusion.refs_1_.refs_5_), custom_call_target="tpu_custom_call" | custom-call | flops 1 | bytes 1 | tf_op jit(solution)/shard_map/stage_weights/pallas_call | solution.py:76
  18.5 1.8 %query_projection.1 = (bf16[4,128,128]{2,1,0:T(8,128)(2,1)S(1)}, bf16[3,128,128]{2,1,0:T(8,128)(2,1)S(1)}, bf16[7,128,128]{2,1,0:T(8,128)(2,1)S(1)}, bf16[128,3072]{1,0:T(8,128)(2,1)S(1)}) custom-call(s32[2]{0:T(128)S(1)} %pad_add_fusion.refs_0_, bf16[1,3072,896]{2,1,0:T(8,128)(2,1)S(1)} %stage_weights.1.refs_1_, ...), custom_call_target="tpu_custom_call" | custom-call | flops 1 | bytes 1 | tf_op jit(solution)/shard_map/query_projection/pallas_call | solution.py:76
  21.0 0.9 %collective-permute-done.2.refs_1_ = bf16[3,128,128]{2,1,0:T(8,128)(2,1)S(1)} collective-permute-done((bf16[3,128,128]{2,1,0:T(8,128)(2,1)S(1)}, bf16[3,128,128]{2,1,0:T(8,128)(2,1)S(1)}, u32[]{:S(2)}, u32[]{:S(2)}) %collective-permute-start.2) | collective-permute-done | bytes 98336 | tf_op jit(solution)/shard_map/ppermute | solution.py:63
  22.5 1.8 %collective-permute-done.5.refs_4_.refs_8_ = bf16[2,256,512]{2,1,0:T(8,128)(2,1)S(1)} collective-permute-done((bf16[2,256,512]{2,1,0:T(8,128)(2,1)S(1)}, bf16[2,256,512]{2,1,0:T(8,128)(2,1)S(1)}, u32[]{:S(2)}, u32[]{:S(2)}) %collective-permute-start.5) | collective-permute-done | bytes 524320 | tf_op jit(solution)/shard_map/ppermute | solution.py:63
  24.4 1.3 %collective-permute-start.6 = (bf16[7,128,128]{2,1,0:T(8,128)(2,1)S(1)}, bf16[7,128,128]{2,1,0:T(8,128)(2,1)S(1)}, u32[]{:S(2)}, u32[]{:S(2)}) collective-permute-start(bf16[7,128,128]{2,1,0:T(8,128)(2,1)S(1)} %join_units.1.refs_1_), channel_id=1, source_target_pairs={{0,4},{2,34},{4,8},{6,38},{8,12},{10,42},{12,0},{14,46},{16,20},{1... | collective-permute-start | bytes 688136 | tf_op jit(solution)/shard_map/ppermute | solution.py:63
  25.6 1.5 %collective-permute-start.7 = (bf16[7,128,128]{2,1,0:T(8,128)(2,1)S(1)}, bf16[7,128,128]{2,1,0:T(8,128)(2,1)S(1)}, u32[]{:S(2)}, u32[]{:S(2)}) collective-permute-start(bf16[7,128,128]{2,1,0:T(8,128)(2,1)S(1)} %join_units.1.refs_1_), channel_id=1, source_target_pairs={{0,12},{2,98},{4,0},{6,102},{8,4},{10,106},{12,8},{14,110},{16,28}... | collective-permute-start | bytes 688136 | tf_op jit(solution)/shard_map/ppermute | solution.py:63
  27.1 1.5 %collective-permute-start.8 = (bf16[7,128,128]{2,1,0:T(8,128)(2,1)S(1)}, bf16[7,128,128]{2,1,0:T(8,128)(2,1)S(1)}, u32[]{:S(2)}, u32[]{:S(2)}) collective-permute-start(bf16[7,128,128]{2,1,0:T(8,128)(2,1)S(1)} %join_units.1.refs_1_), channel_id=1, source_target_pairs={{0,8},{2,66},{4,12},{6,70},{8,0},{10,74},{12,4},{14,78},{16,24},{1... | collective-permute-start | bytes 688136 | tf_op jit(solution)/shard_map/ppermute | solution.py:63
  28.6 2.2 %collective-permute-done.6.refs_0_.refs_2_ = bf16[7,128,128]{2,1,0:T(8,128)(2,1)S(1)} collective-permute-done((bf16[7,128,128]{2,1,0:T(8,128)(2,1)S(1)}, bf16[7,128,128]{2,1,0:T(8,128)(2,1)S(1)}, u32[]{:S(2)}, u32[]{:S(2)}) %collective-permute-start.6) | collective-permute-done | bytes 229408 | tf_op jit(solution)/shard_map/ppermute | solution.py:63
  30.8 3.4 %collective-permute-done.8.refs_2_.refs_4_ = bf16[7,128,128]{2,1,0:T(8,128)(2,1)S(1)} collective-permute-done((bf16[7,128,128]{2,1,0:T(8,128)(2,1)S(1)}, bf16[7,128,128]{2,1,0:T(8,128)(2,1)S(1)}, u32[]{:S(2)}, u32[]{:S(2)}) %collective-permute-start.8) | collective-permute-done | bytes 229408 | tf_op jit(solution)/shard_map/ppermute | solution.py:63
  34.8 2.1 %collective-permute-start.11 = (bf16[2,256,512]{2,1,0:T(8,128)(2,1)S(1)}, bf16[2,256,512]{2,1,0:T(8,128)(2,1)S(1)}, u32[]{:S(2)}, u32[]{:S(2)}) collective-permute-start(bf16[2,256,512]{2,1,0:T(8,128)(2,1)S(1)} %gate.1.refs_9_.refs_7_), channel_id=1, source_target_pairs={{0,96},{2,14},{4,100},{6,2},{8,104},{10,6},{12,108},{14,10},{16,11... | collective-permute-start | bytes 1572872 | tf_op jit(solution)/shard_map/ppermute | solution.py:63
  37.7 5.2 %near_attention.1 = (f32[7,512,128]{2,1,0:T(8,128)S(1)}, f32[512,128]{1,0:T(8,128)S(1)}) custom-call(s32[2]{0:T(128)S(1)} %pad_add_fusion.refs_0_, bf16[7,128,128]{2,1,0:T(8,128)(2,1)S(1)} %join_units.1.refs_1_, bf16[7,128,128]{2,1,0:T(8,128)(2,1)S(1)} %collective-permute-done.6.refs_0_.refs_2_, ...), custom_call_target="tpu_custom_call" | custom-call | flops 1 | bytes 1 | tf_op jit(solution)/shard_map/near_attention/pallas_call | solution.py:76
  42.9 7.4 %home_attention.1 = (bf16[2,128,896]{2,1,0:T(8,128)(2,1)}, bf16[7,128,128]{2,1,0:T(8,128)(2,1)S(1)}, f32[128,128]{1,0:T(8,128)S(1)}) custom-call(s32[2]{0:T(128)S(1)} %pad_add_fusion.refs_0_, s32[1]{0:T(128)S(6)} %copy.15.refs_1_, bf16[3,3072,896]{2,1,0:T(8,128)(2,1)} %bitcast.12, bf16[2,512,896]{2,1,0:T(8,128)(2,1)} %refs_3_.3, ...), custom_call_target="tpu_custom_call" | custom-call | flops 1 | bytes 1 | tf_op jit(solution)/shard_map/home_attention/pallas_call | solution.py:76
  50.3 3.8 %far_attention_0.1 = (bf16[8,64,128]{2,1,0:T(8,128)(2,1)S(1)}, bf16[8,64,128]{2,1,0:T(8,128)(2,1)S(1)}, bf16[8,64,128]{2,1,0:T(8,128)(2,1)S(1)}, bf16[8,64,128]{2,1,0:T(8,128)(2,1)S(1)}) custom-call(s32[2]{0:T(128)S(1)} %pad_add_fusion.refs_0_, bf16[7,128,128]{2,1,0:T(8,128)(2,1)S(1)} %join_units.1.refs_1_, ...), custom_call_target="tpu_custom_call" | custom-call | flops 1 | bytes 1 | tf_op jit(solution)/shard_map/far_attention_0/pallas_call | solution.py:76
  54.2 1.8 %collective-permute-start.17 = (bf16[8,64,128]{2,1,0:T(8,128)(2,1)S(1)}, bf16[8,64,128]{2,1,0:T(8,128)(2,1)S(1)}, u32[]{:S(2)}, u32[]{:S(2)}) collective-permute-start(bf16[8,64,128]{2,1,0:T(8,128)(2,1)S(1)} %get-tuple-element.41), channel_id=1, source_target_pairs={{0,12},{2,98},{4,0},{6,102},{8,4},{10,106},{12,8},{14,110},{16,28}... | collective-permute-start | bytes 393224 | tf_op jit(solution)/shard_map/ppermute | solution.py:63
  55.9 1.3 %collective-permute-start.19 = (bf16[8,64,128]{2,1,0:T(8,128)(2,1)S(1)}, bf16[8,64,128]{2,1,0:T(8,128)(2,1)S(1)}, u32[]{:S(2)}, u32[]{:S(2)}) collective-permute-start(bf16[8,64,128]{2,1,0:T(8,128)(2,1)S(1)} %get-tuple-element.43), channel_id=1, source_target_pairs={{0,8},{2,66},{4,12},{6,70},{8,0},{10,74},{12,4},{14,78},{16,24},{1... | collective-permute-start | bytes 393224 | tf_op jit(solution)/shard_map/ppermute | solution.py:63
  57.2 3.8 %far_attention_1.1 = (bf16[8,64,128]{2,1,0:T(8,128)(2,1)S(1)}, bf16[8,64,128]{2,1,0:T(8,128)(2,1)S(1)}, bf16[8,64,128]{2,1,0:T(8,128)(2,1)S(1)}, bf16[8,64,128]{2,1,0:T(8,128)(2,1)S(1)}) custom-call(s32[2]{0:T(128)S(1)} %pad_add_fusion.refs_0_, bf16[7,128,128]{2,1,0:T(8,128)(2,1)S(1)} %join_units.1.refs_1_, ...), custom_call_target="tpu_custom_call" | custom-call | flops 1 | bytes 1 | tf_op jit(solution)/shard_map/far_attention_1/pallas_call | solution.py:76
  61.0 1.3 %collective-permute-done.18.refs_2_ = bf16[8,64,128]{2,1,0:T(8,128)(2,1)S(1)} collective-permute-done((bf16[8,64,128]{2,1,0:T(8,128)(2,1)S(1)}, bf16[8,64,128]{2,1,0:T(8,128)(2,1)S(1)}, u32[]{:S(2)}, u32[]{:S(2)}) %collective-permute-start.18) | collective-permute-done | bytes 131104 | tf_op jit(solution)/shard_map/ppermute | solution.py:63
  62.8 4.5 %collective-permute-start.20 = (bf16[4,64,128]{2,1,0:T(8,128)(2,1)S(1)}, bf16[4,64,128]{2,1,0:T(8,128)(2,1)S(1)}, u32[]{:S(2)}, u32[]{:S(2)}) collective-permute-start(bf16[4,64,128]{2,1,0:T(8,128)(2,1)S(1)} %get-tuple-element.46), channel_id=1, source_target_pairs={{0,2},{2,0},{4,6},{6,4},{8,10},{10,8},{12,14},{14,12},{16,18},{18,... | collective-permute-start | bytes 196616 | tf_op jit(solution)/shard_map/ppermute | solution.py:63
  68.2 1.8 %output_projection.3 = bf16[64,3072]{1,0:T(8,128)(2,1)S(1)} custom-call(s32[2]{0:T(128)S(1)} %pad_add_fusion.refs_0_, bf16[4,64,128]{2,1,0:T(8,128)(2,1)S(1)} %get-tuple-element.44.refs_1_, f32[64,128]{1,0:T(8,128)S(1)} %get-tuple-element.45.refs_2_, bf16[4,64,128]{2,1,0:T(8,128)(2,1)S(1)} %collective-permute-done.20.refs_3_, ...), custom_call_target="tpu_custom_call" | custom-call | flops 1 | bytes 1 | tf_op jit(solution)/shard_map/output_projection/pallas_call | solution.py:76
  70.3 2.1 %collective-permute-start.13 = (bf16[8,64,128]{2,1,0:T(8,128)(2,1)S(1)}, bf16[8,64,128]{2,1,0:T(8,128)(2,1)S(1)}, u32[]{:S(2)}, u32[]{:S(2)}) collective-permute-start(bf16[8,64,128]{2,1,0:T(8,128)(2,1)S(1)} %get-tuple-element.33), channel_id=1, source_target_pairs={{0,12},{2,98},{4,0},{6,102},{8,4},{10,106},{12,8},{14,110},{16,28}... | collective-permute-start | bytes 393224 | tf_op jit(solution)/shard_map/ppermute | solution.py:63
  72.5 2.1 %collective-permute-start.15 = (bf16[8,64,128]{2,1,0:T(8,128)(2,1)S(1)}, bf16[8,64,128]{2,1,0:T(8,128)(2,1)S(1)}, u32[]{:S(2)}, u32[]{:S(2)}) collective-permute-start(bf16[8,64,128]{2,1,0:T(8,128)(2,1)S(1)} %get-tuple-element.35), channel_id=1, source_target_pairs={{0,8},{2,66},{4,12},{6,70},{8,0},{10,74},{12,4},{14,78},{16,24},{1... | collective-permute-start | bytes 393224 | tf_op jit(solution)/shard_map/ppermute | solution.py:63
  74.6 4.6 %collective-permute-done.14.refs_2_ = bf16[8,64,128]{2,1,0:T(8,128)(2,1)S(1)} collective-permute-done((bf16[8,64,128]{2,1,0:T(8,128)(2,1)S(1)}, bf16[8,64,128]{2,1,0:T(8,128)(2,1)S(1)}, u32[]{:S(2)}, u32[]{:S(2)}) %collective-permute-start.14) | collective-permute-done | bytes 131104 | tf_op jit(solution)/shard_map/ppermute | solution.py:63
  79.7 1.6 %collective-permute-start.16 = (bf16[4,64,128]{2,1,0:T(8,128)(2,1)S(1)}, bf16[4,64,128]{2,1,0:T(8,128)(2,1)S(1)}, u32[]{:S(2)}, u32[]{:S(2)}) collective-permute-start(bf16[4,64,128]{2,1,0:T(8,128)(2,1)S(1)} %get-tuple-element.38), channel_id=1, source_target_pairs={{0,2},{2,0},{4,6},{6,4},{8,10},{10,8},{12,14},{14,12},{16,18},{18,... | collective-permute-start | bytes 196616 | tf_op jit(solution)/shard_map/ppermute | solution.py:63
  82.1 1.8 %output_projection.2 = f32[64,3072]{1,0:T(8,128)S(1)} custom-call(s32[2]{0:T(128)S(1)} %pad_add_fusion.refs_0_, bf16[4,64,128]{2,1,0:T(8,128)(2,1)S(1)} %get-tuple-element.36.refs_1_, f32[64,128]{1,0:T(8,128)S(1)} %get-tuple-element.37.refs_2_, bf16[4,64,128]{2,1,0:T(8,128)(2,1)S(1)} %collective-permute-done.16.refs_3_, ...), custom_call_target="tpu_custom_call" | custom-call | flops 1 | bytes 1 | tf_op jit(solution)/shard_map/output_projection/pallas_call | solution.py:76
  (45 shorter events, 7.4 us)
Async XLA Ops:
  1.7 5.1 %collective-permute-start = (bf16[2,128,512]{2,1,0:T(8,128)(2,1)S(1)}, bf16[2,128,512]{2,1,0:T(8,128)(2,1)S(1)}, u32[]{:S(2)}, u32[]{:S(2)}) collective-permute-start(bf16[2,128,512]{2,1,0:T(8,128)(2,1)S(1)} %get-tuple-element.51), channel_id=1, source_target_pairs={{0,2},{2,0},{4,6},{6,4},{8,10},{10,8},{12,14},{14,12},{16,18},{18,... | collective-permute-start | bytes 786440 | tf_op jit(solution)/shard_map/ppermute | solution.py:63
  3.2 15.3 %collective-permute-start.1 = (bf16[64,3072]{1,0:T(8,128)(2,1)}, bf16[64,3072]{1,0:T(8,128)(2,1)S(1)}, u32[]{:S(2)}, u32[]{:S(2)}) collective-permute-start(bf16[64,3072]{1,0:T(8,128)(2,1)} %refs_3_.2), channel_id=1, source_target_pairs={{0,1},{1,0},{2,3},{3,2},{4,5},{5,4},{6,7},{7,6},{8,9},{9,8},{10,11... | collective-permute-start | bytes 1179656 | tf_op jit(solution)/shard_map/ppermute | solution.py:67
  6.9 15.1 %collective-permute-start.3 = (bf16[2,256,512]{2,1,0:T(8,128)(2,1)S(1)}, bf16[2,256,512]{2,1,0:T(8,128)(2,1)S(1)}, u32[]{:S(2)}, u32[]{:S(2)}) collective-permute-start(bf16[2,256,512]{2,1,0:T(8,128)(2,1)S(1)} %pad_maximum_fusion.refs_1_.refs_5_), channel_id=1, source_target_pairs={{0,32},{2,6},{4,36},{6,10},{8,40},{10,14},{12,44},{14,2},{16,48},{... | collective-permute-start | bytes 1572872 | tf_op jit(solution)/shard_map/ppermute | solution.py:63
  8.6 13.9 %collective-permute-start.4 = (bf16[2,256,512]{2,1,0:T(8,128)(2,1)S(1)}, bf16[2,256,512]{2,1,0:T(8,128)(2,1)S(1)}, u32[]{:S(2)}, u32[]{:S(2)}) collective-permute-start(bf16[2,256,512]{2,1,0:T(8,128)(2,1)S(1)} %pad_maximum_fusion.refs_1_.refs_5_), channel_id=1, source_target_pairs={{0,96},{2,14},{4,100},{6,2},{8,104},{10,6},{12,108},{14,10},{16,11... | collective-permute-start | bytes 1572872 | tf_op jit(solution)/shard_map/ppermute | solution.py:63
  10.8 13.6 %collective-permute-start.5 = (bf16[2,256,512]{2,1,0:T(8,128)(2,1)S(1)}, bf16[2,256,512]{2,1,0:T(8,128)(2,1)S(1)}, u32[]{:S(2)}, u32[]{:S(2)}) collective-permute-start(bf16[2,256,512]{2,1,0:T(8,128)(2,1)S(1)} %pad_maximum_fusion.refs_1_.refs_5_), channel_id=1, source_target_pairs={{0,64},{2,10},{4,68},{6,14},{8,72},{10,2},{12,76},{14,6},{16,80},{... | collective-permute-start | bytes 1572872 | tf_op jit(solution)/shard_map/ppermute | solution.py:63
  13.0 15.6 %collective-permute-start.9 = (bf16[2,256,512]{2,1,0:T(8,128)(2,1)S(1)}, bf16[2,256,512]{2,1,0:T(8,128)(2,1)S(1)}, u32[]{:S(2)}, u32[]{:S(2)}) collective-permute-start(bf16[2,256,512]{2,1,0:T(8,128)(2,1)S(1)} %pad_maximum_fusion.refs_1_.refs_5_), channel_id=1, source_target_pairs={{0,16},{2,18},{4,20},{6,22},{8,24},{10,26},{12,28},{14,30},{16,0},... | collective-permute-start | bytes 1572872 | tf_op jit(solution)/shard_map/ppermute | solution.py:63
  15.8 2.7 %copy-start = (bf16[64,3072]{1,0:T(8,128)(2,1)S(1)}, bf16[64,3072]{1,0:T(8,128)(2,1)}, u32[]{:S(2)}) copy-start(bf16[64,3072]{1,0:T(8,128)(2,1)} %refs_3_.2) | copy-start | bytes 1179652
  20.3 1.6 %collective-permute-start.2 = (bf16[3,128,128]{2,1,0:T(8,128)(2,1)S(1)}, bf16[3,128,128]{2,1,0:T(8,128)(2,1)S(1)}, u32[]{:S(2)}, u32[]{:S(2)}) collective-permute-start(bf16[3,128,128]{2,1,0:T(8,128)(2,1)S(1)} %get-tuple-element.26), channel_id=1, source_target_pairs={{0,2},{2,0},{4,6},{6,4},{8,10},{10,8},{12,14},{14,12},{16,18},{18,... | collective-permute-start | bytes 294920 | tf_op jit(solution)/shard_map/ppermute | solution.py:63
  24.4 6.4 %collective-permute-start.6 = (bf16[7,128,128]{2,1,0:T(8,128)(2,1)S(1)}, bf16[7,128,128]{2,1,0:T(8,128)(2,1)S(1)}, u32[]{:S(2)}, u32[]{:S(2)}) collective-permute-start(bf16[7,128,128]{2,1,0:T(8,128)(2,1)S(1)} %join_units.1.refs_1_), channel_id=1, source_target_pairs={{0,4},{2,34},{4,8},{6,38},{8,12},{10,42},{12,0},{14,46},{16,20},{1... | collective-permute-start | bytes 688136 | tf_op jit(solution)/shard_map/ppermute | solution.py:63
  25.6 5.2 %collective-permute-start.7 = (bf16[7,128,128]{2,1,0:T(8,128)(2,1)S(1)}, bf16[7,128,128]{2,1,0:T(8,128)(2,1)S(1)}, u32[]{:S(2)}, u32[]{:S(2)}) collective-permute-start(bf16[7,128,128]{2,1,0:T(8,128)(2,1)S(1)} %join_units.1.refs_1_), channel_id=1, source_target_pairs={{0,12},{2,98},{4,0},{6,102},{8,4},{10,106},{12,8},{14,110},{16,28}... | collective-permute-start | bytes 688136 | tf_op jit(solution)/shard_map/ppermute | solution.py:63
  27.1 7.1 %collective-permute-start.8 = (bf16[7,128,128]{2,1,0:T(8,128)(2,1)S(1)}, bf16[7,128,128]{2,1,0:T(8,128)(2,1)S(1)}, u32[]{:S(2)}, u32[]{:S(2)}) collective-permute-start(bf16[7,128,128]{2,1,0:T(8,128)(2,1)S(1)} %join_units.1.refs_1_), channel_id=1, source_target_pairs={{0,8},{2,66},{4,12},{6,70},{8,0},{10,74},{12,4},{14,78},{16,24},{1... | collective-permute-start | bytes 688136 | tf_op jit(solution)/shard_map/ppermute | solution.py:63
  34.2 16.0 %collective-permute-start.10 = (bf16[2,256,512]{2,1,0:T(8,128)(2,1)S(1)}, bf16[2,256,512]{2,1,0:T(8,128)(2,1)S(1)}, u32[]{:S(2)}, u32[]{:S(2)}) collective-permute-start(bf16[2,256,512]{2,1,0:T(8,128)(2,1)S(1)} %gate.1.refs_9_.refs_7_), channel_id=1, source_target_pairs={{0,32},{2,6},{4,36},{6,10},{8,40},{10,14},{12,44},{14,2},{16,48},{... | collective-permute-start | bytes 1572872 | tf_op jit(solution)/shard_map/ppermute | solution.py:63
  34.8 15.5 %collective-permute-start.11 = (bf16[2,256,512]{2,1,0:T(8,128)(2,1)S(1)}, bf16[2,256,512]{2,1,0:T(8,128)(2,1)S(1)}, u32[]{:S(2)}, u32[]{:S(2)}) collective-permute-start(bf16[2,256,512]{2,1,0:T(8,128)(2,1)S(1)} %gate.1.refs_9_.refs_7_), channel_id=1, source_target_pairs={{0,96},{2,14},{4,100},{6,2},{8,104},{10,6},{12,108},{14,10},{16,11... | collective-permute-start | bytes 1572872 | tf_op jit(solution)/shard_map/ppermute | solution.py:63
  36.9 13.4 %collective-permute-start.12 = (bf16[2,256,512]{2,1,0:T(8,128)(2,1)S(1)}, bf16[2,256,512]{2,1,0:T(8,128)(2,1)S(1)}, u32[]{:S(2)}, u32[]{:S(2)}) collective-permute-start(bf16[2,256,512]{2,1,0:T(8,128)(2,1)S(1)} %gate.1.refs_9_.refs_7_), channel_id=1, source_target_pairs={{0,64},{2,10},{4,68},{6,14},{8,72},{10,2},{12,76},{14,6},{16,80},{... | collective-permute-start | bytes 1572872 | tf_op jit(solution)/shard_map/ppermute | solution.py:63
  42.9 25.3 %slice-start = ((s8[5505024]{0:T(1024)(128)(4,1)}), s8[4194304]{0:T(1024)(128)(4,1)S(1)}, s32[]{:S(2)}) async-start(s8[5505024]{0:T(1024)(128)(4,1)} %bitcast.9), calls=%async_computation | async-start | bytes 8388608
  42.9 25.3 %slice-start.1 = ((s8[5505024]{0:T(1024)(128)(4,1)}), s8[1310720]{0:T(1024)(128)(4,1)S(1)}, s32[]{:S(2)}) async-start(s8[5505024]{0:T(1024)(128)(4,1)} %bitcast.9), calls=%async_computation.1 | async-start | bytes 2621440
  54.2 6.9 %collective-permute-start.17 = (bf16[8,64,128]{2,1,0:T(8,128)(2,1)S(1)}, bf16[8,64,128]{2,1,0:T(8,128)(2,1)S(1)}, u32[]{:S(2)}, u32[]{:S(2)}) collective-permute-start(bf16[8,64,128]{2,1,0:T(8,128)(2,1)S(1)} %get-tuple-element.41), channel_id=1, source_target_pairs={{0,12},{2,98},{4,0},{6,102},{8,4},{10,106},{12,8},{14,110},{16,28}... | collective-permute-start | bytes 393224 | tf_op jit(solution)/shard_map/ppermute | solution.py:63
  55.9 6.4 %collective-permute-start.18 = (bf16[8,64,128]{2,1,0:T(8,128)(2,1)S(1)}, bf16[8,64,128]{2,1,0:T(8,128)(2,1)S(1)}, u32[]{:S(2)}, u32[]{:S(2)}) collective-permute-start(bf16[8,64,128]{2,1,0:T(8,128)(2,1)S(1)} %get-tuple-element.42), channel_id=1, source_target_pairs={{0,4},{2,34},{4,8},{6,38},{8,12},{10,42},{12,0},{14,46},{16,20},{1... | collective-permute-start | bytes 393224 | tf_op jit(solution)/shard_map/ppermute | solution.py:63
  55.9 6.4 %collective-permute-start.19 = (bf16[8,64,128]{2,1,0:T(8,128)(2,1)S(1)}, bf16[8,64,128]{2,1,0:T(8,128)(2,1)S(1)}, u32[]{:S(2)}, u32[]{:S(2)}) collective-permute-start(bf16[8,64,128]{2,1,0:T(8,128)(2,1)S(1)} %get-tuple-element.43), channel_id=1, source_target_pairs={{0,8},{2,66},{4,12},{6,70},{8,0},{10,74},{12,4},{14,78},{16,24},{1... | collective-permute-start | bytes 393224 | tf_op jit(solution)/shard_map/ppermute | solution.py:63
  62.8 5.4 %collective-permute-start.20 = (bf16[4,64,128]{2,1,0:T(8,128)(2,1)S(1)}, bf16[4,64,128]{2,1,0:T(8,128)(2,1)S(1)}, u32[]{:S(2)}, u32[]{:S(2)}) collective-permute-start(bf16[4,64,128]{2,1,0:T(8,128)(2,1)S(1)} %get-tuple-element.46), channel_id=1, source_target_pairs={{0,2},{2,0},{4,6},{6,4},{8,10},{10,8},{12,14},{14,12},{16,18},{18,... | collective-permute-start | bytes 196616 | tf_op jit(solution)/shard_map/ppermute | solution.py:63
  70.1 13.9 %collective-permute-start.21 = (bf16[64,3072]{1,0:T(8,128)(2,1)S(1)}, bf16[64,3072]{1,0:T(8,128)(2,1)S(1)}, u32[]{:S(2)}, u32[]{:S(2)}) collective-permute-start(bf16[64,3072]{1,0:T(8,128)(2,1)S(1)} %output_projection.3), channel_id=1, source_target_pairs={{0,1},{1,0},{2,3},{3,2},{4,5},{5,4},{6,7},{7,6},{8,9},{9,8},{10,11... | collective-permute-start | bytes 1179656 | tf_op jit(solution)/shard_map/ppermute | solution.py:67
  70.3 4.2 %collective-permute-start.13 = (bf16[8,64,128]{2,1,0:T(8,128)(2,1)S(1)}, bf16[8,64,128]{2,1,0:T(8,128)(2,1)S(1)}, u32[]{:S(2)}, u32[]{:S(2)}) collective-permute-start(bf16[8,64,128]{2,1,0:T(8,128)(2,1)S(1)} %get-tuple-element.33), channel_id=1, source_target_pairs={{0,12},{2,98},{4,0},{6,102},{8,4},{10,106},{12,8},{14,110},{16,28}... | collective-permute-start | bytes 393224 | tf_op jit(solution)/shard_map/ppermute | solution.py:63
  72.5 6.7 %collective-permute-start.14 = (bf16[8,64,128]{2,1,0:T(8,128)(2,1)S(1)}, bf16[8,64,128]{2,1,0:T(8,128)(2,1)S(1)}, u32[]{:S(2)}, u32[]{:S(2)}) collective-permute-start(bf16[8,64,128]{2,1,0:T(8,128)(2,1)S(1)} %get-tuple-element.34), channel_id=1, source_target_pairs={{0,4},{2,34},{4,8},{6,38},{8,12},{10,42},{12,0},{14,46},{16,20},{1... | collective-permute-start | bytes 393224 | tf_op jit(solution)/shard_map/ppermute | solution.py:63
  72.5 6.7 %collective-permute-start.15 = (bf16[8,64,128]{2,1,0:T(8,128)(2,1)S(1)}, bf16[8,64,128]{2,1,0:T(8,128)(2,1)S(1)}, u32[]{:S(2)}, u32[]{:S(2)}) collective-permute-start(bf16[8,64,128]{2,1,0:T(8,128)(2,1)S(1)} %get-tuple-element.35), channel_id=1, source_target_pairs={{0,8},{2,66},{4,12},{6,70},{8,0},{10,74},{12,4},{14,78},{16,24},{1... | collective-permute-start | bytes 393224 | tf_op jit(solution)/shard_map/ppermute | solution.py:63
  79.7 2.5 %collective-permute-start.16 = (bf16[4,64,128]{2,1,0:T(8,128)(2,1)S(1)}, bf16[4,64,128]{2,1,0:T(8,128)(2,1)S(1)}, u32[]{:S(2)}, u32[]{:S(2)}) collective-permute-start(bf16[4,64,128]{2,1,0:T(8,128)(2,1)S(1)} %get-tuple-element.38), channel_id=1, source_target_pairs={{0,2},{2,0},{4,6},{6,4},{8,10},{10,8},{12,14},{14,12},{16,18},{18,... | collective-permute-start | bytes 196616 | tf_op jit(solution)/shard_map/ppermute | solution.py:63

commit v3 on v2

--- a/solution.py
+++ b/solution.py
@@ -67,11 +67,13 @@
     return lax.ppermute(array, "head", [(0, 1), (1, 0)])
 
 
-def kernel_call(kernel, name, out_shape, scratch_shapes, scalars, *arrays, after=(), outside=(), limit=12):
-    first, count = len(scalars) + len(outside) + len(arrays), len(after)
+def kernel_call(kernel, name, out_shape, scratch_shapes, place, scalars, *arrays, after=(), outside=(), limit=12):
+    scalars = [*place, *scalars]
+    begin, first, count = len(place), len(scalars) + len(outside) + len(arrays), len(after)
 
     def run(*refs):
-        kernel(*refs[:first], *refs[first + count :])
+        head = [[ref[0] for ref in refs[:begin]]] if begin else []
+        kernel(*head, *refs[begin:first], *refs[first + count :])
 
     return pl.pallas_call(
         run,
@@ -105,15 +107,18 @@
     return groups
 
 
-def _stage_kernel(w_ref, out_ref, sems):
+def _stage_kernel(w_ref, image_ref, out_ref, own_ref, sems, sem):
+    bring = pltpu.make_async_copy(image_ref, own_ref, sem)
+    bring.start()
     for copy in _bring(w_ref, (0,), out_ref, sems)[0]:
         copy.wait()
-
-
-def stage(w, after):
-    scratch = [pltpu.SemaphoreType.DMA((PIECES,))]
-    outs = [((1, D, FEAT), BF16)]
-    return kernel_call(_stage_kernel, "stage_weights", outs, scratch, [], outside=[w], after=after)[0]
+    bring.wait()
+
+
+def stage(w, image, after):
+    scratch = [pltpu.SemaphoreType.DMA((PIECES,)), pltpu.SemaphoreType.DMA(())]
+    outs = [((1, D, FEAT), BF16), (image.shape, BF16)]
+    return kernel_call(_stage_kernel, "stage", outs, scratch, [], [], outside=[w, image], after=after)
 
 
 def _query_kernel(place, w_ref, oth_ref, own_ref, table_ref, qa_ref, qb_ref, q_ref, x_ref):
@@ -140,35 +145,32 @@
         ((HEADS, TOK, HD), BF16),
         ((TOK, D), BF16),
     ]
-    return kernel_call(_query_kernel, "query_projection", outs, [], [place], *arrays)
+    return kernel_call(_query_kernel, "query_projection", outs, [], place, [], *arrays)
 
 
 def _home_kernel(
-    place, count, w_ref, text_ref, x_ref, table_ref, q_ref, out_ref, home_ref, stat_ref, buffer, text, part, sems
+    place, count, text_ref, w_ref, x_ref, table_ref, q_ref, out_ref, home_ref, stat_ref, text, s_ref, buffer, sem, sems
 ):
-    bring_text = pltpu.make_async_copy(text_ref, text, sems.at[2 * PIECES])
-    bring_text.start()
+    bring = pltpu.make_async_copy(text_ref, text, sem)
+    bring.start()
     groups = _bring(w_ref, (1, 2), buffer, sems)
+    slots = text.shape[1]
     first = pl.ds(pl.multiple_of((1 - place[1]) * HALF, HALF), HALF)
     second = pl.ds(pl.multiple_of(place[1] * HALF, HALF), HALF)
-    bring_text.wait()
-    peaks = []
+    bring.wait()
     for head in range(HEADS):
         at = slice(head * HD, (head + 1) * HD)
         s = _scores(q_ref[head], text[0, :, at])
-        s = jnp.where(_lane(s.shape) < count[0], s, -jnp.inf)
-        peak, part[head] = _fold(s, None, text[1, :, at])
-        peaks.append(peak)
+        s_ref[head, :, :slots] = jnp.where(_lane(s.shape) < count[0], s, -jnp.inf)
     for copy in groups[0]:
         copy.wait()
     projected = jnp.dot(x_ref[...], buffer[0], preferred_element_type=F32)
-    keys = []
     for head in range(HEADS):
         at = slice(head * HD, (head + 1) * HD)
         k = _turn(projected[:, at], table_ref, 1).astype(BF16)
         out_ref[0, first, at] = k[:HALF]
         out_ref[0, second, at] = k[HALF:]
-        keys.append(k)
+        s_ref[head, :, slots:] = _scores(q_ref[head], k)
     for copy in groups[1]:
         copy.wait()
     v = jnp.dot(x_ref[...], buffer[1], preferred_element_type=F32).astype(BF16)
@@ -177,31 +179,31 @@
     stat = jnp.zeros((TOK, HD), F32)
     for head in range(HEADS):
         at = slice(head * HD, (head + 1) * HD)
-        peak, out = _fold(_scores(q_ref[head], keys[head]), peaks[head], v[:, at])
-        out = out + part[head] * jnp.exp2(peaks[head] - peak)
+        peak, out = _fold(s_ref[head], None, jnp.concatenate([text[1, :, at], v[:, at]], axis=0))
         total = out[:, HD:]
         home_ref[head] = (out[:, :HD] / total).astype(BF16)
         stat = jnp.where(_lane(stat.shape) == head, peak + jnp.log2(total), stat)
     stat_ref[...] = stat
 
 
-def attend_home(place, count, w, text_kv, *arrays, after):
+def attend_home(place, count, text_kv, w, *arrays, after):
     outs = [((2, TOK, FEAT), BF16, HBM), ((HEADS, TOK, HD), BF16), ((TOK, HD), F32)]
     scratch = [
+        (text_kv.shape, BF16),
+        ((HEADS, TOK, text_kv.shape[1] + TOK), F32),
         ((2, D, FEAT), BF16),
-        (text_kv.shape, BF16),
-        ((HEADS, TOK, 2 * HD), F32),
-        pltpu.SemaphoreType.DMA((2 * PIECES + 1,)),
+        pltpu.SemaphoreType.DMA(()),
+        pltpu.SemaphoreType.DMA((2 * PIECES,)),
     ]
-    outside = [w, text_kv]
     return kernel_call(
         _home_kernel,
         "home_attention",
         outs,
         scratch,
-        [place, count],
+        place,
+        [count],
         *arrays,
-        outside=outside,
+        outside=[text_kv, w],
         after=after,
         limit=24,
     )
@@ -231,7 +233,7 @@
 
 def join_units(a, b, after):
     outs = [((UNITS, TOK, HD), BF16)]
-    return kernel_call(_join_kernel, "join_units", outs, [], [], a, b, after=after)[0]
+    return kernel_call(_join_kernel, "join_units", outs, [], [], [], a, b, after=after)[0]
 
 
 def _scores(q, k):
@@ -269,6 +271,15 @@
     return (u if u < MINE else u - MINE - 1) + c
 
 
+ORDER = ((1, 2, 3, 0), (0, 1, 2, 3))
+OWN = (slice(3 * HALF, 4 * HALF), slice(0, HALF))
+ROWS = (((1, 0), (2, 0), (3, 0)), ((0, 0), (0, 1), (1, 1), (2, 1), (3, 1)))
+
+
+def _gather(refs, u, rows):
+    return jnp.concatenate([refs[i][u, g * HALF : (g + 1) * HALF] for i, g in rows], axis=0)
+
+
 def _near_kernel(place, *refs):
     queries, keys = refs[:4], refs[4:8]
     acc_ref, stat_ref, s_ref = refs[8:]
@@ -277,12 +288,12 @@
 
     def score(i):
         u, g = steps[i]
-        q = jnp.concatenate([r[u, g * HALF : (g + 1) * HALF] for r in queries], axis=0)
+        q = _gather(queries, u, [(r, g) for r in ORDER[g]])
         for b, k in enumerate(keys):
             s = _scores(q, k[0, :, _cols(_slot_of(u, c))])
             s_ref[i % 2, :, b * 2 * TOK : (b + 1) * 2 * TOK] = s
         patch = slice(0, TOK) if u <= MINE else slice(TOK, 2 * TOK)
-        s_ref[i % 2, :HALF, patch] = jnp.full((HALF, TOK), -jnp.inf, F32)
+        s_ref[i % 2, OWN[g], patch] = jnp.full((HALF, TOK), -jnp.inf, F32)
 
     stats = [jnp.zeros((4 * HALF, HD), F32)] * 2
     score(0)
@@ -300,22 +311,23 @@
 def attend_near(place, queries, pairs, after):
     outs = [((UNITS, 4 * TOK, HD), F32), ((4 * TOK, HD), F32)]
     scratch = [((2, 4 * HALF, 8 * TOK), F32)]
-    return kernel_call(_near_kernel, "near_attention", outs, scratch, [place], *queries, *pairs, after=after)
+    return kernel_call(_near_kernel, "near_attention", outs, scratch, place, [], *queries, *pairs, after=after)
 
 
 def _far_kernel(g, place, *refs):
     queries, (acc_in, stat_in), keys = refs[:4], refs[4:6], refs[6:10]
-    outs, s_ref = refs[10:14], refs[14]
+    outs, s_ref = refs[10:-1], refs[-1]
     c = place[0]
-    rows = slice(g * 4 * HALF, (g + 1) * 4 * HALF)
+    count = len(ROWS[g]) * HALF
+    rows = slice(0, count) if g == 0 else slice(4 * TOK - count, 4 * TOK)
 
     def score(u):
-        q = jnp.concatenate([r[u, g * HALF : (g + 1) * HALF] for r in queries], axis=0)
+        q = _gather(queries, u, ROWS[g])
         for b, k in enumerate(keys):
             s = _scores(q, k[0, :, _cols(_slot_of(u, c))])
             s_ref[u % 2, :, b * 2 * TOK : (b + 1) * 2 * TOK] = s
 
-    mark = jnp.zeros((4 * HALF, HD), F32)
+    mark = jnp.zeros((count, HD), F32)
     score(0)
     for u in range(UNITS):
         if u + 1 < UNITS:
@@ -327,20 +339,26 @@
         total = stat_in[rows, u + 16 : u + 17] * factor + out[:, HD:]
         out = ((acc_in[u, rows] * factor + out[:, :HD]) / total).astype(BF16)
         level = peak + jnp.log2(total)
-        lane = _lane(level.shape)
-        mark = jnp.where(lane % 16 == u, level, mark)
-        for i, o in enumerate(outs):
-            o[u] = out[i * HALF : (i + 1) * HALF]
-    mark = _spread(mark)
-    for i, o in enumerate(outs):
-        o[UNITS] = mark[i * HALF : (i + 1) * HALF]
+        mark = jnp.where(_lane(level.shape) % 16 == u, level, mark)
+        _deal(outs, u, out)
+    _deal(outs, UNITS, _spread(mark))
+
+
+def _deal(outs, u, rows):
+    at = 0
+    for o in outs:
+        o[u] = rows[at : at + o.shape[1]]
+        at += o.shape[1]
 
 
 def attend_far(g, place, queries, acc, stat, pairs, after):
-    outs = [((UNITS + 1, HALF, HD), BF16)] * 4
-    scratch = [((2, 4 * HALF, 8 * TOK), F32)]
+    outs = [((UNITS + 1, HALF, HD), BF16)] * 3
+    if g == 1:
+        outs = [((UNITS + 1, TOK, HD), BF16)] + outs
+    scratch = [((2, len(ROWS[g]) * HALF, 8 * TOK), F32)]
     kernel = functools.partial(_far_kernel, g)
-    return kernel_call(kernel, f"far_attention_{g}", outs, scratch, [place], *queries, acc, stat, *pairs, after=after)
+    arrays = (*queries, acc, stat, *pairs)
+    return kernel_call(kernel, f"far_attention_{g}", outs, scratch, place, [], *arrays, after=after)
 
 
 def _spread(level):
@@ -356,8 +374,8 @@
     return mark + pltpu.roll(mark, HD - 16, 1) + pltpu.roll(mark, HD - 32, 1)
 
 
-def _merge_kernel(p0, p1, p2, p3, mine_ref, stat_ref, sib_ref):
-    parts = (p0, p1, p2, p3)
+def _merge_kernel(g, p0, p1, p2, p3, mine_ref, stat_ref, sib_ref):
+    parts = (p0.at[:, g * HALF : (g + 1) * HALF], p1, p2, p3)
     levels = [_collect(p[UNITS]) for p in parts]
     top = functools.reduce(jnp.maximum, levels)
     weights = [jnp.exp2(v - top) for v in levels]
@@ -379,12 +397,13 @@
     sib_ref[MINE] = _spread(level + pltpu.roll(level, 16, 1) + pltpu.roll(level, 32, 1))
 
 
-def merge(parts, after):
+def merge(g, parts):
     outs = [((MINE + 1, HALF, HD), BF16), ((HALF, HD), F32), ((MINE + 1, HALF, HD), BF16)]
-    return kernel_call(_merge_kernel, "merge_parts", outs, [], [], *parts, after=after)
-
-
-def _out_kernel(g, place, mine_ref, stat_ref, got_ref, home_ref, level_ref, w_ref, out_ref):
+    return kernel_call(functools.partial(_merge_kernel, g), "merge_parts", outs, [], [], [], *parts)
+
+
+def _out_kernel(g, place, mine_ref, stat_ref, got_ref, home_ref, level_ref, w_ref, *rest):
+    *other, out_ref = rest
     rows = slice(g * HALF, (g + 1) * HALF)
     first = place[0] == 0
     mine = stat_ref[...]
@@ -406,13 +425,15 @@
         out = a.astype(F32) * (wa / total) + h.astype(F32) * (wh / total)
         attended.append(out.astype(BF16))
     out = jnp.dot(jnp.concatenate(attended, axis=1), w_ref[...], preferred_element_type=F32)
-    out_ref[...] = out.astype(out_ref.dtype)
-
-
-def project_out(g, place, kind, *arrays):
-    outs = [((HALF, D), kind, HBM)]
+    for ref in other:
+        out = out + ref[...].astype(F32)
+    out_ref[...] = out.astype(BF16)
+
+
+def project_out(g, place, *arrays, after):
+    outs = [((HALF, D), BF16, HBM)]
     kernel = functools.partial(_out_kernel, g)
-    return kernel_call(kernel, "output_projection", outs, [], [place], *arrays)[0]
+    return kernel_call(kernel, "output_projection", outs, [], place, [], *arrays, after=after)[0]
 
 
 def _bands():
@@ -430,7 +451,7 @@
 def body(image, w_qkv, qk_gain, stale_kv, text_kv, text_count, row_offset, w_out):
     core = lax.axis_index("patch") % 2
     group = lax.axis_index("head")
-    place = jnp.stack([core, group]).astype(jnp.int32)
+    place = [core.astype(jnp.int32).reshape(1), group.astype(jnp.int32).reshape(1)]
     other_image = swap_heads(image)
 
     wide = (2, TOK, (MINE + 1) * HD)
@@ -452,22 +473,23 @@
     table = jnp.stack([qk_gain[0] * cosine, swapped[0] * sine, qk_gain[1] * cosine, swapped[1] * sine])
 
     w = jnp.transpose(w_qkv, (1, 0, 2))
-    q_mine, q_given, q_own, x = project_queries(place, stage(w, [pair]), other_image, image, table)
-    units = join_units(q_mine, move(q_given, _core_move), near[1:4])
+    staged, own_image = stage(w, image, [pair])
+    q_mine, q_given, q_own, x = project_queries(place, staged, other_image, own_image, table)
+    units = join_units(q_mine, move(q_given, _core_move), near[1:3])
     queries = [units] + [move(units, _query_move(d)) for d in (1, 3, 2)]
-    far_pair = gate(far_pair, queries[1:4])
-    far = [far_pair] + [move(far_pair, _key_move(d)) for d in (1, 3, 2)]
+    far_two = move(near[3], _y_move)
+    fresh_kv, home, level = attend_home(place, text_count, text_kv, w, x, table, q_own, after=[units, near[3]])
+    far_pair = gate(far_pair, queries[1:4] + [home])
+    far = [far_pair] + [move(far_pair, _key_move(d)) for d in (1, 3)] + [far_two]
     acc, stat = attend_near(place, queries, near, [far_pair])
-    fresh_kv, home, level = attend_home(place, text_count, w, text_kv, x, table, q_own, after=[acc])
-
-    parts = [attend_far(g, place, queries, acc, stat, far, [home]) for g in (0, 1)]
-    halves = []
-    for g, kind in ((0, BF16), (1, F32)):
-        back = [parts[g][0]] + [move(parts[g][i], _query_move(d)) for i, d in ((1, 3), (2, 1), (3, 2))]
-        mine, mine_stat, given_back = merge(back, parts[1][:1] if g == 0 else [])
-        got = move(given_back, _core_move)
-        halves.append(project_out(g, place, kind, mine, mine_stat, got, home, level, w_out))
-    mixed = (halves[1] + swap_heads(halves[0]).astype(F32)).astype(BF16)
+
+    first = attend_far(0, place, queries, acc, stat, far, [])
+    own, *second = attend_far(1, place, queries, acc, stat, far, [])
+    back = [[own] + [move(p, _query_move(d)) for p, d in zip(parts, (3, 1, 2))] for parts in (first, second)]
+    merged = [merge(g, back[g]) for g in (0, 1)]
+    got = [move(merged[g][2], _core_move) for g in (0, 1)]
+    sent = project_out(0, place, *merged[0][:2], got[0], home, level, w_out, after=[])
+    mixed = project_out(1, place, *merged[1][:2], got[1], home, level, w_out, swap_heads(sent), after=[])
     return (mixed, fresh_kv)
 
 

time: 85 us -> 79.2 us (0.932)
  waiting for transfers between devices: 16.7 us -> 10.4 us
  starting transfers between devices: 32 us -> 34.5 us
  Pallas kernels: 29.4 us -> 28.1 us
  other arithmetic: 2 us -> 1.09 us
    ppermute x20, waiting for transfers between devices: 16.7 us -> 10.4 us  [move(): return lax.ppermute(array, 'patch', _perm(how))]
    ppermute x20, starting transfers between devices: 30.4 us -> 33 us  [move(): return lax.ppermute(array, 'patch', _perm(how))]
    pallas_call x11, Pallas kernels: 29.4 us -> 28.1 us  [kernel_call(): pl.pallas_call(run, in_specs=[SMEM] * len(scalars) + [ANY] * len(outside)...]
  transfers between devices with their start and end apart: 22 -> 22, of which waited for: 9 -> 8; matrix products, arithmetic and copies ran while one was open for 3% -> 3% of each run, Pallas kernels for 27% -> 27%
where the time goes in v3:
time: 79.2 us; the launch traced here: 78.9 us
  starting transfers between devices  34.5 us (44%)
  Pallas kernels  28.1 us (35%)
  waiting for transfers between devices  10.4 us (13%)
  local copies, waits for them, and re-layouts  2.56 us (3%)
  between operations  2.18 us (3%)
  other arithmetic  1.09 us (1%)
    ppermute x20, starting transfers between devices, move(): return lax.ppermute(array, 'patch', _perm(how))  33 us
    pallas_call x11, Pallas kernels, kernel_call(): pl.pallas_call(run, in_specs=[SMEM] * len(scalars) + [ANY] * len(outside)...  28.1 us
    ppermute x20, waiting for transfers between devices, move(): return lax.ppermute(array, 'patch', _perm(how))  10.4 us
  transfers between devices with their start and end apart: 22, of which 8 were waited for; matrix products, arithmetic and copies ran while one was open for 3% of the time, Pallas kernels for 27%

profile of v3, /device:TPU:1, one launch (start us, length us, event | category | flops | bytes accessed | tf_op | source)
XLA Modules:
  0.0 78.9 jit_solution(10822170732031567637)
XLA Ops:
  0.7 1.1 %constant_dynamic-slice_fusion.1 = (bf16[2,128,512]{2,1,0:T(8,128)(2,1)S(1)}, bf16[2,128,512]{2,1,0:T(8,128)(2,1)S(1)}) fusion(bf16[2,128,896]{2,1,0:T(8,128)(2,1)} %param.14, s32[]{:T(128)S(6)} %select_n.43, s32[]{:T(128)S(6)} %select_n.44), kind=kLoop, calls=%fused_computation.18 | loop fusion | bytes 1048584 | tf_op jit(solution)/shard_map/dynamic_slice | solution.py:459
  1.7 1.5 %collective-permute-start = (bf16[2,128,512]{2,1,0:T(8,128)(2,1)S(1)}, bf16[2,128,512]{2,1,0:T(8,128)(2,1)S(1)}, u32[]{:S(2)}, u32[]{:S(2)}) collective-permute-start(bf16[2,128,512]{2,1,0:T(8,128)(2,1)S(1)} %get-tuple-element.53), channel_id=1, source_target_pairs={{0,2},{2,0},{4,6},{6,4},{8,10},{10,8},{12,14},{14,12},{16,18},{18,... | collective-permute-start | bytes 786440 | tf_op jit(solution)/shard_map/ppermute | solution.py:63
  3.2 1.4 %collective-permute-start.1 = (bf16[64,3072]{1,0:T(8,128)(2,1)}, bf16[64,3072]{1,0:T(8,128)(2,1)S(1)}, u32[]{:S(2)}, u32[]{:S(2)}) collective-permute-start(bf16[64,3072]{1,0:T(8,128)(2,1)} %refs_1_.1), channel_id=1, source_target_pairs={{0,1},{1,0},{2,3},{3,2},{4,5},{5,4},{6,7},{7,6},{8,9},{9,8},{10,11... | collective-permute-start | bytes 1179656 | tf_op jit(solution)/shard_map/ppermute | solution.py:67
  5.3 0.8 slice_reduce_fusion.1
  6.1 1.7 %collective-permute-start.3 = (bf16[2,256,512]{2,1,0:T(8,128)(2,1)S(1)}, bf16[2,256,512]{2,1,0:T(8,128)(2,1)S(1)}, u32[]{:S(2)}, u32[]{:S(2)}) collective-permute-start(bf16[2,256,512]{2,1,0:T(8,128)(2,1)S(1)} %pad_maximum_fusion.refs_2_.refs_6_), channel_id=1, source_target_pairs={{0,32},{2,6},{4,36},{6,10},{8,40},{10,14},{12,44},{14,2},{16,48},{... | collective-permute-start | bytes 1572872 | tf_op jit(solution)/shard_map/ppermute | solution.py:63
  7.8 2.2 %collective-permute-start.4 = (bf16[2,256,512]{2,1,0:T(8,128)(2,1)S(1)}, bf16[2,256,512]{2,1,0:T(8,128)(2,1)S(1)}, u32[]{:S(2)}, u32[]{:S(2)}) collective-permute-start(bf16[2,256,512]{2,1,0:T(8,128)(2,1)S(1)} %pad_maximum_fusion.refs_2_.refs_6_), channel_id=1, source_target_pairs={{0,96},{2,14},{4,100},{6,2},{8,104},{10,6},{12,108},{14,10},{16,11... | collective-permute-start | bytes 1572872 | tf_op jit(solution)/shard_map/ppermute | solution.py:63
  10.7 1.3 %collective-permute-start.8 = (bf16[2,256,512]{2,1,0:T(8,128)(2,1)S(1)}, bf16[2,256,512]{2,1,0:T(8,128)(2,1)S(1)}, u32[]{:S(2)}, u32[]{:S(2)}) collective-permute-start(bf16[2,256,512]{2,1,0:T(8,128)(2,1)S(1)} %pad_maximum_fusion.refs_2_.refs_6_), channel_id=1, source_target_pairs={{0,64},{2,10},{4,68},{6,14},{8,72},{10,2},{12,76},{14,6},{16,80},{... | collective-permute-start | bytes 1572872 | tf_op jit(solution)/shard_map/ppermute | solution.py:63
  12.1 2.6 %collective-permute-start.9 = (bf16[2,256,512]{2,1,0:T(8,128)(2,1)S(1)}, bf16[2,256,512]{2,1,0:T(8,128)(2,1)S(1)}, u32[]{:S(2)}, u32[]{:S(2)}) collective-permute-start(bf16[2,256,512]{2,1,0:T(8,128)(2,1)S(1)} %pad_maximum_fusion.refs_2_.refs_6_), channel_id=1, source_target_pairs={{0,16},{2,18},{4,20},{6,22},{8,24},{10,26},{12,28},{14,30},{16,0},... | collective-permute-start | bytes 1572872 | tf_op jit(solution)/shard_map/ppermute | solution.py:63
  14.7 1.0 %fusion.4 = (f32[1,128,128]{2,1,0:T(8,128)S(1)}, f32[1,128,128]{2,1,0:T(8,128)S(1)}, f32[1,128,128]{2,1,0:T(8,128)S(1)}, f32[1,128,128]{2,1,0:T(8,128)S(1)}) fusion(f32[128]{0:T(128)} %constant.66.clone, f32[128]{0:T(128)S(1)} %mul.175, f32[128]{0:T(128)} %constant.65.clone, f32[128]{0:T(128)S(1)} %get-tuple-element.60, f32[128]{0:T(128)} %constant.64.clone, ...), kind=kLoop, calls=%fused_computation.8 | loop fusion | flops 131072 | bytes 266752 | tf_op jit(solution)/shard_map/mul | solution.py:473
  15.7 2.7 %stage.1 = (bf16[1,3072,896]{2,1,0:T(8,128)(2,1)S(1)}, bf16[64,3072]{1,0:T(8,128)(2,1)S(1)}) custom-call(bf16[3,3072,896]{2,1,0:T(8,128)(2,1)} %bitcast.11, bf16[64,3072]{1,0:T(8,128)(2,1)} %refs_1_.1, bf16[2,256,512]{2,1,0:T(8,128)(2,1)S(1)} %pad_maximum_fusion.refs_2_.refs_6_), custom_call_target="tpu_custom_call" | custom-call | flops 1 | bytes 1 | tf_op jit(solution)/shard_map/stage/pallas_call | solution.py:78
  18.5 1.3 %query_projection.1 = (bf16[4,128,128]{2,1,0:T(8,128)(2,1)S(1)}, bf16[3,128,128]{2,1,0:T(8,128)(2,1)S(1)}, bf16[7,128,128]{2,1,0:T(8,128)(2,1)S(1)}, bf16[128,3072]{1,0:T(8,128)(2,1)S(1)}) custom-call(s32[1]{0:T(128)} %bitcast.refs_0_, s32[1]{0:T(128)} %bitcast.1.refs_1_, bf16[1,3072,896]{2,1,0:T(8,128)(2,1)S(1)} %get-tuple-element.26.refs_2_, ...), custom_call_target="tpu_custom_call" | custom-call | flops 1 | bytes 1 | tf_op jit(solution)/shard_map/query_projection/pallas_call | solution.py:78
  20.5 0.9 %collective-permute-done.2.refs_1_ = bf16[3,128,128]{2,1,0:T(8,128)(2,1)S(1)} collective-permute-done((bf16[3,128,128]{2,1,0:T(8,128)(2,1)S(1)}, bf16[3,128,128]{2,1,0:T(8,128)(2,1)S(1)}, u32[]{:S(2)}, u32[]{:S(2)}) %collective-permute-start.2) | collective-permute-done | bytes 98336 | tf_op jit(solution)/shard_map/ppermute | solution.py:63
  21.8 1.3 %collective-permute-start.5 = (bf16[7,128,128]{2,1,0:T(8,128)(2,1)S(1)}, bf16[7,128,128]{2,1,0:T(8,128)(2,1)S(1)}, u32[]{:S(2)}, u32[]{:S(2)}) collective-permute-start(bf16[7,128,128]{2,1,0:T(8,128)(2,1)S(1)} %join_units.1.refs_8_.refs_2_), channel_id=1, source_target_pairs={{0,4},{2,34},{4,8},{6,38},{8,12},{10,42},{12,0},{14,46},{16,20},{1... | collective-permute-start | bytes 688136 | tf_op jit(solution)/shard_map/ppermute | solution.py:63
  23.1 1.5 %collective-permute-start.6 = (bf16[7,128,128]{2,1,0:T(8,128)(2,1)S(1)}, bf16[7,128,128]{2,1,0:T(8,128)(2,1)S(1)}, u32[]{:S(2)}, u32[]{:S(2)}) collective-permute-start(bf16[7,128,128]{2,1,0:T(8,128)(2,1)S(1)} %join_units.1.refs_8_.refs_2_), channel_id=1, source_target_pairs={{0,12},{2,98},{4,0},{6,102},{8,4},{10,106},{12,8},{14,110},{16,28}... | collective-permute-start | bytes 688136 | tf_op jit(solution)/shard_map/ppermute | solution.py:63
  24.5 1.5 %collective-permute-start.7 = (bf16[7,128,128]{2,1,0:T(8,128)(2,1)S(1)}, bf16[7,128,128]{2,1,0:T(8,128)(2,1)S(1)}, u32[]{:S(2)}, u32[]{:S(2)}) collective-permute-start(bf16[7,128,128]{2,1,0:T(8,128)(2,1)S(1)} %join_units.1.refs_8_.refs_2_), channel_id=1, source_target_pairs={{0,8},{2,66},{4,12},{6,70},{8,0},{10,74},{12,4},{14,78},{16,24},{1... | collective-permute-start | bytes 688136 | tf_op jit(solution)/shard_map/ppermute | solution.py:63
  26.7 2.7 %collective-permute-start.12 = (bf16[2,256,512]{2,1,0:T(8,128)(2,1)S(1)}, bf16[2,256,512]{2,1,0:T(8,128)(2,1)S(1)}, u32[]{:S(2)}, u32[]{:S(2)}) collective-permute-start(bf16[2,256,512]{2,1,0:T(8,128)(2,1)S(1)} %collective-permute-done.8.refs_9_), channel_id=1, source_target_pairs={{0,16},{2,18},{4,20},{6,22},{8,24},{10,26},{12,28},{14,30},{16,0},... | collective-permute-start | bytes 1572872 | tf_op jit(solution)/shard_map/ppermute | solution.py:63
  29.4 8.3 %home_attention.1 = (bf16[2,128,896]{2,1,0:T(8,128)(2,1)}, bf16[7,128,128]{2,1,0:T(8,128)(2,1)S(1)}, f32[128,128]{1,0:T(8,128)S(1)}) custom-call(s32[1]{0:T(128)} %bitcast.refs_0_, s32[1]{0:T(128)} %bitcast.1.refs_1_, s32[1]{0:T(128)S(6)} %copy.15.refs_2_, bf16[2,512,896]{2,1,0:T(8,128)(2,1)} %refs_3_.1, bf16[3,3072,896]{2,1,0:T(8,128)(2,1)} %bitcast.12, ...), custom_call_target="tpu_custom_call" | custom-call | flops 1 | bytes 1 | tf_op jit(solution)/shard_map/home_attention/pallas_call | solution.py:78
  37.9 3.5 %collective-permute-start.11 = (bf16[2,256,512]{2,1,0:T(8,128)(2,1)S(1)}, bf16[2,256,512]{2,1,0:T(8,128)(2,1)S(1)}, u32[]{:S(2)}, u32[]{:S(2)}) collective-permute-start(bf16[2,256,512]{2,1,0:T(8,128)(2,1)S(1)} %gate.1.refs_10_.refs_8_), channel_id=1, source_target_pairs={{0,96},{2,14},{4,100},{6,2},{8,104},{10,6},{12,108},{14,10},{16,11... | collective-permute-start | bytes 1572872 | tf_op jit(solution)/shard_map/ppermute | solution.py:63
  41.4 4.7 %near_attention.1 = (f32[7,512,128]{2,1,0:T(8,128)S(1)}, f32[512,128]{1,0:T(8,128)S(1)}) custom-call(s32[1]{0:T(128)} %bitcast.refs_0_, s32[1]{0:T(128)} %bitcast.1.refs_1_, bf16[7,128,128]{2,1,0:T(8,128)(2,1)S(1)} %join_units.1.refs_8_.refs_2_, bf16[7,128,128]{2,1,0:T(8,128)(2,1)S(1)} %collective-permute-done.5.refs_0_.refs_3_, ...), custom_call_target="tpu_custom_call" | custom-call | flops 1 | bytes 1 | tf_op jit(solution)/shard_map/near_attention/pallas_call | solution.py:78
  46.1 1.8 %collective-permute-done.10.refs_9_ = bf16[2,256,512]{2,1,0:T(8,128)(2,1)S(1)} collective-permute-done((bf16[2,256,512]{2,1,0:T(8,128)(2,1)S(1)}, bf16[2,256,512]{2,1,0:T(8,128)(2,1)S(1)}, u32[]{:S(2)}, u32[]{:S(2)}) %collective-permute-start.10) | collective-permute-done | bytes 524320 | tf_op jit(solution)/shard_map/ppermute | solution.py:63
  48.0 2.7 %far_attention_0.1 = (bf16[8,64,128]{2,1,0:T(8,128)(2,1)S(1)}, bf16[8,64,128]{2,1,0:T(8,128)(2,1)S(1)}, bf16[8,64,128]{2,1,0:T(8,128)(2,1)S(1)}) custom-call(s32[1]{0:T(128)} %bitcast.refs_0_, s32[1]{0:T(128)} %bitcast.1.refs_1_, bf16[7,128,128]{2,1,0:T(8,128)(2,1)S(1)} %join_units.1.refs_8_.refs_2_, ...), custom_call_target="tpu_custom_call" | custom-call | flops 1 | bytes 1 | tf_op jit(solution)/shard_map/far_attention_0/pallas_call | solution.py:78
  50.6 0.9 %collective-permute-start.17 = (bf16[8,64,128]{2,1,0:T(8,128)(2,1)S(1)}, bf16[8,64,128]{2,1,0:T(8,128)(2,1)S(1)}, u32[]{:S(2)}, u32[]{:S(2)}) collective-permute-start(bf16[8,64,128]{2,1,0:T(8,128)(2,1)S(1)} %get-tuple-element.43), channel_id=1, source_target_pairs={{0,12},{2,98},{4,0},{6,102},{8,4},{10,106},{12,8},{14,110},{16,28}... | collective-permute-start | bytes 393224 | tf_op jit(solution)/shard_map/ppermute | solution.py:63
  52.2 1.3 %collective-permute-start.19 = (bf16[8,64,128]{2,1,0:T(8,128)(2,1)S(1)}, bf16[8,64,128]{2,1,0:T(8,128)(2,1)S(1)}, u32[]{:S(2)}, u32[]{:S(2)}) collective-permute-start(bf16[8,64,128]{2,1,0:T(8,128)(2,1)S(1)} %get-tuple-element.45), channel_id=1, source_target_pairs={{0,8},{2,66},{4,12},{6,70},{8,0},{10,74},{12,4},{14,78},{16,24},{1... | collective-permute-start | bytes 393224 | tf_op jit(solution)/shard_map/ppermute | solution.py:63
  53.5 4.1 %far_attention_1.1 = (bf16[8,128,128]{2,1,0:T(8,128)(2,1)S(1)}, bf16[8,64,128]{2,1,0:T(8,128)(2,1)S(1)}, bf16[8,64,128]{2,1,0:T(8,128)(2,1)S(1)}, bf16[8,64,128]{2,1,0:T(8,128)(2,1)S(1)}) custom-call(s32[1]{0:T(128)} %bitcast.refs_0_, s32[1]{0:T(128)} %bitcast.1.refs_1_, bf16[7,128,128]{2,1,0:T(8,128)(2,1)S(1)} %join_units.1.refs_8_.refs_2_, ...), custom_call_target="tpu_custom_call" | custom-call | flops 1 | bytes 1 | tf_op jit(solution)/shard_map/far_attention_1/pallas_call | solution.py:78
  58.5 4.5 %collective-permute-start.20 = (bf16[4,64,128]{2,1,0:T(8,128)(2,1)S(1)}, bf16[4,64,128]{2,1,0:T(8,128)(2,1)S(1)}, u32[]{:S(2)}, u32[]{:S(2)}) collective-permute-start(bf16[4,64,128]{2,1,0:T(8,128)(2,1)S(1)} %get-tuple-element.48), channel_id=1, source_target_pairs={{0,2},{2,0},{4,6},{6,4},{8,10},{10,8},{12,14},{14,12},{16,18},{18,... | collective-permute-start | bytes 196616 | tf_op jit(solution)/shard_map/ppermute | solution.py:63
  63.0 0.9 %collective-permute-done.20.refs_4_ = bf16[4,64,128]{2,1,0:T(8,128)(2,1)S(1)} collective-permute-done((bf16[4,64,128]{2,1,0:T(8,128)(2,1)S(1)}, bf16[4,64,128]{2,1,0:T(8,128)(2,1)S(1)}, u32[]{:S(2)}, u32[]{:S(2)}) %collective-permute-start.20) | collective-permute-done | bytes 65568 | tf_op jit(solution)/shard_map/ppermute | solution.py:63
  63.9 1.3 %output_projection.2 = bf16[64,3072]{1,0:T(8,128)(2,1)S(1)} custom-call(s32[1]{0:T(128)} %bitcast.refs_0_, s32[1]{0:T(128)} %bitcast.1.refs_1_, bf16[4,64,128]{2,1,0:T(8,128)(2,1)S(1)} %get-tuple-element.46.refs_2_, f32[64,128]{1,0:T(8,128)S(1)} %get-tuple-element.47.refs_3_, bf16[4,64,128]{2,1,0:T(8,128)(2,1)S(1)} %collective-permute-done.20.refs_4_, ...), custom_call_target="tpu_custom_call" | custom-call | flops 1 | bytes 1 | tf_op jit(solution)/shard_map/output_projection/pallas_call | solution.py:78
  65.3 3.3 %collective-permute-start.13 = (bf16[8,64,128]{2,1,0:T(8,128)(2,1)S(1)}, bf16[8,64,128]{2,1,0:T(8,128)(2,1)S(1)}, u32[]{:S(2)}, u32[]{:S(2)}) collective-permute-start(bf16[8,64,128]{2,1,0:T(8,128)(2,1)S(1)} %get-tuple-element.36), channel_id=1, source_target_pairs={{0,12},{2,98},{4,0},{6,102},{8,4},{10,106},{12,8},{14,110},{16,28}... | collective-permute-start | bytes 393224 | tf_op jit(solution)/shard_map/ppermute | solution.py:63
  68.6 1.5 %collective-permute-start.15 = (bf16[8,64,128]{2,1,0:T(8,128)(2,1)S(1)}, bf16[8,64,128]{2,1,0:T(8,128)(2,1)S(1)}, u32[]{:S(2)}, u32[]{:S(2)}) collective-permute-start(bf16[8,64,128]{2,1,0:T(8,128)(2,1)S(1)} %get-tuple-element.38), channel_id=1, source_target_pairs={{0,8},{2,66},{4,12},{6,70},{8,0},{10,74},{12,4},{14,78},{16,24},{1... | collective-permute-start | bytes 393224 | tf_op jit(solution)/shard_map/ppermute | solution.py:63
  70.5 4.5 %collective-permute-done.14.refs_2_ = bf16[8,64,128]{2,1,0:T(8,128)(2,1)S(1)} collective-permute-done((bf16[8,64,128]{2,1,0:T(8,128)(2,1)S(1)}, bf16[8,64,128]{2,1,0:T(8,128)(2,1)S(1)}, u32[]{:S(2)}, u32[]{:S(2)}) %collective-permute-start.14) | collective-permute-done | bytes 131104 | tf_op jit(solution)/shard_map/ppermute | solution.py:63
  75.9 1.0 %collective-permute-done.16.refs_4_ = bf16[4,64,128]{2,1,0:T(8,128)(2,1)S(1)} collective-permute-done((bf16[4,64,128]{2,1,0:T(8,128)(2,1)S(1)}, bf16[4,64,128]{2,1,0:T(8,128)(2,1)S(1)}, u32[]{:S(2)}, u32[]{:S(2)}) %collective-permute-start.16) | collective-permute-done | bytes 65568 | tf_op jit(solution)/shard_map/ppermute | solution.py:63
  76.8 2.1 %output_projection.3 = bf16[64,3072]{1,0:T(8,128)(2,1)} custom-call(s32[1]{0:T(128)} %bitcast.refs_0_, s32[1]{0:T(128)} %bitcast.1.refs_1_, bf16[4,64,128]{2,1,0:T(8,128)(2,1)S(1)} %get-tuple-element.39.refs_2_, f32[64,128]{1,0:T(8,128)S(1)} %get-tuple-element.40.refs_3_, bf16[4,64,128]{2,1,0:T(8,128)(2,1)S(1)} %collective-permute-done.16.refs_4_, ...), custom_call_target="tpu_custom_call" | custom-call | flops 1 | bytes 1 | tf_op jit(solution)/shard_map/output_projection/pallas_call | solution.py:78
  (41 shorter events, 4.9 us)
Async XLA Ops:
  1.7 4.3 %collective-permute-start = (bf16[2,128,512]{2,1,0:T(8,128)(2,1)S(1)}, bf16[2,128,512]{2,1,0:T(8,128)(2,1)S(1)}, u32[]{:S(2)}, u32[]{:S(2)}) collective-permute-start(bf16[2,128,512]{2,1,0:T(8,128)(2,1)S(1)} %get-tuple-element.53), channel_id=1, source_target_pairs={{0,2},{2,0},{4,6},{6,4},{8,10},{10,8},{12,14},{14,12},{16,18},{18,... | collective-permute-start | bytes 786440 | tf_op jit(solution)/shard_map/ppermute | solution.py:63
  3.2 15.3 %collective-permute-start.1 = (bf16[64,3072]{1,0:T(8,128)(2,1)}, bf16[64,3072]{1,0:T(8,128)(2,1)S(1)}, u32[]{:S(2)}, u32[]{:S(2)}) collective-permute-start(bf16[64,3072]{1,0:T(8,128)(2,1)} %refs_1_.1), channel_id=1, source_target_pairs={{0,1},{1,0},{2,3},{3,2},{4,5},{5,4},{6,7},{7,6},{8,9},{9,8},{10,11... | collective-permute-start | bytes 1179656 | tf_op jit(solution)/shard_map/ppermute | solution.py:67
  6.1 15.3 %collective-permute-start.3 = (bf16[2,256,512]{2,1,0:T(8,128)(2,1)S(1)}, bf16[2,256,512]{2,1,0:T(8,128)(2,1)S(1)}, u32[]{:S(2)}, u32[]{:S(2)}) collective-permute-start(bf16[2,256,512]{2,1,0:T(8,128)(2,1)S(1)} %pad_maximum_fusion.refs_2_.refs_6_), channel_id=1, source_target_pairs={{0,32},{2,6},{4,36},{6,10},{8,40},{10,14},{12,44},{14,2},{16,48},{... | collective-permute-start | bytes 1572872 | tf_op jit(solution)/shard_map/ppermute | solution.py:63
  7.8 13.9 %collective-permute-start.4 = (bf16[2,256,512]{2,1,0:T(8,128)(2,1)S(1)}, bf16[2,256,512]{2,1,0:T(8,128)(2,1)S(1)}, u32[]{:S(2)}, u32[]{:S(2)}) collective-permute-start(bf16[2,256,512]{2,1,0:T(8,128)(2,1)S(1)} %pad_maximum_fusion.refs_2_.refs_6_), channel_id=1, source_target_pairs={{0,96},{2,14},{4,100},{6,2},{8,104},{10,6},{12,108},{14,10},{16,11... | collective-permute-start | bytes 1572872 | tf_op jit(solution)/shard_map/ppermute | solution.py:63
  10.7 16.0 %collective-permute-start.8 = (bf16[2,256,512]{2,1,0:T(8,128)(2,1)S(1)}, bf16[2,256,512]{2,1,0:T(8,128)(2,1)S(1)}, u32[]{:S(2)}, u32[]{:S(2)}) collective-permute-start(bf16[2,256,512]{2,1,0:T(8,128)(2,1)S(1)} %pad_maximum_fusion.refs_2_.refs_6_), channel_id=1, source_target_pairs={{0,64},{2,10},{4,68},{6,14},{8,72},{10,2},{12,76},{14,6},{16,80},{... | collective-permute-start | bytes 1572872 | tf_op jit(solution)/shard_map/ppermute | solution.py:63
  12.1 25.7 %collective-permute-start.9 = (bf16[2,256,512]{2,1,0:T(8,128)(2,1)S(1)}, bf16[2,256,512]{2,1,0:T(8,128)(2,1)S(1)}, u32[]{:S(2)}, u32[]{:S(2)}) collective-permute-start(bf16[2,256,512]{2,1,0:T(8,128)(2,1)S(1)} %pad_maximum_fusion.refs_2_.refs_6_), channel_id=1, source_target_pairs={{0,16},{2,18},{4,20},{6,22},{8,24},{10,26},{12,28},{14,30},{16,0},... | collective-permute-start | bytes 1572872 | tf_op jit(solution)/shard_map/ppermute | solution.py:63
  19.8 1.6 %collective-permute-start.2 = (bf16[3,128,128]{2,1,0:T(8,128)(2,1)S(1)}, bf16[3,128,128]{2,1,0:T(8,128)(2,1)S(1)}, u32[]{:S(2)}, u32[]{:S(2)}) collective-permute-start(bf16[3,128,128]{2,1,0:T(8,128)(2,1)S(1)} %get-tuple-element.29), channel_id=1, source_target_pairs={{0,2},{2,0},{4,6},{6,4},{8,10},{10,8},{12,14},{14,12},{16,18},{18,... | collective-permute-start | bytes 294920 | tf_op jit(solution)/shard_map/ppermute | solution.py:63
  21.8 16.0 %collective-permute-start.5 = (bf16[7,128,128]{2,1,0:T(8,128)(2,1)S(1)}, bf16[7,128,128]{2,1,0:T(8,128)(2,1)S(1)}, u32[]{:S(2)}, u32[]{:S(2)}) collective-permute-start(bf16[7,128,128]{2,1,0:T(8,128)(2,1)S(1)} %join_units.1.refs_8_.refs_2_), channel_id=1, source_target_pairs={{0,4},{2,34},{4,8},{6,38},{8,12},{10,42},{12,0},{14,46},{16,20},{1... | collective-permute-start | bytes 688136 | tf_op jit(solution)/shard_map/ppermute | solution.py:63
  23.1 14.7 %collective-permute-start.6 = (bf16[7,128,128]{2,1,0:T(8,128)(2,1)S(1)}, bf16[7,128,128]{2,1,0:T(8,128)(2,1)S(1)}, u32[]{:S(2)}, u32[]{:S(2)}) collective-permute-start(bf16[7,128,128]{2,1,0:T(8,128)(2,1)S(1)} %join_units.1.refs_8_.refs_2_), channel_id=1, source_target_pairs={{0,12},{2,98},{4,0},{6,102},{8,4},{10,106},{12,8},{14,110},{16,28}... | collective-permute-start | bytes 688136 | tf_op jit(solution)/shard_map/ppermute | solution.py:63
  24.5 13.2 %collective-permute-start.7 = (bf16[7,128,128]{2,1,0:T(8,128)(2,1)S(1)}, bf16[7,128,128]{2,1,0:T(8,128)(2,1)S(1)}, u32[]{:S(2)}, u32[]{:S(2)}) collective-permute-start(bf16[7,128,128]{2,1,0:T(8,128)(2,1)S(1)} %join_units.1.refs_8_.refs_2_), channel_id=1, source_target_pairs={{0,8},{2,66},{4,12},{6,70},{8,0},{10,74},{12,4},{14,78},{16,24},{1... | collective-permute-start | bytes 688136 | tf_op jit(solution)/shard_map/ppermute | solution.py:63
  26.7 19.4 %collective-permute-start.12 = (bf16[2,256,512]{2,1,0:T(8,128)(2,1)S(1)}, bf16[2,256,512]{2,1,0:T(8,128)(2,1)S(1)}, u32[]{:S(2)}, u32[]{:S(2)}) collective-permute-start(bf16[2,256,512]{2,1,0:T(8,128)(2,1)S(1)} %collective-permute-done.8.refs_9_), channel_id=1, source_target_pairs={{0,16},{2,18},{4,20},{6,22},{8,24},{10,26},{12,28},{14,30},{16,0},... | collective-permute-start | bytes 1572872 | tf_op jit(solution)/shard_map/ppermute | solution.py:63
  37.8 10.2 %collective-permute-start.10 = (bf16[2,256,512]{2,1,0:T(8,128)(2,1)S(1)}, bf16[2,256,512]{2,1,0:T(8,128)(2,1)S(1)}, u32[]{:S(2)}, u32[]{:S(2)}) collective-permute-start(bf16[2,256,512]{2,1,0:T(8,128)(2,1)S(1)} %gate.1.refs_10_.refs_8_), channel_id=1, source_target_pairs={{0,32},{2,6},{4,36},{6,10},{8,40},{10,14},{12,44},{14,2},{16,48},{... | collective-permute-start | bytes 1572872 | tf_op jit(solution)/shard_map/ppermute | solution.py:63
  37.9 10.1 %collective-permute-start.11 = (bf16[2,256,512]{2,1,0:T(8,128)(2,1)S(1)}, bf16[2,256,512]{2,1,0:T(8,128)(2,1)S(1)}, u32[]{:S(2)}, u32[]{:S(2)}) collective-permute-start(bf16[2,256,512]{2,1,0:T(8,128)(2,1)S(1)} %gate.1.refs_10_.refs_8_), channel_id=1, source_target_pairs={{0,96},{2,14},{4,100},{6,2},{8,104},{10,6},{12,108},{14,10},{16,11... | collective-permute-start | bytes 1572872 | tf_op jit(solution)/shard_map/ppermute | solution.py:63
  41.4 22.5 %slice-start = ((s8[5505024]{0:T(1024)(128)(4,1)}), s8[4194304]{0:T(1024)(128)(4,1)S(1)}, s32[]{:S(2)}) async-start(s8[5505024]{0:T(1024)(128)(4,1)} %bitcast.9), calls=%async_computation | async-start | bytes 8388608
  48.0 15.9 %slice-start.1 = ((s8[5505024]{0:T(1024)(128)(4,1)}), s8[1310720]{0:T(1024)(128)(4,1)S(1)}, s32[]{:S(2)}) async-start(s8[5505024]{0:T(1024)(128)(4,1)} %bitcast.9), calls=%async_computation.1 | async-start | bytes 2621440
  50.6 6.9 %collective-permute-start.17 = (bf16[8,64,128]{2,1,0:T(8,128)(2,1)S(1)}, bf16[8,64,128]{2,1,0:T(8,128)(2,1)S(1)}, u32[]{:S(2)}, u32[]{:S(2)}) collective-permute-start(bf16[8,64,128]{2,1,0:T(8,128)(2,1)S(1)} %get-tuple-element.43), channel_id=1, source_target_pairs={{0,12},{2,98},{4,0},{6,102},{8,4},{10,106},{12,8},{14,110},{16,28}... | collective-permute-start | bytes 393224 | tf_op jit(solution)/shard_map/ppermute | solution.py:63
  51.5 6.4 %collective-permute-start.18 = (bf16[8,64,128]{2,1,0:T(8,128)(2,1)S(1)}, bf16[8,64,128]{2,1,0:T(8,128)(2,1)S(1)}, u32[]{:S(2)}, u32[]{:S(2)}) collective-permute-start(bf16[8,64,128]{2,1,0:T(8,128)(2,1)S(1)} %get-tuple-element.44), channel_id=1, source_target_pairs={{0,4},{2,34},{4,8},{6,38},{8,12},{10,42},{12,0},{14,46},{16,20},{1... | collective-permute-start | bytes 393224 | tf_op jit(solution)/shard_map/ppermute | solution.py:63
  52.2 5.8 %collective-permute-start.19 = (bf16[8,64,128]{2,1,0:T(8,128)(2,1)S(1)}, bf16[8,64,128]{2,1,0:T(8,128)(2,1)S(1)}, u32[]{:S(2)}, u32[]{:S(2)}) collective-permute-start(bf16[8,64,128]{2,1,0:T(8,128)(2,1)S(1)} %get-tuple-element.45), channel_id=1, source_target_pairs={{0,8},{2,66},{4,12},{6,70},{8,0},{10,74},{12,4},{14,78},{16,24},{1... | collective-permute-start | bytes 393224 | tf_op jit(solution)/shard_map/ppermute | solution.py:63
  58.5 5.4 %collective-permute-start.20 = (bf16[4,64,128]{2,1,0:T(8,128)(2,1)S(1)}, bf16[4,64,128]{2,1,0:T(8,128)(2,1)S(1)}, u32[]{:S(2)}, u32[]{:S(2)}) collective-permute-start(bf16[4,64,128]{2,1,0:T(8,128)(2,1)S(1)} %get-tuple-element.48), channel_id=1, source_target_pairs={{0,2},{2,0},{4,6},{6,4},{8,10},{10,8},{12,14},{14,12},{16,18},{18,... | collective-permute-start | bytes 196616 | tf_op jit(solution)/shard_map/ppermute | solution.py:63
  65.2 11.6 %collective-permute-start.21 = (bf16[64,3072]{1,0:T(8,128)(2,1)S(1)}, bf16[64,3072]{1,0:T(8,128)(2,1)S(1)}, u32[]{:S(2)}, u32[]{:S(2)}) collective-permute-start(bf16[64,3072]{1,0:T(8,128)(2,1)S(1)} %output_projection.2), channel_id=1, source_target_pairs={{0,1},{1,0},{2,3},{3,2},{4,5},{5,4},{6,7},{7,6},{8,9},{9,8},{10,11... | collective-permute-start | bytes 1179656 | tf_op jit(solution)/shard_map/ppermute | solution.py:67
  65.3 5.2 %collective-permute-start.13 = (bf16[8,64,128]{2,1,0:T(8,128)(2,1)S(1)}, bf16[8,64,128]{2,1,0:T(8,128)(2,1)S(1)}, u32[]{:S(2)}, u32[]{:S(2)}) collective-permute-start(bf16[8,64,128]{2,1,0:T(8,128)(2,1)S(1)} %get-tuple-element.36), channel_id=1, source_target_pairs={{0,12},{2,98},{4,0},{6,102},{8,4},{10,106},{12,8},{14,110},{16,28}... | collective-permute-start | bytes 393224 | tf_op jit(solution)/shard_map/ppermute | solution.py:63
  68.6 6.4 %collective-permute-start.14 = (bf16[8,64,128]{2,1,0:T(8,128)(2,1)S(1)}, bf16[8,64,128]{2,1,0:T(8,128)(2,1)S(1)}, u32[]{:S(2)}, u32[]{:S(2)}) collective-permute-start(bf16[8,64,128]{2,1,0:T(8,128)(2,1)S(1)} %get-tuple-element.37), channel_id=1, source_target_pairs={{0,4},{2,34},{4,8},{6,38},{8,12},{10,42},{12,0},{14,46},{16,20},{1... | collective-permute-start | bytes 393224 | tf_op jit(solution)/shard_map/ppermute | solution.py:63
  68.6 6.4 %collective-permute-start.15 = (bf16[8,64,128]{2,1,0:T(8,128)(2,1)S(1)}, bf16[8,64,128]{2,1,0:T(8,128)(2,1)S(1)}, u32[]{:S(2)}, u32[]{:S(2)}) collective-permute-start(bf16[8,64,128]{2,1,0:T(8,128)(2,1)S(1)} %get-tuple-element.38), channel_id=1, source_target_pairs={{0,8},{2,66},{4,12},{6,70},{8,0},{10,74},{12,4},{14,78},{16,24},{1... | collective-permute-start | bytes 393224 | tf_op jit(solution)/shard_map/ppermute | solution.py:63
  75.5 1.3 %collective-permute-start.16 = (bf16[4,64,128]{2,1,0:T(8,128)(2,1)S(1)}, bf16[4,64,128]{2,1,0:T(8,128)(2,1)S(1)}, u32[]{:S(2)}, u32[]{:S(2)}) collective-permute-start(bf16[4,64,128]{2,1,0:T(8,128)(2,1)S(1)} %get-tuple-element.41), channel_id=1, source_target_pairs={{0,2},{2,0},{4,6},{6,4},{8,10},{10,8},{12,14},{14,12},{16,18},{18,... | collective-permute-start | bytes 196616 | tf_op jit(solution)/shard_map/ppermute | solution.py:63

commit v4 on v3

--- a/solution.py
+++ b/solution.py
@@ -107,18 +107,27 @@
     return groups
 
 
-def _stage_kernel(w_ref, image_ref, out_ref, own_ref, sems, sem):
-    bring = pltpu.make_async_copy(image_ref, own_ref, sem)
-    bring.start()
-    for copy in _bring(w_ref, (0,), out_ref, sems)[0]:
+def _stage_kernel(w_ref, image_ref, g_ref, turn_ref, out_ref, own_ref, table_ref, gain_ref, sems, more):
+    copies = _bring(w_ref, (0,), out_ref, sems)[0]
+    small = [pltpu.make_async_copy(g_ref, gain_ref, more.at[0]), pltpu.make_async_copy(image_ref, own_ref, more.at[1])]
+    for copy in small:
+        copy.start()
+    small[0].wait()
+    even = _lane((8, HD)) % 2 == 0
+    for i in range(2):
+        gain = jnp.broadcast_to(gain_ref[i : i + 1, :], (8, HD))
+        swapped = jnp.where(even, pltpu.roll(gain, HD - 1, 1), pltpu.roll(gain, 1, 1))
+        table_ref[2 * i] = turn_ref[0] * gain[0:1]
+        table_ref[2 * i + 1] = turn_ref[1] * swapped[0:1]
+    for copy in copies:
         copy.wait()
-    bring.wait()
-
-
-def stage(w, image, after):
-    scratch = [pltpu.SemaphoreType.DMA((PIECES,)), pltpu.SemaphoreType.DMA(())]
-    outs = [((1, D, FEAT), BF16), (image.shape, BF16)]
-    return kernel_call(_stage_kernel, "stage", outs, scratch, [], [], outside=[w, image], after=after)
+    small[1].wait()
+
+
+def stage(w, image, gain, turns, after):
+    scratch = [((2, HD), F32), pltpu.SemaphoreType.DMA((PIECES,)), pltpu.SemaphoreType.DMA((2,))]
+    outs = [((1, D, FEAT), BF16), (image.shape, BF16), ((4, TOK, HD), F32)]
+    return kernel_call(_stage_kernel, "stage", outs, scratch, [], [], turns, outside=[w, image, gain], after=after)
 
 
 def _query_kernel(place, w_ref, oth_ref, own_ref, table_ref, qa_ref, qb_ref, q_ref, x_ref):
@@ -149,11 +158,10 @@
 
 
 def _home_kernel(
-    place, count, text_ref, w_ref, x_ref, table_ref, q_ref, out_ref, home_ref, stat_ref, text, s_ref, buffer, sem, sems
+    place, count, text_ref, w_ref, x_ref, table_ref, q_ref, out_ref, home_ref, stat_ref, text, s_ref, sem
 ):
     bring = pltpu.make_async_copy(text_ref, text, sem)
     bring.start()
-    groups = _bring(w_ref, (1, 2), buffer, sems)
     slots = text.shape[1]
     first = pl.ds(pl.multiple_of((1 - place[1]) * HALF, HALF), HALF)
     second = pl.ds(pl.multiple_of(place[1] * HALF, HALF), HALF)
@@ -162,18 +170,14 @@
         at = slice(head * HD, (head + 1) * HD)
         s = _scores(q_ref[head], text[0, :, at])
         s_ref[head, :, :slots] = jnp.where(_lane(s.shape) < count[0], s, -jnp.inf)
-    for copy in groups[0]:
-        copy.wait()
-    projected = jnp.dot(x_ref[...], buffer[0], preferred_element_type=F32)
+    projected = jnp.dot(x_ref[...], w_ref[1], preferred_element_type=F32)
     for head in range(HEADS):
         at = slice(head * HD, (head + 1) * HD)
         k = _turn(projected[:, at], table_ref, 1).astype(BF16)
         out_ref[0, first, at] = k[:HALF]
         out_ref[0, second, at] = k[HALF:]
         s_ref[head, :, slots:] = _scores(q_ref[head], k)
-    for copy in groups[1]:
-        copy.wait()
-    v = jnp.dot(x_ref[...], buffer[1], preferred_element_type=F32).astype(BF16)
+    v = jnp.dot(x_ref[...], w_ref[2], preferred_element_type=F32).astype(BF16)
     out_ref[1, first, :] = v[:HALF]
     out_ref[1, second, :] = v[HALF:]
     stat = jnp.zeros((TOK, HD), F32)
@@ -191,9 +195,7 @@
     scratch = [
         (text_kv.shape, BF16),
         ((HEADS, TOK, text_kv.shape[1] + TOK), F32),
-        ((2, D, FEAT), BF16),
         pltpu.SemaphoreType.DMA(()),
-        pltpu.SemaphoreType.DMA((2 * PIECES,)),
     ]
     return kernel_call(
         _home_kernel,
@@ -202,10 +204,11 @@
         scratch,
         place,
         [count],
+        w,
         *arrays,
-        outside=[text_kv, w],
+        outside=[text_kv],
         after=after,
-        limit=24,
+        limit=12,
     )
 
 
@@ -467,13 +470,10 @@
     cols = (within % COLS).astype(F32)[:, None]
     along_rows, along_cols, sign = _bands()
     angles = rows * along_rows + cols * along_cols
-    cosine = jnp.cos(angles)
-    sine = jnp.sin(angles) * sign
-    swapped = qk_gain.reshape(2, HD // 2, 2)[:, :, ::-1].reshape(2, HD)
-    table = jnp.stack([qk_gain[0] * cosine, swapped[0] * sine, qk_gain[1] * cosine, swapped[1] * sine])
+    turns = jnp.stack([jnp.cos(angles), jnp.sin(angles) * sign])
 
     w = jnp.transpose(w_qkv, (1, 0, 2))
-    staged, own_image = stage(w, image, [pair])
+    staged, own_image, table = stage(w, image, qk_gain, turns, [pair])
     q_mine, q_given, q_own, x = project_queries(place, staged, other_image, own_image, table)
     units = join_units(q_mine, move(q_given, _core_move), near[1:3])
     queries = [units] + [move(units, _query_move(d)) for d in (1, 3, 2)]

time: 79.2 us -> 75.3 us (0.951)
  Pallas kernels: 28.1 us -> 25 us
  local copies, waits for them, and re-layouts: 2.56 us -> 1.08 us
    pallas_call x11, Pallas kernels: 28.1 us -> 25 us  [kernel_call(): pl.pallas_call(run, in_specs=[SMEM] * len(scalars) + [ANY] * len(outside)...]
    slice x5 -> x0, local copies, waits for them, and re-layouts: 1.18 us -> none  [the longest x1 0.77 us: body(): qk_gain[0] * cosine]
    mul x1 -> x0, other arithmetic: 1.02 us -> none  [body(): swapped[0] * sine]
    cos x0 -> x1, other arithmetic: none -> 1.01 us  [body(): turns = jnp.stack([jnp.cos(angles), jnp.sin(angles) * sign])]
  transfers between devices with their start and end apart: 22 -> 22, of which waited for: 8 -> 8; matrix products, arithmetic and copies ran while one was open for 3% -> 1% of each run, Pallas kernels for 27% -> 25%
where the time goes in v4:
time: 75.3 us; the launch traced here: 74.9 us
  starting transfers between devices  34.5 us (46%)
  Pallas kernels  25 us (33%)
  waiting for transfers between devices  11 us (15%)
  between operations  2.17 us (3%)
  local copies, waits for them, and re-layouts  1.08 us (1%)
  other arithmetic  1.07 us (1%)
    ppermute x20, starting transfers between devices, move(): return lax.ppermute(array, 'patch', _perm(how))  33.1 us
    pallas_call x11, Pallas kernels, kernel_call(): pl.pallas_call(run, in_specs=[SMEM] * len(scalars) + [ANY] * len(outside)...  25 us
    ppermute x20, waiting for transfers between devices, move(): return lax.ppermute(array, 'patch', _perm(how))  11 us
  transfers between devices with their start and end apart: 22, of which 8 were waited for; matrix products, arithmetic and copies ran while one was open for 1% of the time, Pallas kernels for 25%

profile of v4, /device:TPU:1, one launch (start us, length us, event | category | flops | bytes accessed | tf_op | source)
XLA Modules:
  0.0 74.9 jit_solution(16871798040396086975)
XLA Ops:
  0.7 1.1 %constant_dynamic-slice_fusion.1 = (bf16[2,128,512]{2,1,0:T(8,128)(2,1)S(1)}, bf16[2,128,512]{2,1,0:T(8,128)(2,1)S(1)}) fusion(bf16[2,128,896]{2,1,0:T(8,128)(2,1)} %param.14, s32[]{:T(128)S(6)} %select_n.46, s32[]{:T(128)S(6)} %select_n.47), kind=kLoop, calls=%fused_computation.14 | loop fusion | bytes 1048584 | tf_op jit(solution)/shard_map/dynamic_slice | solution.py:462
  1.7 1.5 %collective-permute-start = (bf16[2,128,512]{2,1,0:T(8,128)(2,1)S(1)}, bf16[2,128,512]{2,1,0:T(8,128)(2,1)S(1)}, u32[]{:S(2)}, u32[]{:S(2)}) collective-permute-start(bf16[2,128,512]{2,1,0:T(8,128)(2,1)S(1)} %get-tuple-element.53), channel_id=1, source_target_pairs={{0,2},{2,0},{4,6},{6,4},{8,10},{10,8},{12,14},{14,12},{16,18},{18,... | collective-permute-start | bytes 786440 | tf_op jit(solution)/shard_map/ppermute | solution.py:63
  3.2 1.4 %collective-permute-start.1 = (bf16[64,3072]{1,0:T(8,128)(2,1)}, bf16[64,3072]{1,0:T(8,128)(2,1)S(1)}, u32[]{:S(2)}, u32[]{:S(2)}) collective-permute-start(bf16[64,3072]{1,0:T(8,128)(2,1)} %refs_1_.1), channel_id=1, source_target_pairs={{0,1},{1,0},{2,3},{3,2},{4,5},{5,4},{6,7},{7,6},{8,9},{9,8},{10,11... | collective-permute-start | bytes 1179656 | tf_op jit(solution)/shard_map/ppermute | solution.py:67
  5.3 1.7 %collective-permute-start.3 = (bf16[2,256,512]{2,1,0:T(8,128)(2,1)S(1)}, bf16[2,256,512]{2,1,0:T(8,128)(2,1)S(1)}, u32[]{:S(2)}, u32[]{:S(2)}) collective-permute-start(bf16[2,256,512]{2,1,0:T(8,128)(2,1)S(1)} %pad_maximum_fusion.refs_4_.refs_6_), channel_id=1, source_target_pairs={{0,32},{2,6},{4,36},{6,10},{8,40},{10,14},{12,44},{14,2},{16,48},{... | collective-permute-start | bytes 1572872 | tf_op jit(solution)/shard_map/ppermute | solution.py:63
  7.0 2.2 %collective-permute-start.4 = (bf16[2,256,512]{2,1,0:T(8,128)(2,1)S(1)}, bf16[2,256,512]{2,1,0:T(8,128)(2,1)S(1)}, u32[]{:S(2)}, u32[]{:S(2)}) collective-permute-start(bf16[2,256,512]{2,1,0:T(8,128)(2,1)S(1)} %pad_maximum_fusion.refs_4_.refs_6_), channel_id=1, source_target_pairs={{0,96},{2,14},{4,100},{6,2},{8,104},{10,6},{12,108},{14,10},{16,11... | collective-permute-start | bytes 1572872 | tf_op jit(solution)/shard_map/ppermute | solution.py:63
  9.3 1.3 %collective-permute-start.8 = (bf16[2,256,512]{2,1,0:T(8,128)(2,1)S(1)}, bf16[2,256,512]{2,1,0:T(8,128)(2,1)S(1)}, u32[]{:S(2)}, u32[]{:S(2)}) collective-permute-start(bf16[2,256,512]{2,1,0:T(8,128)(2,1)S(1)} %pad_maximum_fusion.refs_4_.refs_6_), channel_id=1, source_target_pairs={{0,64},{2,10},{4,68},{6,14},{8,72},{10,2},{12,76},{14,6},{16,80},{... | collective-permute-start | bytes 1572872 | tf_op jit(solution)/shard_map/ppermute | solution.py:63
  10.6 2.6 %collective-permute-start.9 = (bf16[2,256,512]{2,1,0:T(8,128)(2,1)S(1)}, bf16[2,256,512]{2,1,0:T(8,128)(2,1)S(1)}, u32[]{:S(2)}, u32[]{:S(2)}) collective-permute-start(bf16[2,256,512]{2,1,0:T(8,128)(2,1)S(1)} %pad_maximum_fusion.refs_4_.refs_6_), channel_id=1, source_target_pairs={{0,16},{2,18},{4,20},{6,22},{8,24},{10,26},{12,28},{14,30},{16,0},... | collective-permute-start | bytes 1572872 | tf_op jit(solution)/shard_map/ppermute | solution.py:63
  13.2 1.0 %fusion = (f32[1,128,128]{2,1,0:T(8,128)S(1)}, f32[1,128,128]{2,1,0:T(8,128)S(1)}) fusion(f32[128]{0:T(128)} %constant.65.clone, f32[128]{0:T(128)S(1)} %get-tuple-element.56, f32[128]{0:T(128)} %constant.64.clone, f32[128]{0:T(128)S(1)} %get-tuple-element.57, f32[128]{0:T(128)} %constant.66.clone), kind=kLoop, calls=%fused_computation.4 | loop fusion | flops 65536 | bytes 133632 | tf_op jit(solution)/shard_map/cos | solution.py:473
  14.2 2.9 %stage.1 = (bf16[1,3072,896]{2,1,0:T(8,128)(2,1)S(1)}, bf16[64,3072]{1,0:T(8,128)(2,1)S(1)}, f32[4,128,128]{2,1,0:T(8,128)S(1)}) custom-call(bf16[3,3072,896]{2,1,0:T(8,128)(2,1)} %bitcast.5, bf16[64,3072]{1,0:T(8,128)(2,1)} %refs_1_.1, f32[2,128]{1,0:T(2,128)} %refs_2_.2, f32[2,128,128]{2,1,0:T(8,128)S(1)} %pad_maximum_fusion.1.refs_3_, ...), custom_call_target="tpu_custom_call" | custom-call | flops 1 | bytes 1 | tf_op jit(solution)/shard_map/stage/pallas_call | solution.py:78
  17.1 1.3 %query_projection.1 = (bf16[4,128,128]{2,1,0:T(8,128)(2,1)S(1)}, bf16[3,128,128]{2,1,0:T(8,128)(2,1)S(1)}, bf16[7,128,128]{2,1,0:T(8,128)(2,1)S(1)}, bf16[128,3072]{1,0:T(8,128)(2,1)S(1)}) custom-call(s32[1]{0:T(128)} %bitcast.refs_0_, s32[1]{0:T(128)} %bitcast.1.refs_1_, bf16[1,3072,896]{2,1,0:T(8,128)(2,1)S(1)} %get-tuple-element.27.refs_2_, ...), custom_call_target="tpu_custom_call" | custom-call | flops 1 | bytes 1 | tf_op jit(solution)/shard_map/query_projection/pallas_call | solution.py:78
  19.1 0.9 %collective-permute-done.2.refs_1_ = bf16[3,128,128]{2,1,0:T(8,128)(2,1)S(1)} collective-permute-done((bf16[3,128,128]{2,1,0:T(8,128)(2,1)S(1)}, bf16[3,128,128]{2,1,0:T(8,128)(2,1)S(1)}, u32[]{:S(2)}, u32[]{:S(2)}) %collective-permute-start.2) | collective-permute-done | bytes 98336 | tf_op jit(solution)/shard_map/ppermute | solution.py:63
  20.1 0.9 %collective-permute-done.4.refs_3_.refs_8_ = bf16[2,256,512]{2,1,0:T(8,128)(2,1)S(1)} collective-permute-done((bf16[2,256,512]{2,1,0:T(8,128)(2,1)S(1)}, bf16[2,256,512]{2,1,0:T(8,128)(2,1)S(1)}, u32[]{:S(2)}, u32[]{:S(2)}) %collective-permute-start.4) | collective-permute-done | bytes 524320 | tf_op jit(solution)/shard_map/ppermute | solution.py:63
  21.0 1.3 %collective-permute-start.5 = (bf16[7,128,128]{2,1,0:T(8,128)(2,1)S(1)}, bf16[7,128,128]{2,1,0:T(8,128)(2,1)S(1)}, u32[]{:S(2)}, u32[]{:S(2)}) collective-permute-start(bf16[7,128,128]{2,1,0:T(8,128)(2,1)S(1)} %join_units.1.refs_8_.refs_2_), channel_id=1, source_target_pairs={{0,4},{2,34},{4,8},{6,38},{8,12},{10,42},{12,0},{14,46},{16,20},{1... | collective-permute-start | bytes 688136 | tf_op jit(solution)/shard_map/ppermute | solution.py:63
  22.3 1.5 %collective-permute-start.6 = (bf16[7,128,128]{2,1,0:T(8,128)(2,1)S(1)}, bf16[7,128,128]{2,1,0:T(8,128)(2,1)S(1)}, u32[]{:S(2)}, u32[]{:S(2)}) collective-permute-start(bf16[7,128,128]{2,1,0:T(8,128)(2,1)S(1)} %join_units.1.refs_8_.refs_2_), channel_id=1, source_target_pairs={{0,12},{2,98},{4,0},{6,102},{8,4},{10,106},{12,8},{14,110},{16,28}... | collective-permute-start | bytes 688136 | tf_op jit(solution)/shard_map/ppermute | solution.py:63
  23.7 1.5 %collective-permute-start.7 = (bf16[7,128,128]{2,1,0:T(8,128)(2,1)S(1)}, bf16[7,128,128]{2,1,0:T(8,128)(2,1)S(1)}, u32[]{:S(2)}, u32[]{:S(2)}) collective-permute-start(bf16[7,128,128]{2,1,0:T(8,128)(2,1)S(1)} %join_units.1.refs_8_.refs_2_), channel_id=1, source_target_pairs={{0,8},{2,66},{4,12},{6,70},{8,0},{10,74},{12,4},{14,78},{16,24},{1... | collective-permute-start | bytes 688136 | tf_op jit(solution)/shard_map/ppermute | solution.py:63
  25.9 2.7 %collective-permute-start.12 = (bf16[2,256,512]{2,1,0:T(8,128)(2,1)S(1)}, bf16[2,256,512]{2,1,0:T(8,128)(2,1)S(1)}, u32[]{:S(2)}, u32[]{:S(2)}) collective-permute-start(bf16[2,256,512]{2,1,0:T(8,128)(2,1)S(1)} %collective-permute-done.8.refs_9_), channel_id=1, source_target_pairs={{0,16},{2,18},{4,20},{6,22},{8,24},{10,26},{12,28},{14,30},{16,0},... | collective-permute-start | bytes 1572872 | tf_op jit(solution)/shard_map/ppermute | solution.py:63
  28.6 5.1 %home_attention.1 = (bf16[2,128,896]{2,1,0:T(8,128)(2,1)}, bf16[7,128,128]{2,1,0:T(8,128)(2,1)S(1)}, f32[128,128]{1,0:T(8,128)S(1)}) custom-call(s32[1]{0:T(128)} %bitcast.refs_0_, s32[1]{0:T(128)} %bitcast.1.refs_1_, s32[1]{0:T(128)S(6)} %copy.15.refs_2_, bf16[2,512,896]{2,1,0:T(8,128)(2,1)} %refs_3_.1, bf16[3,3072,896]{2,1,0:T(8,128)(2,1)S(1)} %bitcast.6, ...), custom_call_target="tpu_custom_call" | custom-call | flops 1 | bytes 1 | tf_op jit(solution)/shard_map/home_attention/pallas_call | solution.py:78
  33.9 3.5 %collective-permute-start.11 = (bf16[2,256,512]{2,1,0:T(8,128)(2,1)S(1)}, bf16[2,256,512]{2,1,0:T(8,128)(2,1)S(1)}, u32[]{:S(2)}, u32[]{:S(2)}) collective-permute-start(bf16[2,256,512]{2,1,0:T(8,128)(2,1)S(1)} %gate.1.refs_10_.refs_8_), channel_id=1, source_target_pairs={{0,96},{2,14},{4,100},{6,2},{8,104},{10,6},{12,108},{14,10},{16,11... | collective-permute-start | bytes 1572872 | tf_op jit(solution)/shard_map/ppermute | solution.py:63
  37.4 4.7 %near_attention.1 = (f32[7,512,128]{2,1,0:T(8,128)S(1)}, f32[512,128]{1,0:T(8,128)S(1)}) custom-call(s32[1]{0:T(128)} %bitcast.refs_0_, s32[1]{0:T(128)} %bitcast.1.refs_1_, bf16[7,128,128]{2,1,0:T(8,128)(2,1)S(1)} %join_units.1.refs_8_.refs_2_, bf16[7,128,128]{2,1,0:T(8,128)(2,1)S(1)} %collective-permute-done.5.refs_0_.refs_3_, ...), custom_call_target="tpu_custom_call" | custom-call | flops 1 | bytes 1 | tf_op jit(solution)/shard_map/near_attention/pallas_call | solution.py:78
  42.1 1.9 %collective-permute-done.10.refs_9_ = bf16[2,256,512]{2,1,0:T(8,128)(2,1)S(1)} collective-permute-done((bf16[2,256,512]{2,1,0:T(8,128)(2,1)S(1)}, bf16[2,256,512]{2,1,0:T(8,128)(2,1)S(1)}, u32[]{:S(2)}, u32[]{:S(2)}) %collective-permute-start.10) | collective-permute-done | bytes 524320 | tf_op jit(solution)/shard_map/ppermute | solution.py:63
  44.0 2.7 %far_attention_0.1 = (bf16[8,64,128]{2,1,0:T(8,128)(2,1)S(1)}, bf16[8,64,128]{2,1,0:T(8,128)(2,1)S(1)}, bf16[8,64,128]{2,1,0:T(8,128)(2,1)S(1)}) custom-call(s32[1]{0:T(128)} %bitcast.refs_0_, s32[1]{0:T(128)} %bitcast.1.refs_1_, bf16[7,128,128]{2,1,0:T(8,128)(2,1)S(1)} %join_units.1.refs_8_.refs_2_, ...), custom_call_target="tpu_custom_call" | custom-call | flops 1 | bytes 1 | tf_op jit(solution)/shard_map/far_attention_0/pallas_call | solution.py:78
  46.7 0.9 %collective-permute-start.17 = (bf16[8,64,128]{2,1,0:T(8,128)(2,1)S(1)}, bf16[8,64,128]{2,1,0:T(8,128)(2,1)S(1)}, u32[]{:S(2)}, u32[]{:S(2)}) collective-permute-start(bf16[8,64,128]{2,1,0:T(8,128)(2,1)S(1)} %get-tuple-element.45), channel_id=1, source_target_pairs={{0,12},{2,98},{4,0},{6,102},{8,4},{10,106},{12,8},{14,110},{16,28}... | collective-permute-start | bytes 393224 | tf_op jit(solution)/shard_map/ppermute | solution.py:63
  48.2 1.3 %collective-permute-start.19 = (bf16[8,64,128]{2,1,0:T(8,128)(2,1)S(1)}, bf16[8,64,128]{2,1,0:T(8,128)(2,1)S(1)}, u32[]{:S(2)}, u32[]{:S(2)}) collective-permute-start(bf16[8,64,128]{2,1,0:T(8,128)(2,1)S(1)} %get-tuple-element.47), channel_id=1, source_target_pairs={{0,8},{2,66},{4,12},{6,70},{8,0},{10,74},{12,4},{14,78},{16,24},{1... | collective-permute-start | bytes 393224 | tf_op jit(solution)/shard_map/ppermute | solution.py:63
  49.5 4.1 %far_attention_1.1 = (bf16[8,128,128]{2,1,0:T(8,128)(2,1)S(1)}, bf16[8,64,128]{2,1,0:T(8,128)(2,1)S(1)}, bf16[8,64,128]{2,1,0:T(8,128)(2,1)S(1)}, bf16[8,64,128]{2,1,0:T(8,128)(2,1)S(1)}) custom-call(s32[1]{0:T(128)} %bitcast.refs_0_, s32[1]{0:T(128)} %bitcast.1.refs_1_, bf16[7,128,128]{2,1,0:T(8,128)(2,1)S(1)} %join_units.1.refs_8_.refs_2_, ...), custom_call_target="tpu_custom_call" | custom-call | flops 1 | bytes 1 | tf_op jit(solution)/shard_map/far_attention_1/pallas_call | solution.py:78
  54.5 4.5 %collective-permute-start.20 = (bf16[4,64,128]{2,1,0:T(8,128)(2,1)S(1)}, bf16[4,64,128]{2,1,0:T(8,128)(2,1)S(1)}, u32[]{:S(2)}, u32[]{:S(2)}) collective-permute-start(bf16[4,64,128]{2,1,0:T(8,128)(2,1)S(1)} %get-tuple-element.50), channel_id=1, source_target_pairs={{0,2},{2,0},{4,6},{6,4},{8,10},{10,8},{12,14},{14,12},{16,18},{18,... | collective-permute-start | bytes 196616 | tf_op jit(solution)/shard_map/ppermute | solution.py:63
  59.0 0.9 %collective-permute-done.20.refs_4_ = bf16[4,64,128]{2,1,0:T(8,128)(2,1)S(1)} collective-permute-done((bf16[4,64,128]{2,1,0:T(8,128)(2,1)S(1)}, bf16[4,64,128]{2,1,0:T(8,128)(2,1)S(1)}, u32[]{:S(2)}, u32[]{:S(2)}) %collective-permute-start.20) | collective-permute-done | bytes 65568 | tf_op jit(solution)/shard_map/ppermute | solution.py:63
  59.9 1.3 %output_projection.2 = bf16[64,3072]{1,0:T(8,128)(2,1)S(1)} custom-call(s32[1]{0:T(128)} %bitcast.refs_0_, s32[1]{0:T(128)} %bitcast.1.refs_1_, bf16[4,64,128]{2,1,0:T(8,128)(2,1)S(1)} %get-tuple-element.48.refs_2_, f32[64,128]{1,0:T(8,128)S(1)} %get-tuple-element.49.refs_3_, bf16[4,64,128]{2,1,0:T(8,128)(2,1)S(1)} %collective-permute-done.20.refs_4_, ...), custom_call_target="tpu_custom_call" | custom-call | flops 1 | bytes 1 | tf_op jit(solution)/shard_map/output_projection/pallas_call | solution.py:78
  61.3 3.3 %collective-permute-start.13 = (bf16[8,64,128]{2,1,0:T(8,128)(2,1)S(1)}, bf16[8,64,128]{2,1,0:T(8,128)(2,1)S(1)}, u32[]{:S(2)}, u32[]{:S(2)}) collective-permute-start(bf16[8,64,128]{2,1,0:T(8,128)(2,1)S(1)} %get-tuple-element.38), channel_id=1, source_target_pairs={{0,12},{2,98},{4,0},{6,102},{8,4},{10,106},{12,8},{14,110},{16,28}... | collective-permute-start | bytes 393224 | tf_op jit(solution)/shard_map/ppermute | solution.py:63
  64.6 1.5 %collective-permute-start.15 = (bf16[8,64,128]{2,1,0:T(8,128)(2,1)S(1)}, bf16[8,64,128]{2,1,0:T(8,128)(2,1)S(1)}, u32[]{:S(2)}, u32[]{:S(2)}) collective-permute-start(bf16[8,64,128]{2,1,0:T(8,128)(2,1)S(1)} %get-tuple-element.40), channel_id=1, source_target_pairs={{0,8},{2,66},{4,12},{6,70},{8,0},{10,74},{12,4},{14,78},{16,24},{1... | collective-permute-start | bytes 393224 | tf_op jit(solution)/shard_map/ppermute | solution.py:63
  66.6 4.5 %collective-permute-done.14.refs_2_ = bf16[8,64,128]{2,1,0:T(8,128)(2,1)S(1)} collective-permute-done((bf16[8,64,128]{2,1,0:T(8,128)(2,1)S(1)}, bf16[8,64,128]{2,1,0:T(8,128)(2,1)S(1)}, u32[]{:S(2)}, u32[]{:S(2)}) %collective-permute-start.14) | collective-permute-done | bytes 131104 | tf_op jit(solution)/shard_map/ppermute | solution.py:63
  71.9 0.9 %collective-permute-done.16.refs_4_ = bf16[4,64,128]{2,1,0:T(8,128)(2,1)S(1)} collective-permute-done((bf16[4,64,128]{2,1,0:T(8,128)(2,1)S(1)}, bf16[4,64,128]{2,1,0:T(8,128)(2,1)S(1)}, u32[]{:S(2)}, u32[]{:S(2)}) %collective-permute-start.16) | collective-permute-done | bytes 65568 | tf_op jit(solution)/shard_map/ppermute | solution.py:63
  72.9 2.1 %output_projection.3 = bf16[64,3072]{1,0:T(8,128)(2,1)} custom-call(s32[1]{0:T(128)} %bitcast.refs_0_, s32[1]{0:T(128)} %bitcast.1.refs_1_, bf16[4,64,128]{2,1,0:T(8,128)(2,1)S(1)} %get-tuple-element.41.refs_2_, f32[64,128]{1,0:T(8,128)S(1)} %get-tuple-element.42.refs_3_, bf16[4,64,128]{2,1,0:T(8,128)(2,1)S(1)} %collective-permute-done.16.refs_4_, ...), custom_call_target="tpu_custom_call" | custom-call | flops 1 | bytes 1 | tf_op jit(solution)/shard_map/output_projection/pallas_call | solution.py:78
  (36 shorter events, 3.9 us)
Async XLA Ops:
  1.7 3.6 %collective-permute-start = (bf16[2,128,512]{2,1,0:T(8,128)(2,1)S(1)}, bf16[2,128,512]{2,1,0:T(8,128)(2,1)S(1)}, u32[]{:S(2)}, u32[]{:S(2)}) collective-permute-start(bf16[2,128,512]{2,1,0:T(8,128)(2,1)S(1)} %get-tuple-element.53), channel_id=1, source_target_pairs={{0,2},{2,0},{4,6},{6,4},{8,10},{10,8},{12,14},{14,12},{16,18},{18,... | collective-permute-start | bytes 786440 | tf_op jit(solution)/shard_map/ppermute | solution.py:63
  3.2 13.9 %collective-permute-start.1 = (bf16[64,3072]{1,0:T(8,128)(2,1)}, bf16[64,3072]{1,0:T(8,128)(2,1)S(1)}, u32[]{:S(2)}, u32[]{:S(2)}) collective-permute-start(bf16[64,3072]{1,0:T(8,128)(2,1)} %refs_1_.1), channel_id=1, source_target_pairs={{0,1},{1,0},{2,3},{3,2},{4,5},{5,4},{6,7},{7,6},{8,9},{9,8},{10,11... | collective-permute-start | bytes 1179656 | tf_op jit(solution)/shard_map/ppermute | solution.py:67
  5.3 14.7 %collective-permute-start.3 = (bf16[2,256,512]{2,1,0:T(8,128)(2,1)S(1)}, bf16[2,256,512]{2,1,0:T(8,128)(2,1)S(1)}, u32[]{:S(2)}, u32[]{:S(2)}) collective-permute-start(bf16[2,256,512]{2,1,0:T(8,128)(2,1)S(1)} %pad_maximum_fusion.refs_4_.refs_6_), channel_id=1, source_target_pairs={{0,32},{2,6},{4,36},{6,10},{8,40},{10,14},{12,44},{14,2},{16,48},{... | collective-permute-start | bytes 1572872 | tf_op jit(solution)/shard_map/ppermute | solution.py:63
  7.0 13.9 %collective-permute-start.4 = (bf16[2,256,512]{2,1,0:T(8,128)(2,1)S(1)}, bf16[2,256,512]{2,1,0:T(8,128)(2,1)S(1)}, u32[]{:S(2)}, u32[]{:S(2)}) collective-permute-start(bf16[2,256,512]{2,1,0:T(8,128)(2,1)S(1)} %pad_maximum_fusion.refs_4_.refs_6_), channel_id=1, source_target_pairs={{0,96},{2,14},{4,100},{6,2},{8,104},{10,6},{12,108},{14,10},{16,11... | collective-permute-start | bytes 1572872 | tf_op jit(solution)/shard_map/ppermute | solution.py:63
  9.3 16.7 %collective-permute-start.8 = (bf16[2,256,512]{2,1,0:T(8,128)(2,1)S(1)}, bf16[2,256,512]{2,1,0:T(8,128)(2,1)S(1)}, u32[]{:S(2)}, u32[]{:S(2)}) collective-permute-start(bf16[2,256,512]{2,1,0:T(8,128)(2,1)S(1)} %pad_maximum_fusion.refs_4_.refs_6_), channel_id=1, source_target_pairs={{0,64},{2,10},{4,68},{6,14},{8,72},{10,2},{12,76},{14,6},{16,80},{... | collective-permute-start | bytes 1572872 | tf_op jit(solution)/shard_map/ppermute | solution.py:63
  10.6 23.2 %collective-permute-start.9 = (bf16[2,256,512]{2,1,0:T(8,128)(2,1)S(1)}, bf16[2,256,512]{2,1,0:T(8,128)(2,1)S(1)}, u32[]{:S(2)}, u32[]{:S(2)}) collective-permute-start(bf16[2,256,512]{2,1,0:T(8,128)(2,1)S(1)} %pad_maximum_fusion.refs_4_.refs_6_), channel_id=1, source_target_pairs={{0,16},{2,18},{4,20},{6,22},{8,24},{10,26},{12,28},{14,30},{16,0},... | collective-permute-start | bytes 1572872 | tf_op jit(solution)/shard_map/ppermute | solution.py:63
  14.2 14.4 %copy-start = (bf16[3072,3,896]{2,0,1:T(8,128)(2,1)S(1)}, bf16[3072,3,896]{2,0,1:T(8,128)(2,1)}, u32[]{:S(2)}) copy-start(bf16[3072,3,896]{2,0,1:T(8,128)(2,1)} %param.12) | copy-start | bytes 49545220
  18.4 1.6 %collective-permute-start.2 = (bf16[3,128,128]{2,1,0:T(8,128)(2,1)S(1)}, bf16[3,128,128]{2,1,0:T(8,128)(2,1)S(1)}, u32[]{:S(2)}, u32[]{:S(2)}) collective-permute-start(bf16[3,128,128]{2,1,0:T(8,128)(2,1)S(1)} %get-tuple-element.31), channel_id=1, source_target_pairs={{0,2},{2,0},{4,6},{6,4},{8,10},{10,8},{12,14},{14,12},{16,18},{18,... | collective-permute-start | bytes 294920 | tf_op jit(solution)/shard_map/ppermute | solution.py:63
  21.0 12.8 %collective-permute-start.5 = (bf16[7,128,128]{2,1,0:T(8,128)(2,1)S(1)}, bf16[7,128,128]{2,1,0:T(8,128)(2,1)S(1)}, u32[]{:S(2)}, u32[]{:S(2)}) collective-permute-start(bf16[7,128,128]{2,1,0:T(8,128)(2,1)S(1)} %join_units.1.refs_8_.refs_2_), channel_id=1, source_target_pairs={{0,4},{2,34},{4,8},{6,38},{8,12},{10,42},{12,0},{14,46},{16,20},{1... | collective-permute-start | bytes 688136 | tf_op jit(solution)/shard_map/ppermute | solution.py:63
  22.3 11.5 %collective-permute-start.6 = (bf16[7,128,128]{2,1,0:T(8,128)(2,1)S(1)}, bf16[7,128,128]{2,1,0:T(8,128)(2,1)S(1)}, u32[]{:S(2)}, u32[]{:S(2)}) collective-permute-start(bf16[7,128,128]{2,1,0:T(8,128)(2,1)S(1)} %join_units.1.refs_8_.refs_2_), channel_id=1, source_target_pairs={{0,12},{2,98},{4,0},{6,102},{8,4},{10,106},{12,8},{14,110},{16,28}... | collective-permute-start | bytes 688136 | tf_op jit(solution)/shard_map/ppermute | solution.py:63
  23.7 10.0 %collective-permute-start.7 = (bf16[7,128,128]{2,1,0:T(8,128)(2,1)S(1)}, bf16[7,128,128]{2,1,0:T(8,128)(2,1)S(1)}, u32[]{:S(2)}, u32[]{:S(2)}) collective-permute-start(bf16[7,128,128]{2,1,0:T(8,128)(2,1)S(1)} %join_units.1.refs_8_.refs_2_), channel_id=1, source_target_pairs={{0,8},{2,66},{4,12},{6,70},{8,0},{10,74},{12,4},{14,78},{16,24},{1... | collective-permute-start | bytes 688136 | tf_op jit(solution)/shard_map/ppermute | solution.py:63
  25.9 16.2 %collective-permute-start.12 = (bf16[2,256,512]{2,1,0:T(8,128)(2,1)S(1)}, bf16[2,256,512]{2,1,0:T(8,128)(2,1)S(1)}, u32[]{:S(2)}, u32[]{:S(2)}) collective-permute-start(bf16[2,256,512]{2,1,0:T(8,128)(2,1)S(1)} %collective-permute-done.8.refs_9_), channel_id=1, source_target_pairs={{0,16},{2,18},{4,20},{6,22},{8,24},{10,26},{12,28},{14,30},{16,0},... | collective-permute-start | bytes 1572872 | tf_op jit(solution)/shard_map/ppermute | solution.py:63
  33.8 10.2 %collective-permute-start.10 = (bf16[2,256,512]{2,1,0:T(8,128)(2,1)S(1)}, bf16[2,256,512]{2,1,0:T(8,128)(2,1)S(1)}, u32[]{:S(2)}, u32[]{:S(2)}) collective-permute-start(bf16[2,256,512]{2,1,0:T(8,128)(2,1)S(1)} %gate.1.refs_10_.refs_8_), channel_id=1, source_target_pairs={{0,32},{2,6},{4,36},{6,10},{8,40},{10,14},{12,44},{14,2},{16,48},{... | collective-permute-start | bytes 1572872 | tf_op jit(solution)/shard_map/ppermute | solution.py:63
  33.9 10.1 %collective-permute-start.11 = (bf16[2,256,512]{2,1,0:T(8,128)(2,1)S(1)}, bf16[2,256,512]{2,1,0:T(8,128)(2,1)S(1)}, u32[]{:S(2)}, u32[]{:S(2)}) collective-permute-start(bf16[2,256,512]{2,1,0:T(8,128)(2,1)S(1)} %gate.1.refs_10_.refs_8_), channel_id=1, source_target_pairs={{0,96},{2,14},{4,100},{6,2},{8,104},{10,6},{12,108},{14,10},{16,11... | collective-permute-start | bytes 1572872 | tf_op jit(solution)/shard_map/ppermute | solution.py:63
  37.4 22.5 %slice-start = ((s8[5505024]{0:T(1024)(128)(4,1)}), s8[4194304]{0:T(1024)(128)(4,1)S(1)}, s32[]{:S(2)}) async-start(s8[5505024]{0:T(1024)(128)(4,1)} %bitcast.7), calls=%async_computation | async-start | bytes 8388608
  44.0 15.9 %slice-start.1 = ((s8[5505024]{0:T(1024)(128)(4,1)}), s8[1310720]{0:T(1024)(128)(4,1)S(1)}, s32[]{:S(2)}) async-start(s8[5505024]{0:T(1024)(128)(4,1)} %bitcast.7), calls=%async_computation.1 | async-start | bytes 2621440
  46.7 6.9 %collective-permute-start.17 = (bf16[8,64,128]{2,1,0:T(8,128)(2,1)S(1)}, bf16[8,64,128]{2,1,0:T(8,128)(2,1)S(1)}, u32[]{:S(2)}, u32[]{:S(2)}) collective-permute-start(bf16[8,64,128]{2,1,0:T(8,128)(2,1)S(1)} %get-tuple-element.45), channel_id=1, source_target_pairs={{0,12},{2,98},{4,0},{6,102},{8,4},{10,106},{12,8},{14,110},{16,28}... | collective-permute-start | bytes 393224 | tf_op jit(solution)/shard_map/ppermute | solution.py:63
  47.6 6.4 %collective-permute-start.18 = (bf16[8,64,128]{2,1,0:T(8,128)(2,1)S(1)}, bf16[8,64,128]{2,1,0:T(8,128)(2,1)S(1)}, u32[]{:S(2)}, u32[]{:S(2)}) collective-permute-start(bf16[8,64,128]{2,1,0:T(8,128)(2,1)S(1)} %get-tuple-element.46), channel_id=1, source_target_pairs={{0,4},{2,34},{4,8},{6,38},{8,12},{10,42},{12,0},{14,46},{16,20},{1... | collective-permute-start | bytes 393224 | tf_op jit(solution)/shard_map/ppermute | solution.py:63
  48.2 5.8 %collective-permute-start.19 = (bf16[8,64,128]{2,1,0:T(8,128)(2,1)S(1)}, bf16[8,64,128]{2,1,0:T(8,128)(2,1)S(1)}, u32[]{:S(2)}, u32[]{:S(2)}) collective-permute-start(bf16[8,64,128]{2,1,0:T(8,128)(2,1)S(1)} %get-tuple-element.47), channel_id=1, source_target_pairs={{0,8},{2,66},{4,12},{6,70},{8,0},{10,74},{12,4},{14,78},{16,24},{1... | collective-permute-start | bytes 393224 | tf_op jit(solution)/shard_map/ppermute | solution.py:63
  54.5 5.4 %collective-permute-start.20 = (bf16[4,64,128]{2,1,0:T(8,128)(2,1)S(1)}, bf16[4,64,128]{2,1,0:T(8,128)(2,1)S(1)}, u32[]{:S(2)}, u32[]{:S(2)}) collective-permute-start(bf16[4,64,128]{2,1,0:T(8,128)(2,1)S(1)} %get-tuple-element.50), channel_id=1, source_target_pairs={{0,2},{2,0},{4,6},{6,4},{8,10},{10,8},{12,14},{14,12},{16,18},{18,... | collective-permute-start | bytes 196616 | tf_op jit(solution)/shard_map/ppermute | solution.py:63
  61.2 11.6 %collective-permute-start.21 = (bf16[64,3072]{1,0:T(8,128)(2,1)S(1)}, bf16[64,3072]{1,0:T(8,128)(2,1)S(1)}, u32[]{:S(2)}, u32[]{:S(2)}) collective-permute-start(bf16[64,3072]{1,0:T(8,128)(2,1)S(1)} %output_projection.2), channel_id=1, source_target_pairs={{0,1},{1,0},{2,3},{3,2},{4,5},{5,4},{6,7},{7,6},{8,9},{9,8},{10,11... | collective-permute-start | bytes 1179656 | tf_op jit(solution)/shard_map/ppermute | solution.py:67
  61.3 5.2 %collective-permute-start.13 = (bf16[8,64,128]{2,1,0:T(8,128)(2,1)S(1)}, bf16[8,64,128]{2,1,0:T(8,128)(2,1)S(1)}, u32[]{:S(2)}, u32[]{:S(2)}) collective-permute-start(bf16[8,64,128]{2,1,0:T(8,128)(2,1)S(1)} %get-tuple-element.38), channel_id=1, source_target_pairs={{0,12},{2,98},{4,0},{6,102},{8,4},{10,106},{12,8},{14,110},{16,28}... | collective-permute-start | bytes 393224 | tf_op jit(solution)/shard_map/ppermute | solution.py:63
  64.6 6.4 %collective-permute-start.14 = (bf16[8,64,128]{2,1,0:T(8,128)(2,1)S(1)}, bf16[8,64,128]{2,1,0:T(8,128)(2,1)S(1)}, u32[]{:S(2)}, u32[]{:S(2)}) collective-permute-start(bf16[8,64,128]{2,1,0:T(8,128)(2,1)S(1)} %get-tuple-element.39), channel_id=1, source_target_pairs={{0,4},{2,34},{4,8},{6,38},{8,12},{10,42},{12,0},{14,46},{16,20},{1... | collective-permute-start | bytes 393224 | tf_op jit(solution)/shard_map/ppermute | solution.py:63
  64.6 6.4 %collective-permute-start.15 = (bf16[8,64,128]{2,1,0:T(8,128)(2,1)S(1)}, bf16[8,64,128]{2,1,0:T(8,128)(2,1)S(1)}, u32[]{:S(2)}, u32[]{:S(2)}) collective-permute-start(bf16[8,64,128]{2,1,0:T(8,128)(2,1)S(1)} %get-tuple-element.40), channel_id=1, source_target_pairs={{0,8},{2,66},{4,12},{6,70},{8,0},{10,74},{12,4},{14,78},{16,24},{1... | collective-permute-start | bytes 393224 | tf_op jit(solution)/shard_map/ppermute | solution.py:63
  71.5 1.3 %collective-permute-start.16 = (bf16[4,64,128]{2,1,0:T(8,128)(2,1)S(1)}, bf16[4,64,128]{2,1,0:T(8,128)(2,1)S(1)}, u32[]{:S(2)}, u32[]{:S(2)}) collective-permute-start(bf16[4,64,128]{2,1,0:T(8,128)(2,1)S(1)} %get-tuple-element.43), channel_id=1, source_target_pairs={{0,2},{2,0},{4,6},{6,4},{8,10},{10,8},{12,14},{14,12},{16,18},{18,... | collective-permute-start | bytes 196616 | tf_op jit(solution)/shard_map/ppermute | solution.py:63

commit v5 on v4

--- a/solution.py
+++ b/solution.py
@@ -157,59 +157,53 @@
     return kernel_call(_query_kernel, "query_projection", outs, [], place, [], *arrays)
 
 
-def _home_kernel(
-    place, count, text_ref, w_ref, x_ref, table_ref, q_ref, out_ref, home_ref, stat_ref, text, s_ref, sem
-):
-    bring = pltpu.make_async_copy(text_ref, text, sem)
-    bring.start()
-    slots = text.shape[1]
+def _kv_kernel(place, w_ref, x_ref, table_ref, out_ref, kv_ref):
     first = pl.ds(pl.multiple_of((1 - place[1]) * HALF, HALF), HALF)
     second = pl.ds(pl.multiple_of(place[1] * HALF, HALF), HALF)
-    bring.wait()
-    for head in range(HEADS):
-        at = slice(head * HD, (head + 1) * HD)
-        s = _scores(q_ref[head], text[0, :, at])
-        s_ref[head, :, :slots] = jnp.where(_lane(s.shape) < count[0], s, -jnp.inf)
     projected = jnp.dot(x_ref[...], w_ref[1], preferred_element_type=F32)
     for head in range(HEADS):
         at = slice(head * HD, (head + 1) * HD)
         k = _turn(projected[:, at], table_ref, 1).astype(BF16)
         out_ref[0, first, at] = k[:HALF]
         out_ref[0, second, at] = k[HALF:]
-        s_ref[head, :, slots:] = _scores(q_ref[head], k)
+        kv_ref[0, :, at] = k
     v = jnp.dot(x_ref[...], w_ref[2], preferred_element_type=F32).astype(BF16)
     out_ref[1, first, :] = v[:HALF]
     out_ref[1, second, :] = v[HALF:]
+    kv_ref[1] = v
+
+
+def project_keys(place, *arrays, after):
+    outs = [((2, TOK, FEAT), BF16, HBM), ((2, TOK, FEAT), BF16)]
+    return kernel_call(_kv_kernel, "key_value_projection", outs, [], place, [], *arrays, after=after)
+
+
+def _home_kernel(count, text, q_ref, kv_ref, home_ref, stat_ref, s_ref):
+    slots = text.shape[1]
+
+    def score(head):
+        at = slice(head * HD, (head + 1) * HD)
+        s_ref[head, :, slots:] = _scores(q_ref[head], kv_ref[0, :, at])
+        s = _scores(q_ref[head], text[0, :, at])
+        s_ref[head, :, :slots] = jnp.where(_lane(s.shape) < count[0], s, -jnp.inf)
+
     stat = jnp.zeros((TOK, HD), F32)
+    score(0)
     for head in range(HEADS):
+        if head + 1 < HEADS:
+            score(head + 1)
         at = slice(head * HD, (head + 1) * HD)
-        peak, out = _fold(s_ref[head], None, jnp.concatenate([text[1, :, at], v[:, at]], axis=0))
+        peak, out = _fold(s_ref[head], None, jnp.concatenate([text[1, :, at], kv_ref[1, :, at]], axis=0))
         total = out[:, HD:]
         home_ref[head] = (out[:, :HD] / total).astype(BF16)
         stat = jnp.where(_lane(stat.shape) == head, peak + jnp.log2(total), stat)
     stat_ref[...] = stat
 
 
-def attend_home(place, count, text_kv, w, *arrays, after):
-    outs = [((2, TOK, FEAT), BF16, HBM), ((HEADS, TOK, HD), BF16), ((TOK, HD), F32)]
-    scratch = [
-        (text_kv.shape, BF16),
-        ((HEADS, TOK, text_kv.shape[1] + TOK), F32),
-        pltpu.SemaphoreType.DMA(()),
-    ]
-    return kernel_call(
-        _home_kernel,
-        "home_attention",
-        outs,
-        scratch,
-        place,
-        [count],
-        w,
-        *arrays,
-        outside=[text_kv],
-        after=after,
-        limit=12,
-    )
+def attend_home(count, text_kv, *arrays, after):
+    outs = [((HEADS, TOK, HD), BF16), ((TOK, HD), F32)]
+    scratch = [((HEADS, TOK, text_kv.shape[1] + TOK), F32)]
+    return kernel_call(_home_kernel, "home_attention", outs, scratch, [], [count], text_kv, *arrays, after=after)
 
 
 def _join_kernel(a_ref, b_ref, out_ref):
@@ -478,10 +472,11 @@
     units = join_units(q_mine, move(q_given, _core_move), near[1:3])
     queries = [units] + [move(units, _query_move(d)) for d in (1, 3, 2)]
     far_two = move(near[3], _y_move)
-    fresh_kv, home, level = attend_home(place, text_count, text_kv, w, x, table, q_own, after=[units, near[3]])
-    far_pair = gate(far_pair, queries[1:4] + [home])
+    fresh_kv, kv = project_keys(place, w, x, table, after=[units, near[3]])
+    far_pair = gate(far_pair, queries[1:4] + [kv])
     far = [far_pair] + [move(far_pair, _key_move(d)) for d in (1, 3)] + [far_two]
-    acc, stat = attend_near(place, queries, near, [far_pair])
+    home, level = attend_home(text_count, text_kv, q_own, kv, after=[far_pair])
+    acc, stat = attend_near(place, queries, near, [home])
 
     first = attend_far(0, place, queries, acc, stat, far, [])
     own, *second = attend_far(1, place, queries, acc, stat, far, [])

time: 75.3 us -> 73.8 us (0.980)
  Pallas kernels: 25 us -> 23.8 us
    pallas_call x11 -> x12, Pallas kernels: 25 us -> 23.8 us  [kernel_call(): pl.pallas_call(run, in_specs=[SMEM] * len(scalars) + [ANY] * len(outside)...]
  transfers between devices with their start and end apart: 22 -> 22, of which waited for: 8 -> 9; matrix products, arithmetic and copies ran while one was open for 1% -> 1% of each run, Pallas kernels for 25% -> 24%
where the time goes in v5:
time: 73.8 us; the launch traced here: 73.6 us
  starting transfers between devices  34.9 us (47%)
  Pallas kernels  23.8 us (32%)
  waiting for transfers between devices  10.5 us (14%)
  between operations  2.13 us (3%)
  local copies, waits for them, and re-layouts  1.09 us (1%)
  other arithmetic  1.07 us (1%)
    ppermute x20, starting transfers between devices, move(): return lax.ppermute(array, 'patch', _perm(how))  32.9 us
    pallas_call x12, Pallas kernels, kernel_call(): pl.pallas_call(run, in_specs=[SMEM] * len(scalars) + [ANY] * len(outside)...  23.8 us
    ppermute x20, waiting for transfers between devices, move(): return lax.ppermute(array, 'patch', _perm(how))  10.5 us
    ppermute x2, starting transfers between devices, swap_heads(): return lax.ppermute(array, 'head', [(0, 1), (1, 0)])  1.97 us
  transfers between devices with their start and end apart: 22, of which 9 were waited for; matrix products, arithmetic and copies ran while one was open for 1% of the time, Pallas kernels for 24%

profile of v5, /device:TPU:1, one launch (start us, length us, event | category | flops | bytes accessed | tf_op | source)
XLA Modules:
  0.0 73.6 jit_solution(6150943614388607378)
XLA Ops:
  0.7 1.1 %constant_dynamic-slice_fusion.1 = (bf16[2,128,512]{2,1,0:T(8,128)(2,1)S(1)}, bf16[2,128,512]{2,1,0:T(8,128)(2,1)S(1)}) fusion(bf16[2,128,896]{2,1,0:T(8,128)(2,1)} %param.14, s32[]{:T(128)S(6)} %select_n.46, s32[]{:T(128)S(6)} %select_n.47), kind=kLoop, calls=%fused_computation.14 | loop fusion | bytes 1048584 | tf_op jit(solution)/shard_map/dynamic_slice | solution.py:456
  1.7 1.5 %collective-permute-start = (bf16[2,128,512]{2,1,0:T(8,128)(2,1)S(1)}, bf16[2,128,512]{2,1,0:T(8,128)(2,1)S(1)}, u32[]{:S(2)}, u32[]{:S(2)}) collective-permute-start(bf16[2,128,512]{2,1,0:T(8,128)(2,1)S(1)} %get-tuple-element.55), channel_id=1, source_target_pairs={{0,2},{2,0},{4,6},{6,4},{8,10},{10,8},{12,14},{14,12},{16,18},{18,... | collective-permute-start | bytes 786440 | tf_op jit(solution)/shard_map/ppermute | solution.py:63
  3.2 1.4 %collective-permute-start.1 = (bf16[64,3072]{1,0:T(8,128)(2,1)}, bf16[64,3072]{1,0:T(8,128)(2,1)S(1)}, u32[]{:S(2)}, u32[]{:S(2)}) collective-permute-start(bf16[64,3072]{1,0:T(8,128)(2,1)} %refs_1_.2), channel_id=1, source_target_pairs={{0,1},{1,0},{2,3},{3,2},{4,5},{5,4},{6,7},{7,6},{8,9},{9,8},{10,11... | collective-permute-start | bytes 1179656 | tf_op jit(solution)/shard_map/ppermute | solution.py:67
  5.3 1.7 %collective-permute-start.3 = (bf16[2,256,512]{2,1,0:T(8,128)(2,1)S(1)}, bf16[2,256,512]{2,1,0:T(8,128)(2,1)S(1)}, u32[]{:S(2)}, u32[]{:S(2)}) collective-permute-start(bf16[2,256,512]{2,1,0:T(8,128)(2,1)S(1)} %pad_maximum_fusion.refs_4_.refs_6_), channel_id=1, source_target_pairs={{0,32},{2,6},{4,36},{6,10},{8,40},{10,14},{12,44},{14,2},{16,48},{... | collective-permute-start | bytes 1572872 | tf_op jit(solution)/shard_map/ppermute | solution.py:63
  7.0 2.2 %collective-permute-start.4 = (bf16[2,256,512]{2,1,0:T(8,128)(2,1)S(1)}, bf16[2,256,512]{2,1,0:T(8,128)(2,1)S(1)}, u32[]{:S(2)}, u32[]{:S(2)}) collective-permute-start(bf16[2,256,512]{2,1,0:T(8,128)(2,1)S(1)} %pad_maximum_fusion.refs_4_.refs_6_), channel_id=1, source_target_pairs={{0,96},{2,14},{4,100},{6,2},{8,104},{10,6},{12,108},{14,10},{16,11... | collective-permute-start | bytes 1572872 | tf_op jit(solution)/shard_map/ppermute | solution.py:63
  9.3 1.3 %collective-permute-start.8 = (bf16[2,256,512]{2,1,0:T(8,128)(2,1)S(1)}, bf16[2,256,512]{2,1,0:T(8,128)(2,1)S(1)}, u32[]{:S(2)}, u32[]{:S(2)}) collective-permute-start(bf16[2,256,512]{2,1,0:T(8,128)(2,1)S(1)} %pad_maximum_fusion.refs_4_.refs_6_), channel_id=1, source_target_pairs={{0,64},{2,10},{4,68},{6,14},{8,72},{10,2},{12,76},{14,6},{16,80},{... | collective-permute-start | bytes 1572872 | tf_op jit(solution)/shard_map/ppermute | solution.py:63
  10.6 2.6 %collective-permute-start.9 = (bf16[2,256,512]{2,1,0:T(8,128)(2,1)S(1)}, bf16[2,256,512]{2,1,0:T(8,128)(2,1)S(1)}, u32[]{:S(2)}, u32[]{:S(2)}) collective-permute-start(bf16[2,256,512]{2,1,0:T(8,128)(2,1)S(1)} %pad_maximum_fusion.refs_4_.refs_6_), channel_id=1, source_target_pairs={{0,16},{2,18},{4,20},{6,22},{8,24},{10,26},{12,28},{14,30},{16,0},... | collective-permute-start | bytes 1572872 | tf_op jit(solution)/shard_map/ppermute | solution.py:63
  13.2 1.0 %fusion = (f32[1,128,128]{2,1,0:T(8,128)S(1)}, f32[1,128,128]{2,1,0:T(8,128)S(1)}) fusion(f32[128]{0:T(128)} %constant.65.clone, f32[128]{0:T(128)S(1)} %get-tuple-element.58, f32[128]{0:T(128)} %constant.64.clone, f32[128]{0:T(128)S(1)} %get-tuple-element.59, f32[128]{0:T(128)} %constant.66.clone), kind=kLoop, calls=%fused_computation.4 | loop fusion | flops 65536 | bytes 133632 | tf_op jit(solution)/shard_map/cos | solution.py:467
  14.2 2.9 %stage.1 = (bf16[1,3072,896]{2,1,0:T(8,128)(2,1)S(1)}, bf16[64,3072]{1,0:T(8,128)(2,1)S(1)}, f32[4,128,128]{2,1,0:T(8,128)S(1)}) custom-call(bf16[3,3072,896]{2,1,0:T(8,128)(2,1)} %bitcast.5, bf16[64,3072]{1,0:T(8,128)(2,1)} %refs_1_.2, f32[2,128]{1,0:T(2,128)} %refs_2_.1, f32[2,128,128]{2,1,0:T(8,128)S(1)} %pad_maximum_fusion.1.refs_3_, ...), custom_call_target="tpu_custom_call" | custom-call | flops 1 | bytes 1 | tf_op jit(solution)/shard_map/stage/pallas_call | solution.py:78
  17.1 1.3 %query_projection.1 = (bf16[4,128,128]{2,1,0:T(8,128)(2,1)S(1)}, bf16[3,128,128]{2,1,0:T(8,128)(2,1)S(1)}, bf16[7,128,128]{2,1,0:T(8,128)(2,1)S(1)}, bf16[128,3072]{1,0:T(8,128)(2,1)S(1)}) custom-call(s32[1]{0:T(128)} %bitcast.refs_0_, s32[1]{0:T(128)} %bitcast.1.refs_1_, bf16[1,3072,896]{2,1,0:T(8,128)(2,1)S(1)} %get-tuple-element.28.refs_2_, ...), custom_call_target="tpu_custom_call" | custom-call | flops 1 | bytes 1 | tf_op jit(solution)/shard_map/query_projection/pallas_call | solution.py:78
  19.1 0.9 %collective-permute-done.2.refs_1_ = bf16[3,128,128]{2,1,0:T(8,128)(2,1)S(1)} collective-permute-done((bf16[3,128,128]{2,1,0:T(8,128)(2,1)S(1)}, bf16[3,128,128]{2,1,0:T(8,128)(2,1)S(1)}, u32[]{:S(2)}, u32[]{:S(2)}) %collective-permute-start.2) | collective-permute-done | bytes 98336 | tf_op jit(solution)/shard_map/ppermute | solution.py:63
  20.1 0.9 %collective-permute-done.4.refs_3_.refs_8_ = bf16[2,256,512]{2,1,0:T(8,128)(2,1)S(1)} collective-permute-done((bf16[2,256,512]{2,1,0:T(8,128)(2,1)S(1)}, bf16[2,256,512]{2,1,0:T(8,128)(2,1)S(1)}, u32[]{:S(2)}, u32[]{:S(2)}) %collective-permute-start.4) | collective-permute-done | bytes 524320 | tf_op jit(solution)/shard_map/ppermute | solution.py:63
  21.0 1.3 %collective-permute-start.5 = (bf16[7,128,128]{2,1,0:T(8,128)(2,1)S(1)}, bf16[7,128,128]{2,1,0:T(8,128)(2,1)S(1)}, u32[]{:S(2)}, u32[]{:S(2)}) collective-permute-start(bf16[7,128,128]{2,1,0:T(8,128)(2,1)S(1)} %join_units.1.refs_5_.refs_2_), channel_id=1, source_target_pairs={{0,4},{2,34},{4,8},{6,38},{8,12},{10,42},{12,0},{14,46},{16,20},{1... | collective-permute-start | bytes 688136 | tf_op jit(solution)/shard_map/ppermute | solution.py:63
  22.3 1.5 %collective-permute-start.6 = (bf16[7,128,128]{2,1,0:T(8,128)(2,1)S(1)}, bf16[7,128,128]{2,1,0:T(8,128)(2,1)S(1)}, u32[]{:S(2)}, u32[]{:S(2)}) collective-permute-start(bf16[7,128,128]{2,1,0:T(8,128)(2,1)S(1)} %join_units.1.refs_5_.refs_2_), channel_id=1, source_target_pairs={{0,12},{2,98},{4,0},{6,102},{8,4},{10,106},{12,8},{14,110},{16,28}... | collective-permute-start | bytes 688136 | tf_op jit(solution)/shard_map/ppermute | solution.py:63
  23.7 1.5 %collective-permute-start.7 = (bf16[7,128,128]{2,1,0:T(8,128)(2,1)S(1)}, bf16[7,128,128]{2,1,0:T(8,128)(2,1)S(1)}, u32[]{:S(2)}, u32[]{:S(2)}) collective-permute-start(bf16[7,128,128]{2,1,0:T(8,128)(2,1)S(1)} %join_units.1.refs_5_.refs_2_), channel_id=1, source_target_pairs={{0,8},{2,66},{4,12},{6,70},{8,0},{10,74},{12,4},{14,78},{16,24},{1... | collective-permute-start | bytes 688136 | tf_op jit(solution)/shard_map/ppermute | solution.py:63
  25.3 2.6 %collective-permute-start.12 = (bf16[2,256,512]{2,1,0:T(8,128)(2,1)S(1)}, bf16[2,256,512]{2,1,0:T(8,128)(2,1)S(1)}, u32[]{:S(2)}, u32[]{:S(2)}) collective-permute-start(bf16[2,256,512]{2,1,0:T(8,128)(2,1)S(1)} %collective-permute-done.8.refs_6_.refs_9_), channel_id=1, source_target_pairs={{0,16},{2,18},{4,20},{6,22},{8,24},{10,26},{12,28},{14,30},{16,0},... | collective-permute-start | bytes 1572872 | tf_op jit(solution)/shard_map/ppermute | solution.py:63
  27.9 2.7 %key_value_projection.1 = (bf16[2,128,896]{2,1,0:T(8,128)(2,1)}, bf16[2,128,896]{2,1,0:T(8,128)(2,1)S(1)}) custom-call(s32[1]{0:T(128)} %bitcast.refs_0_, s32[1]{0:T(128)} %bitcast.1.refs_1_, bf16[3,3072,896]{2,1,0:T(8,128)(2,1)S(1)} %bitcast.6, bf16[128,3072]{1,0:T(8,128)(2,1)S(1)} %get-tuple-element.34.refs_3_, ...), custom_call_target="tpu_custom_call" | custom-call | flops 1 | bytes 1 | tf_op jit(solution)/shard_map/key_value_projection/pallas_call | solution.py:78
  30.9 3.4 %collective-permute-start.11 = (bf16[2,256,512]{2,1,0:T(8,128)(2,1)S(1)}, bf16[2,256,512]{2,1,0:T(8,128)(2,1)S(1)}, u32[]{:S(2)}, u32[]{:S(2)}) collective-permute-start(bf16[2,256,512]{2,1,0:T(8,128)(2,1)S(1)} %gate.1.refs_4_.refs_8_), channel_id=1, source_target_pairs={{0,96},{2,14},{4,100},{6,2},{8,104},{10,6},{12,108},{14,10},{16,11... | collective-permute-start | bytes 1572872 | tf_op jit(solution)/shard_map/ppermute | solution.py:63
  35.0 1.2 %home_attention.1 = (bf16[7,128,128]{2,1,0:T(8,128)(2,1)S(1)}, f32[128,128]{1,0:T(8,128)S(1)}) custom-call(s32[1]{0:T(128)S(6)} %copy.15.refs_0_, bf16[2,512,896]{2,1,0:T(8,128)(2,1)S(1)} %copy-done.1, bf16[7,128,128]{2,1,0:T(8,128)(2,1)S(1)} %get-tuple-element.33.refs_2_, bf16[2,128,896]{2,1,0:T(8,128)(2,1)S(1)} %get-tuple-element.35.refs_3_, ...), custom_call_target="tpu_custom_call" | custom-call | flops 1 | bytes 1 | tf_op jit(solution)/shard_map/home_attention/pallas_call | solution.py:78
  36.2 4.7 %near_attention.1 = (f32[7,512,128]{2,1,0:T(8,128)S(1)}, f32[512,128]{1,0:T(8,128)S(1)}) custom-call(s32[1]{0:T(128)} %bitcast.refs_0_, s32[1]{0:T(128)} %bitcast.1.refs_1_, bf16[7,128,128]{2,1,0:T(8,128)(2,1)S(1)} %join_units.1.refs_5_.refs_2_, bf16[7,128,128]{2,1,0:T(8,128)(2,1)S(1)} %collective-permute-done.5.refs_0_.refs_3_, ...), custom_call_target="tpu_custom_call" | custom-call | flops 1 | bytes 1 | tf_op jit(solution)/shard_map/near_attention/pallas_call | solution.py:78
  41.2 2.7 %far_attention_0.1 = (bf16[8,64,128]{2,1,0:T(8,128)(2,1)S(1)}, bf16[8,64,128]{2,1,0:T(8,128)(2,1)S(1)}, bf16[8,64,128]{2,1,0:T(8,128)(2,1)S(1)}) custom-call(s32[1]{0:T(128)} %bitcast.refs_0_, s32[1]{0:T(128)} %bitcast.1.refs_1_, bf16[7,128,128]{2,1,0:T(8,128)(2,1)S(1)} %join_units.1.refs_5_.refs_2_, ...), custom_call_target="tpu_custom_call" | custom-call | flops 1 | bytes 1 | tf_op jit(solution)/shard_map/far_attention_0/pallas_call | solution.py:78
  43.8 1.8 %collective-permute-start.17 = (bf16[8,64,128]{2,1,0:T(8,128)(2,1)S(1)}, bf16[8,64,128]{2,1,0:T(8,128)(2,1)S(1)}, u32[]{:S(2)}, u32[]{:S(2)}) collective-permute-start(bf16[8,64,128]{2,1,0:T(8,128)(2,1)S(1)} %get-tuple-element.47), channel_id=1, source_target_pairs={{0,12},{2,98},{4,0},{6,102},{8,4},{10,106},{12,8},{14,110},{16,28}... | collective-permute-start | bytes 393224 | tf_op jit(solution)/shard_map/ppermute | solution.py:63
  45.6 1.3 %collective-permute-start.19 = (bf16[8,64,128]{2,1,0:T(8,128)(2,1)S(1)}, bf16[8,64,128]{2,1,0:T(8,128)(2,1)S(1)}, u32[]{:S(2)}, u32[]{:S(2)}) collective-permute-start(bf16[8,64,128]{2,1,0:T(8,128)(2,1)S(1)} %get-tuple-element.49), channel_id=1, source_target_pairs={{0,8},{2,66},{4,12},{6,70},{8,0},{10,74},{12,4},{14,78},{16,24},{1... | collective-permute-start | bytes 393224 | tf_op jit(solution)/shard_map/ppermute | solution.py:63
  46.9 4.1 %far_attention_1.1 = (bf16[8,128,128]{2,1,0:T(8,128)(2,1)S(1)}, bf16[8,64,128]{2,1,0:T(8,128)(2,1)S(1)}, bf16[8,64,128]{2,1,0:T(8,128)(2,1)S(1)}, bf16[8,64,128]{2,1,0:T(8,128)(2,1)S(1)}) custom-call(s32[1]{0:T(128)} %bitcast.refs_0_, s32[1]{0:T(128)} %bitcast.1.refs_1_, bf16[7,128,128]{2,1,0:T(8,128)(2,1)S(1)} %join_units.1.refs_5_.refs_2_, ...), custom_call_target="tpu_custom_call" | custom-call | flops 1 | bytes 1 | tf_op jit(solution)/shard_map/far_attention_1/pallas_call | solution.py:78
  51.0 1.1 %collective-permute-done.18.refs_2_ = bf16[8,64,128]{2,1,0:T(8,128)(2,1)S(1)} collective-permute-done((bf16[8,64,128]{2,1,0:T(8,128)(2,1)S(1)}, bf16[8,64,128]{2,1,0:T(8,128)(2,1)S(1)}, u32[]{:S(2)}, u32[]{:S(2)}) %collective-permute-start.18) | collective-permute-done | bytes 131104 | tf_op jit(solution)/shard_map/ppermute | solution.py:63
  52.6 4.4 %collective-permute-start.20 = (bf16[4,64,128]{2,1,0:T(8,128)(2,1)S(1)}, bf16[4,64,128]{2,1,0:T(8,128)(2,1)S(1)}, u32[]{:S(2)}, u32[]{:S(2)}) collective-permute-start(bf16[4,64,128]{2,1,0:T(8,128)(2,1)S(1)} %get-tuple-element.52), channel_id=1, source_target_pairs={{0,2},{2,0},{4,6},{6,4},{8,10},{10,8},{12,14},{14,12},{16,18},{18,... | collective-permute-start | bytes 196616 | tf_op jit(solution)/shard_map/ppermute | solution.py:63
  57.8 1.3 %output_projection.2 = bf16[64,3072]{1,0:T(8,128)(2,1)S(1)} custom-call(s32[1]{0:T(128)} %bitcast.refs_0_, s32[1]{0:T(128)} %bitcast.1.refs_1_, bf16[4,64,128]{2,1,0:T(8,128)(2,1)S(1)} %get-tuple-element.50.refs_2_, f32[64,128]{1,0:T(8,128)S(1)} %get-tuple-element.51.refs_3_, bf16[4,64,128]{2,1,0:T(8,128)(2,1)S(1)} %collective-permute-done.20.refs_4_, ...), custom_call_target="tpu_custom_call" | custom-call | flops 1 | bytes 1 | tf_op jit(solution)/shard_map/output_projection/pallas_call | solution.py:78
  59.7 3.2 %collective-permute-start.13 = (bf16[8,64,128]{2,1,0:T(8,128)(2,1)S(1)}, bf16[8,64,128]{2,1,0:T(8,128)(2,1)S(1)}, u32[]{:S(2)}, u32[]{:S(2)}) collective-permute-start(bf16[8,64,128]{2,1,0:T(8,128)(2,1)S(1)} %get-tuple-element.40), channel_id=1, source_target_pairs={{0,12},{2,98},{4,0},{6,102},{8,4},{10,106},{12,8},{14,110},{16,28}... | collective-permute-start | bytes 393224 | tf_op jit(solution)/shard_map/ppermute | solution.py:63
  62.9 1.5 %collective-permute-start.15 = (bf16[8,64,128]{2,1,0:T(8,128)(2,1)S(1)}, bf16[8,64,128]{2,1,0:T(8,128)(2,1)S(1)}, u32[]{:S(2)}, u32[]{:S(2)}) collective-permute-start(bf16[8,64,128]{2,1,0:T(8,128)(2,1)S(1)} %get-tuple-element.42), channel_id=1, source_target_pairs={{0,8},{2,66},{4,12},{6,70},{8,0},{10,74},{12,4},{14,78},{16,24},{1... | collective-permute-start | bytes 393224 | tf_op jit(solution)/shard_map/ppermute | solution.py:63
  64.9 4.8 %collective-permute-done.14.refs_2_ = bf16[8,64,128]{2,1,0:T(8,128)(2,1)S(1)} collective-permute-done((bf16[8,64,128]{2,1,0:T(8,128)(2,1)S(1)}, bf16[8,64,128]{2,1,0:T(8,128)(2,1)S(1)}, u32[]{:S(2)}, u32[]{:S(2)}) %collective-permute-start.14) | collective-permute-done | bytes 131104 | tf_op jit(solution)/shard_map/ppermute | solution.py:63
  70.6 0.9 %collective-permute-done.16.refs_4_ = bf16[4,64,128]{2,1,0:T(8,128)(2,1)S(1)} collective-permute-done((bf16[4,64,128]{2,1,0:T(8,128)(2,1)S(1)}, bf16[4,64,128]{2,1,0:T(8,128)(2,1)S(1)}, u32[]{:S(2)}, u32[]{:S(2)}) %collective-permute-start.16) | collective-permute-done | bytes 65568 | tf_op jit(solution)/shard_map/ppermute | solution.py:63
  71.5 2.1 %output_projection.3 = bf16[64,3072]{1,0:T(8,128)(2,1)} custom-call(s32[1]{0:T(128)} %bitcast.refs_0_, s32[1]{0:T(128)} %bitcast.1.refs_1_, bf16[4,64,128]{2,1,0:T(8,128)(2,1)S(1)} %get-tuple-element.43.refs_2_, f32[64,128]{1,0:T(8,128)S(1)} %get-tuple-element.44.refs_3_, bf16[4,64,128]{2,1,0:T(8,128)(2,1)S(1)} %collective-permute-done.16.refs_4_, ...), custom_call_target="tpu_custom_call" | custom-call | flops 1 | bytes 1 | tf_op jit(solution)/shard_map/output_projection/pallas_call | solution.py:78
  (39 shorter events, 4.7 us)
Async XLA Ops:
  1.7 3.6 %collective-permute-start = (bf16[2,128,512]{2,1,0:T(8,128)(2,1)S(1)}, bf16[2,128,512]{2,1,0:T(8,128)(2,1)S(1)}, u32[]{:S(2)}, u32[]{:S(2)}) collective-permute-start(bf16[2,128,512]{2,1,0:T(8,128)(2,1)S(1)} %get-tuple-element.55), channel_id=1, source_target_pairs={{0,2},{2,0},{4,6},{6,4},{8,10},{10,8},{12,14},{14,12},{16,18},{18,... | collective-permute-start | bytes 786440 | tf_op jit(solution)/shard_map/ppermute | solution.py:63
  3.2 13.9 %collective-permute-start.1 = (bf16[64,3072]{1,0:T(8,128)(2,1)}, bf16[64,3072]{1,0:T(8,128)(2,1)S(1)}, u32[]{:S(2)}, u32[]{:S(2)}) collective-permute-start(bf16[64,3072]{1,0:T(8,128)(2,1)} %refs_1_.2), channel_id=1, source_target_pairs={{0,1},{1,0},{2,3},{3,2},{4,5},{5,4},{6,7},{7,6},{8,9},{9,8},{10,11... | collective-permute-start | bytes 1179656 | tf_op jit(solution)/shard_map/ppermute | solution.py:67
  5.3 14.7 %collective-permute-start.3 = (bf16[2,256,512]{2,1,0:T(8,128)(2,1)S(1)}, bf16[2,256,512]{2,1,0:T(8,128)(2,1)S(1)}, u32[]{:S(2)}, u32[]{:S(2)}) collective-permute-start(bf16[2,256,512]{2,1,0:T(8,128)(2,1)S(1)} %pad_maximum_fusion.refs_4_.refs_6_), channel_id=1, source_target_pairs={{0,32},{2,6},{4,36},{6,10},{8,40},{10,14},{12,44},{14,2},{16,48},{... | collective-permute-start | bytes 1572872 | tf_op jit(solution)/shard_map/ppermute | solution.py:63
  7.0 13.9 %collective-permute-start.4 = (bf16[2,256,512]{2,1,0:T(8,128)(2,1)S(1)}, bf16[2,256,512]{2,1,0:T(8,128)(2,1)S(1)}, u32[]{:S(2)}, u32[]{:S(2)}) collective-permute-start(bf16[2,256,512]{2,1,0:T(8,128)(2,1)S(1)} %pad_maximum_fusion.refs_4_.refs_6_), channel_id=1, source_target_pairs={{0,96},{2,14},{4,100},{6,2},{8,104},{10,6},{12,108},{14,10},{16,11... | collective-permute-start | bytes 1572872 | tf_op jit(solution)/shard_map/ppermute | solution.py:63
  9.3 16.0 %collective-permute-start.8 = (bf16[2,256,512]{2,1,0:T(8,128)(2,1)S(1)}, bf16[2,256,512]{2,1,0:T(8,128)(2,1)S(1)}, u32[]{:S(2)}, u32[]{:S(2)}) collective-permute-start(bf16[2,256,512]{2,1,0:T(8,128)(2,1)S(1)} %pad_maximum_fusion.refs_4_.refs_6_), channel_id=1, source_target_pairs={{0,64},{2,10},{4,68},{6,14},{8,72},{10,2},{12,76},{14,6},{16,80},{... | collective-permute-start | bytes 1572872 | tf_op jit(solution)/shard_map/ppermute | solution.py:63
  10.6 20.1 %collective-permute-start.9 = (bf16[2,256,512]{2,1,0:T(8,128)(2,1)S(1)}, bf16[2,256,512]{2,1,0:T(8,128)(2,1)S(1)}, u32[]{:S(2)}, u32[]{:S(2)}) collective-permute-start(bf16[2,256,512]{2,1,0:T(8,128)(2,1)S(1)} %pad_maximum_fusion.refs_4_.refs_6_), channel_id=1, source_target_pairs={{0,16},{2,18},{4,20},{6,22},{8,24},{10,26},{12,28},{14,30},{16,0},... | collective-permute-start | bytes 1572872 | tf_op jit(solution)/shard_map/ppermute | solution.py:63
  14.2 13.7 %copy-start = (bf16[3072,3,896]{2,0,1:T(8,128)(2,1)S(1)}, bf16[3072,3,896]{2,0,1:T(8,128)(2,1)}, u32[]{:S(2)}) copy-start(bf16[3072,3,896]{2,0,1:T(8,128)(2,1)} %param.12) | copy-start | bytes 49545220
  18.4 1.6 %collective-permute-start.2 = (bf16[3,128,128]{2,1,0:T(8,128)(2,1)S(1)}, bf16[3,128,128]{2,1,0:T(8,128)(2,1)S(1)}, u32[]{:S(2)}, u32[]{:S(2)}) collective-permute-start(bf16[3,128,128]{2,1,0:T(8,128)(2,1)S(1)} %get-tuple-element.32), channel_id=1, source_target_pairs={{0,2},{2,0},{4,6},{6,4},{8,10},{10,8},{12,14},{14,12},{16,18},{18,... | collective-permute-start | bytes 294920 | tf_op jit(solution)/shard_map/ppermute | solution.py:63
  21.0 9.6 %collective-permute-start.5 = (bf16[7,128,128]{2,1,0:T(8,128)(2,1)S(1)}, bf16[7,128,128]{2,1,0:T(8,128)(2,1)S(1)}, u32[]{:S(2)}, u32[]{:S(2)}) collective-permute-start(bf16[7,128,128]{2,1,0:T(8,128)(2,1)S(1)} %join_units.1.refs_5_.refs_2_), channel_id=1, source_target_pairs={{0,4},{2,34},{4,8},{6,38},{8,12},{10,42},{12,0},{14,46},{16,20},{1... | collective-permute-start | bytes 688136 | tf_op jit(solution)/shard_map/ppermute | solution.py:63
  22.3 8.3 %collective-permute-start.6 = (bf16[7,128,128]{2,1,0:T(8,128)(2,1)S(1)}, bf16[7,128,128]{2,1,0:T(8,128)(2,1)S(1)}, u32[]{:S(2)}, u32[]{:S(2)}) collective-permute-start(bf16[7,128,128]{2,1,0:T(8,128)(2,1)S(1)} %join_units.1.refs_5_.refs_2_), channel_id=1, source_target_pairs={{0,12},{2,98},{4,0},{6,102},{8,4},{10,106},{12,8},{14,110},{16,28}... | collective-permute-start | bytes 688136 | tf_op jit(solution)/shard_map/ppermute | solution.py:63
  23.7 7.1 %collective-permute-start.7 = (bf16[7,128,128]{2,1,0:T(8,128)(2,1)S(1)}, bf16[7,128,128]{2,1,0:T(8,128)(2,1)S(1)}, u32[]{:S(2)}, u32[]{:S(2)}) collective-permute-start(bf16[7,128,128]{2,1,0:T(8,128)(2,1)S(1)} %join_units.1.refs_5_.refs_2_), channel_id=1, source_target_pairs={{0,8},{2,66},{4,12},{6,70},{8,0},{10,74},{12,4},{14,78},{16,24},{1... | collective-permute-start | bytes 688136 | tf_op jit(solution)/shard_map/ppermute | solution.py:63
  25.3 15.6 %collective-permute-start.12 = (bf16[2,256,512]{2,1,0:T(8,128)(2,1)S(1)}, bf16[2,256,512]{2,1,0:T(8,128)(2,1)S(1)}, u32[]{:S(2)}, u32[]{:S(2)}) collective-permute-start(bf16[2,256,512]{2,1,0:T(8,128)(2,1)S(1)} %collective-permute-done.8.refs_6_.refs_9_), channel_id=1, source_target_pairs={{0,16},{2,18},{4,20},{6,22},{8,24},{10,26},{12,28},{14,30},{16,0},... | collective-permute-start | bytes 1572872 | tf_op jit(solution)/shard_map/ppermute | solution.py:63
  27.9 7.1 %copy-start.1 = (bf16[2,512,896]{2,1,0:T(8,128)(2,1)S(1)}, bf16[2,512,896]{2,1,0:T(8,128)(2,1)}, u32[]{:S(2)}) copy-start(bf16[2,512,896]{2,1,0:T(8,128)(2,1)} %refs_1_.3) | copy-start | bytes 5505028
  30.9 10.3 %collective-permute-start.10 = (bf16[2,256,512]{2,1,0:T(8,128)(2,1)S(1)}, bf16[2,256,512]{2,1,0:T(8,128)(2,1)S(1)}, u32[]{:S(2)}, u32[]{:S(2)}) collective-permute-start(bf16[2,256,512]{2,1,0:T(8,128)(2,1)S(1)} %gate.1.refs_4_.refs_8_), channel_id=1, source_target_pairs={{0,32},{2,6},{4,36},{6,10},{8,40},{10,14},{12,44},{14,2},{16,48},{... | collective-permute-start | bytes 1572872 | tf_op jit(solution)/shard_map/ppermute | solution.py:63
  30.9 10.3 %collective-permute-start.11 = (bf16[2,256,512]{2,1,0:T(8,128)(2,1)S(1)}, bf16[2,256,512]{2,1,0:T(8,128)(2,1)S(1)}, u32[]{:S(2)}, u32[]{:S(2)}) collective-permute-start(bf16[2,256,512]{2,1,0:T(8,128)(2,1)S(1)} %gate.1.refs_4_.refs_8_), channel_id=1, source_target_pairs={{0,96},{2,14},{4,100},{6,2},{8,104},{10,6},{12,108},{14,10},{16,11... | collective-permute-start | bytes 1572872 | tf_op jit(solution)/shard_map/ppermute | solution.py:63
  36.2 21.7 %slice-start = ((s8[5505024]{0:T(1024)(128)(4,1)}), s8[4194304]{0:T(1024)(128)(4,1)S(1)}, s32[]{:S(2)}) async-start(s8[5505024]{0:T(1024)(128)(4,1)} %bitcast.7), calls=%async_computation | async-start | bytes 8388608
  41.2 16.7 %slice-start.1 = ((s8[5505024]{0:T(1024)(128)(4,1)}), s8[1310720]{0:T(1024)(128)(4,1)S(1)}, s32[]{:S(2)}) async-start(s8[5505024]{0:T(1024)(128)(4,1)} %bitcast.7), calls=%async_computation.1 | async-start | bytes 2621440
  43.8 7.1 %collective-permute-start.17 = (bf16[8,64,128]{2,1,0:T(8,128)(2,1)S(1)}, bf16[8,64,128]{2,1,0:T(8,128)(2,1)S(1)}, u32[]{:S(2)}, u32[]{:S(2)}) collective-permute-start(bf16[8,64,128]{2,1,0:T(8,128)(2,1)S(1)} %get-tuple-element.47), channel_id=1, source_target_pairs={{0,12},{2,98},{4,0},{6,102},{8,4},{10,106},{12,8},{14,110},{16,28}... | collective-permute-start | bytes 393224 | tf_op jit(solution)/shard_map/ppermute | solution.py:63
  45.6 6.4 %collective-permute-start.18 = (bf16[8,64,128]{2,1,0:T(8,128)(2,1)S(1)}, bf16[8,64,128]{2,1,0:T(8,128)(2,1)S(1)}, u32[]{:S(2)}, u32[]{:S(2)}) collective-permute-start(bf16[8,64,128]{2,1,0:T(8,128)(2,1)S(1)} %get-tuple-element.48), channel_id=1, source_target_pairs={{0,4},{2,34},{4,8},{6,38},{8,12},{10,42},{12,0},{14,46},{16,20},{1... | collective-permute-start | bytes 393224 | tf_op jit(solution)/shard_map/ppermute | solution.py:63
  45.6 6.4 %collective-permute-start.19 = (bf16[8,64,128]{2,1,0:T(8,128)(2,1)S(1)}, bf16[8,64,128]{2,1,0:T(8,128)(2,1)S(1)}, u32[]{:S(2)}, u32[]{:S(2)}) collective-permute-start(bf16[8,64,128]{2,1,0:T(8,128)(2,1)S(1)} %get-tuple-element.49), channel_id=1, source_target_pairs={{0,8},{2,66},{4,12},{6,70},{8,0},{10,74},{12,4},{14,78},{16,24},{1... | collective-permute-start | bytes 393224 | tf_op jit(solution)/shard_map/ppermute | solution.py:63
  52.6 5.3 %collective-permute-start.20 = (bf16[4,64,128]{2,1,0:T(8,128)(2,1)S(1)}, bf16[4,64,128]{2,1,0:T(8,128)(2,1)S(1)}, u32[]{:S(2)}, u32[]{:S(2)}) collective-permute-start(bf16[4,64,128]{2,1,0:T(8,128)(2,1)S(1)} %get-tuple-element.52), channel_id=1, source_target_pairs={{0,2},{2,0},{4,6},{6,4},{8,10},{10,8},{12,14},{14,12},{16,18},{18,... | collective-permute-start | bytes 196616 | tf_op jit(solution)/shard_map/ppermute | solution.py:63
  59.1 12.4 %collective-permute-start.21 = (bf16[64,3072]{1,0:T(8,128)(2,1)S(1)}, bf16[64,3072]{1,0:T(8,128)(2,1)S(1)}, u32[]{:S(2)}, u32[]{:S(2)}) collective-permute-start(bf16[64,3072]{1,0:T(8,128)(2,1)S(1)} %output_projection.2), channel_id=1, source_target_pairs={{0,1},{1,0},{2,3},{3,2},{4,5},{5,4},{6,7},{7,6},{8,9},{9,8},{10,11... | collective-permute-start | bytes 1179656 | tf_op jit(solution)/shard_map/ppermute | solution.py:67
  59.7 5.1 %collective-permute-start.13 = (bf16[8,64,128]{2,1,0:T(8,128)(2,1)S(1)}, bf16[8,64,128]{2,1,0:T(8,128)(2,1)S(1)}, u32[]{:S(2)}, u32[]{:S(2)}) collective-permute-start(bf16[8,64,128]{2,1,0:T(8,128)(2,1)S(1)} %get-tuple-element.40), channel_id=1, source_target_pairs={{0,12},{2,98},{4,0},{6,102},{8,4},{10,106},{12,8},{14,110},{16,28}... | collective-permute-start | bytes 393224 | tf_op jit(solution)/shard_map/ppermute | solution.py:63
  62.9 6.7 %collective-permute-start.14 = (bf16[8,64,128]{2,1,0:T(8,128)(2,1)S(1)}, bf16[8,64,128]{2,1,0:T(8,128)(2,1)S(1)}, u32[]{:S(2)}, u32[]{:S(2)}) collective-permute-start(bf16[8,64,128]{2,1,0:T(8,128)(2,1)S(1)} %get-tuple-element.41), channel_id=1, source_target_pairs={{0,4},{2,34},{4,8},{6,38},{8,12},{10,42},{12,0},{14,46},{16,20},{1... | collective-permute-start | bytes 393224 | tf_op jit(solution)/shard_map/ppermute | solution.py:63
  62.9 6.7 %collective-permute-start.15 = (bf16[8,64,128]{2,1,0:T(8,128)(2,1)S(1)}, bf16[8,64,128]{2,1,0:T(8,128)(2,1)S(1)}, u32[]{:S(2)}, u32[]{:S(2)}) collective-permute-start(bf16[8,64,128]{2,1,0:T(8,128)(2,1)S(1)} %get-tuple-element.42), channel_id=1, source_target_pairs={{0,8},{2,66},{4,12},{6,70},{8,0},{10,74},{12,4},{14,78},{16,24},{1... | collective-permute-start | bytes 393224 | tf_op jit(solution)/shard_map/ppermute | solution.py:63
  70.1 1.4 %collective-permute-start.16 = (bf16[4,64,128]{2,1,0:T(8,128)(2,1)S(1)}, bf16[4,64,128]{2,1,0:T(8,128)(2,1)S(1)}, u32[]{:S(2)}, u32[]{:S(2)}) collective-permute-start(bf16[4,64,128]{2,1,0:T(8,128)(2,1)S(1)} %get-tuple-element.45), channel_id=1, source_target_pairs={{0,2},{2,0},{4,6},{6,4},{8,10},{10,8},{12,14},{14,12},{16,18},{18,... | collective-permute-start | bytes 196616 | tf_op jit(solution)/shard_map/ppermute | solution.py:63

commit v6 on v5

--- a/solution.py
+++ b/solution.py
@@ -399,38 +399,61 @@
     return kernel_call(functools.partial(_merge_kernel, g), "merge_parts", outs, [], [], [], *parts)
 
 
-def _out_kernel(g, place, mine_ref, stat_ref, got_ref, home_ref, level_ref, w_ref, *rest):
+def _blend(a, la, h, lh):
+    top = jnp.maximum(la, lh)
+    wa, wh = jnp.exp2(la - top), jnp.exp2(lh - top)
+    total = wa + wh
+    return (a.astype(F32) * (wa / total) + h.astype(F32) * (wh / total)).astype(BF16)
+
+
+def _rows(head):
+    return pl.ds(pl.multiple_of(head * HD, HD), HD)
+
+
+def _mine_kernel(g, place, mine_ref, stat_ref, home_ref, level_ref, w_ref, out_ref):
+    rows = slice(g * HALF, (g + 1) * HALF)
+    c = place[0]
+    low, mine, level = c == 0, stat_ref[...], level_ref[rows]
+    attended, weights = [], []
+    for slot in range(MINE + 1):
+        high = slot if slot == MINE else slot + MINE + 1
+        head = slot + (high - slot) * c
+        lh = jnp.where(low, level[:, slot : slot + 1], level[:, high : high + 1])
+        attended.append(_blend(mine_ref[slot], mine[:, slot : slot + 1], home_ref[head, rows], lh))
+        weights.append(w_ref[_rows(head), :])
+    attended, weights = jnp.concatenate(attended, axis=1), jnp.concatenate(weights, axis=0)
+    out_ref[...] = jnp.dot(attended, weights, preferred_element_type=F32)
+
+
+def _got_kernel(g, place, part_ref, got_ref, home_ref, level_ref, w_ref, *rest):
     *other, out_ref = rest
     rows = slice(g * HALF, (g + 1) * HALF)
-    first = place[0] == 0
-    mine = stat_ref[...]
+    c = place[0]
+    low, level = c == 0, level_ref[rows]
     got = _collect(got_ref[MINE])
-    attended = []
-    for head in range(HEADS):
-        slot = head % (MINE + 1)
-        a, la = mine_ref[slot], mine[:, slot : slot + 1]
-        if head != MINE:
-            low = head < MINE
-            b, lb = got_ref[slot], got[:, slot + MINE + 1 : slot + MINE + 2]
-            a, b = (a, b) if low else (b, a)
-            la, lb = (la, lb) if low else (lb, la)
-            a, la = jnp.where(first, a, b), jnp.where(first, la, lb)
-        h, lh = home_ref[head, rows], level_ref[rows, head : head + 1]
-        top = jnp.maximum(la, lh)
-        wa, wh = jnp.exp2(la - top), jnp.exp2(lh - top)
-        total = wa + wh
-        out = a.astype(F32) * (wa / total) + h.astype(F32) * (wh / total)
-        attended.append(out.astype(BF16))
-    out = jnp.dot(jnp.concatenate(attended, axis=1), w_ref[...], preferred_element_type=F32)
+    attended, weights = [], []
+    for slot in range(MINE):
+        high = slot + MINE + 1
+        head = high - (high - slot) * c
+        lh = jnp.where(low, level[:, high : high + 1], level[:, slot : slot + 1])
+        attended.append(_blend(got_ref[slot], got[:, high : high + 1], home_ref[head, rows], lh))
+        weights.append(w_ref[_rows(head), :])
+    attended, weights = jnp.concatenate(attended, axis=1), jnp.concatenate(weights, axis=0)
+    out = part_ref[...] + jnp.dot(attended, weights, preferred_element_type=F32)
     for ref in other:
         out = out + ref[...].astype(F32)
     out_ref[...] = out.astype(BF16)
 
 
-def project_out(g, place, *arrays, after):
+def project_out(g, place, mine, stat, got, home, level, w_out, *other):
+    outs = [((HALF, D), F32)]
+    arrays = (mine, stat, home, level, w_out)
+    kernel = functools.partial(_mine_kernel, g)
+    part = kernel_call(kernel, "output_projection_mine", outs, [], place, [], *arrays)[0]
     outs = [((HALF, D), BF16, HBM)]
-    kernel = functools.partial(_out_kernel, g)
-    return kernel_call(kernel, "output_projection", outs, [], place, [], *arrays, after=after)[0]
+    arrays = (part, got, home, level, w_out, *other)
+    kernel = functools.partial(_got_kernel, g)
+    return kernel_call(kernel, "output_projection_got", outs, [], place, [], *arrays)[0]
 
 
 def _bands():
@@ -483,8 +506,8 @@
     back = [[own] + [move(p, _query_move(d)) for p, d in zip(parts, (3, 1, 2))] for parts in (first, second)]
     merged = [merge(g, back[g]) for g in (0, 1)]
     got = [move(merged[g][2], _core_move) for g in (0, 1)]
-    sent = project_out(0, place, *merged[0][:2], got[0], home, level, w_out, after=[])
-    mixed = project_out(1, place, *merged[1][:2], got[1], home, level, w_out, swap_heads(sent), after=[])
+    sent = project_out(0, place, *merged[0][:2], got[0], home, level, w_out)
+    mixed = project_out(1, place, *merged[1][:2], got[1], home, level, w_out, swap_heads(sent))
     return (mixed, fresh_kv)
 
 

time: 73.8 us -> 72.5 us (0.982)
  waiting for transfers between devices: 10.5 us -> 8.96 us
    ppermute x20, waiting for transfers between devices: 10.5 us -> 8.96 us  [move(): return lax.ppermute(array, 'patch', _perm(how))]
    pallas_call x12 -> x14, Pallas kernels: 23.8 us -> 24.2 us  [kernel_call(): pl.pallas_call(run, in_specs=[SMEM] * len(scalars) + [ANY] * len(outside)...]
  transfers between devices with their start and end apart: 22 -> 22, of which waited for: 9 -> 9; matrix products, arithmetic and copies ran while one was open for 1% -> 1% of each run, Pallas kernels for 24% -> 26%
where the time goes in v6:
time: 72.5 us; the launch traced here: 72.4 us
  starting transfers between devices  34.9 us (48%)
  Pallas kernels  24.2 us (33%)
  waiting for transfers between devices  8.96 us (12%)
  between operations  2.14 us (3%)
  local copies, waits for them, and re-layouts  1.09 us (2%)
  other arithmetic  1.07 us (1%)
    ppermute x20, starting transfers between devices, move(): return lax.ppermute(array, 'patch', _perm(how))  33 us
    pallas_call x14, Pallas kernels, kernel_call(): pl.pallas_call(run, in_specs=[SMEM] * len(scalars) + [ANY] * len(outside)...  24.2 us
    ppermute x20, waiting for transfers between devices, move(): return lax.ppermute(array, 'patch', _perm(how))  8.96 us
    ppermute x2, starting transfers between devices, swap_heads(): return lax.ppermute(array, 'head', [(0, 1), (1, 0)])  1.97 us
  transfers between devices with their start and end apart: 22, of which 9 were waited for; matrix products, arithmetic and copies ran while one was open for 1% of the time, Pallas kernels for 26%

profile of v6, /device:TPU:1, one launch (start us, length us, event | category | flops | bytes accessed | tf_op | source)
XLA Modules:
  0.0 72.4 jit_solution(17478134907818689852)
XLA Ops:
  0.7 1.1 %constant_dynamic-slice_fusion.1 = (bf16[2,128,512]{2,1,0:T(8,128)(2,1)S(1)}, bf16[2,128,512]{2,1,0:T(8,128)(2,1)S(1)}) fusion(bf16[2,128,896]{2,1,0:T(8,128)(2,1)} %param.14, s32[]{:T(128)S(6)} %select_n.46, s32[]{:T(128)S(6)} %select_n.47), kind=kLoop, calls=%fused_computation.14 | loop fusion | bytes 1048584 | tf_op jit(solution)/shard_map/dynamic_slice | solution.py:479
  1.7 1.5 %collective-permute-start = (bf16[2,128,512]{2,1,0:T(8,128)(2,1)S(1)}, bf16[2,128,512]{2,1,0:T(8,128)(2,1)S(1)}, u32[]{:S(2)}, u32[]{:S(2)}) collective-permute-start(bf16[2,128,512]{2,1,0:T(8,128)(2,1)S(1)} %get-tuple-element.55), channel_id=1, source_target_pairs={{0,2},{2,0},{4,6},{6,4},{8,10},{10,8},{12,14},{14,12},{16,18},{18,... | collective-permute-start | bytes 786440 | tf_op jit(solution)/shard_map/ppermute | solution.py:63
  3.2 1.4 %collective-permute-start.1 = (bf16[64,3072]{1,0:T(8,128)(2,1)}, bf16[64,3072]{1,0:T(8,128)(2,1)S(1)}, u32[]{:S(2)}, u32[]{:S(2)}) collective-permute-start(bf16[64,3072]{1,0:T(8,128)(2,1)} %refs_1_.2), channel_id=1, source_target_pairs={{0,1},{1,0},{2,3},{3,2},{4,5},{5,4},{6,7},{7,6},{8,9},{9,8},{10,11... | collective-permute-start | bytes 1179656 | tf_op jit(solution)/shard_map/ppermute | solution.py:67
  5.3 1.7 %collective-permute-start.3 = (bf16[2,256,512]{2,1,0:T(8,128)(2,1)S(1)}, bf16[2,256,512]{2,1,0:T(8,128)(2,1)S(1)}, u32[]{:S(2)}, u32[]{:S(2)}) collective-permute-start(bf16[2,256,512]{2,1,0:T(8,128)(2,1)S(1)} %pad_maximum_fusion.refs_4_.refs_6_), channel_id=1, source_target_pairs={{0,32},{2,6},{4,36},{6,10},{8,40},{10,14},{12,44},{14,2},{16,48},{... | collective-permute-start | bytes 1572872 | tf_op jit(solution)/shard_map/ppermute | solution.py:63
  7.0 2.2 %collective-permute-start.4 = (bf16[2,256,512]{2,1,0:T(8,128)(2,1)S(1)}, bf16[2,256,512]{2,1,0:T(8,128)(2,1)S(1)}, u32[]{:S(2)}, u32[]{:S(2)}) collective-permute-start(bf16[2,256,512]{2,1,0:T(8,128)(2,1)S(1)} %pad_maximum_fusion.refs_4_.refs_6_), channel_id=1, source_target_pairs={{0,96},{2,14},{4,100},{6,2},{8,104},{10,6},{12,108},{14,10},{16,11... | collective-permute-start | bytes 1572872 | tf_op jit(solution)/shard_map/ppermute | solution.py:63
  9.3 1.3 %collective-permute-start.8 = (bf16[2,256,512]{2,1,0:T(8,128)(2,1)S(1)}, bf16[2,256,512]{2,1,0:T(8,128)(2,1)S(1)}, u32[]{:S(2)}, u32[]{:S(2)}) collective-permute-start(bf16[2,256,512]{2,1,0:T(8,128)(2,1)S(1)} %pad_maximum_fusion.refs_4_.refs_6_), channel_id=1, source_target_pairs={{0,64},{2,10},{4,68},{6,14},{8,72},{10,2},{12,76},{14,6},{16,80},{... | collective-permute-start | bytes 1572872 | tf_op jit(solution)/shard_map/ppermute | solution.py:63
  10.6 2.6 %collective-permute-start.9 = (bf16[2,256,512]{2,1,0:T(8,128)(2,1)S(1)}, bf16[2,256,512]{2,1,0:T(8,128)(2,1)S(1)}, u32[]{:S(2)}, u32[]{:S(2)}) collective-permute-start(bf16[2,256,512]{2,1,0:T(8,128)(2,1)S(1)} %pad_maximum_fusion.refs_4_.refs_6_), channel_id=1, source_target_pairs={{0,16},{2,18},{4,20},{6,22},{8,24},{10,26},{12,28},{14,30},{16,0},... | collective-permute-start | bytes 1572872 | tf_op jit(solution)/shard_map/ppermute | solution.py:63
  13.2 1.0 %fusion = (f32[1,128,128]{2,1,0:T(8,128)S(1)}, f32[1,128,128]{2,1,0:T(8,128)S(1)}) fusion(f32[128]{0:T(128)} %constant.65.clone, f32[128]{0:T(128)S(1)} %get-tuple-element.58, f32[128]{0:T(128)} %constant.64.clone, f32[128]{0:T(128)S(1)} %get-tuple-element.59, f32[128]{0:T(128)} %constant.66.clone), kind=kLoop, calls=%fused_computation.4 | loop fusion | flops 65536 | bytes 133632 | tf_op jit(solution)/shard_map/cos | solution.py:490
  14.2 2.9 %stage.1 = (bf16[1,3072,896]{2,1,0:T(8,128)(2,1)S(1)}, bf16[64,3072]{1,0:T(8,128)(2,1)S(1)}, f32[4,128,128]{2,1,0:T(8,128)S(1)}) custom-call(bf16[3,3072,896]{2,1,0:T(8,128)(2,1)} %bitcast.7, bf16[64,3072]{1,0:T(8,128)(2,1)} %refs_1_.2, f32[2,128]{1,0:T(2,128)} %refs_2_.1, f32[2,128,128]{2,1,0:T(8,128)S(1)} %pad_maximum_fusion.1.refs_3_, ...), custom_call_target="tpu_custom_call" | custom-call | flops 1 | bytes 1 | tf_op jit(solution)/shard_map/stage/pallas_call | solution.py:78
  17.1 1.3 %query_projection.1 = (bf16[4,128,128]{2,1,0:T(8,128)(2,1)S(1)}, bf16[3,128,128]{2,1,0:T(8,128)(2,1)S(1)}, bf16[7,128,128]{2,1,0:T(8,128)(2,1)S(1)}, bf16[128,3072]{1,0:T(8,128)(2,1)S(1)}) custom-call(s32[1]{0:T(128)} %bitcast.refs_0_, s32[1]{0:T(128)} %bitcast.1.refs_1_, bf16[1,3072,896]{2,1,0:T(8,128)(2,1)S(1)} %get-tuple-element.28.refs_2_, ...), custom_call_target="tpu_custom_call" | custom-call | flops 1 | bytes 1 | tf_op jit(solution)/shard_map/query_projection/pallas_call | solution.py:78
  19.1 0.9 %collective-permute-done.2.refs_1_ = bf16[3,128,128]{2,1,0:T(8,128)(2,1)S(1)} collective-permute-done((bf16[3,128,128]{2,1,0:T(8,128)(2,1)S(1)}, bf16[3,128,128]{2,1,0:T(8,128)(2,1)S(1)}, u32[]{:S(2)}, u32[]{:S(2)}) %collective-permute-start.2) | collective-permute-done | bytes 98336 | tf_op jit(solution)/shard_map/ppermute | solution.py:63
  20.1 0.9 %collective-permute-done.4.refs_3_.refs_8_ = bf16[2,256,512]{2,1,0:T(8,128)(2,1)S(1)} collective-permute-done((bf16[2,256,512]{2,1,0:T(8,128)(2,1)S(1)}, bf16[2,256,512]{2,1,0:T(8,128)(2,1)S(1)}, u32[]{:S(2)}, u32[]{:S(2)}) %collective-permute-start.4) | collective-permute-done | bytes 524320 | tf_op jit(solution)/shard_map/ppermute | solution.py:63
  21.0 1.3 %collective-permute-start.5 = (bf16[7,128,128]{2,1,0:T(8,128)(2,1)S(1)}, bf16[7,128,128]{2,1,0:T(8,128)(2,1)S(1)}, u32[]{:S(2)}, u32[]{:S(2)}) collective-permute-start(bf16[7,128,128]{2,1,0:T(8,128)(2,1)S(1)} %join_units.1.refs_5_.refs_2_), channel_id=1, source_target_pairs={{0,4},{2,34},{4,8},{6,38},{8,12},{10,42},{12,0},{14,46},{16,20},{1... | collective-permute-start | bytes 688136 | tf_op jit(solution)/shard_map/ppermute | solution.py:63
  22.3 1.5 %collective-permute-start.6 = (bf16[7,128,128]{2,1,0:T(8,128)(2,1)S(1)}, bf16[7,128,128]{2,1,0:T(8,128)(2,1)S(1)}, u32[]{:S(2)}, u32[]{:S(2)}) collective-permute-start(bf16[7,128,128]{2,1,0:T(8,128)(2,1)S(1)} %join_units.1.refs_5_.refs_2_), channel_id=1, source_target_pairs={{0,12},{2,98},{4,0},{6,102},{8,4},{10,106},{12,8},{14,110},{16,28}... | collective-permute-start | bytes 688136 | tf_op jit(solution)/shard_map/ppermute | solution.py:63
  23.7 1.5 %collective-permute-start.7 = (bf16[7,128,128]{2,1,0:T(8,128)(2,1)S(1)}, bf16[7,128,128]{2,1,0:T(8,128)(2,1)S(1)}, u32[]{:S(2)}, u32[]{:S(2)}) collective-permute-start(bf16[7,128,128]{2,1,0:T(8,128)(2,1)S(1)} %join_units.1.refs_5_.refs_2_), channel_id=1, source_target_pairs={{0,8},{2,66},{4,12},{6,70},{8,0},{10,74},{12,4},{14,78},{16,24},{1... | collective-permute-start | bytes 688136 | tf_op jit(solution)/shard_map/ppermute | solution.py:63
  25.3 2.6 %collective-permute-start.12 = (bf16[2,256,512]{2,1,0:T(8,128)(2,1)S(1)}, bf16[2,256,512]{2,1,0:T(8,128)(2,1)S(1)}, u32[]{:S(2)}, u32[]{:S(2)}) collective-permute-start(bf16[2,256,512]{2,1,0:T(8,128)(2,1)S(1)} %collective-permute-done.8.refs_6_.refs_9_), channel_id=1, source_target_pairs={{0,16},{2,18},{4,20},{6,22},{8,24},{10,26},{12,28},{14,30},{16,0},... | collective-permute-start | bytes 1572872 | tf_op jit(solution)/shard_map/ppermute | solution.py:63
  27.9 2.7 %key_value_projection.1 = (bf16[2,128,896]{2,1,0:T(8,128)(2,1)}, bf16[2,128,896]{2,1,0:T(8,128)(2,1)S(1)}) custom-call(s32[1]{0:T(128)} %bitcast.refs_0_, s32[1]{0:T(128)} %bitcast.1.refs_1_, bf16[3,3072,896]{2,1,0:T(8,128)(2,1)S(1)} %bitcast.8, bf16[128,3072]{1,0:T(8,128)(2,1)S(1)} %get-tuple-element.34.refs_3_, ...), custom_call_target="tpu_custom_call" | custom-call | flops 1 | bytes 1 | tf_op jit(solution)/shard_map/key_value_projection/pallas_call | solution.py:78
  30.9 3.4 %collective-permute-start.11 = (bf16[2,256,512]{2,1,0:T(8,128)(2,1)S(1)}, bf16[2,256,512]{2,1,0:T(8,128)(2,1)S(1)}, u32[]{:S(2)}, u32[]{:S(2)}) collective-permute-start(bf16[2,256,512]{2,1,0:T(8,128)(2,1)S(1)} %gate.1.refs_4_.refs_8_), channel_id=1, source_target_pairs={{0,96},{2,14},{4,100},{6,2},{8,104},{10,6},{12,108},{14,10},{16,11... | collective-permute-start | bytes 1572872 | tf_op jit(solution)/shard_map/ppermute | solution.py:63
  35.0 1.2 %home_attention.1 = (bf16[7,128,128]{2,1,0:T(8,128)(2,1)S(1)}, f32[128,128]{1,0:T(8,128)S(1)}) custom-call(s32[1]{0:T(128)S(6)} %copy.15.refs_0_, bf16[2,512,896]{2,1,0:T(8,128)(2,1)S(1)} %copy-done.1, bf16[7,128,128]{2,1,0:T(8,128)(2,1)S(1)} %get-tuple-element.33.refs_2_, bf16[2,128,896]{2,1,0:T(8,128)(2,1)S(1)} %get-tuple-element.35.refs_3_, ...), custom_call_target="tpu_custom_call" | custom-call | flops 1 | bytes 1 | tf_op jit(solution)/shard_map/home_attention/pallas_call | solution.py:78
  36.2 4.7 %near_attention.1 = (f32[7,512,128]{2,1,0:T(8,128)S(1)}, f32[512,128]{1,0:T(8,128)S(1)}) custom-call(s32[1]{0:T(128)} %bitcast.refs_0_, s32[1]{0:T(128)} %bitcast.1.refs_1_, bf16[7,128,128]{2,1,0:T(8,128)(2,1)S(1)} %join_units.1.refs_5_.refs_2_, bf16[7,128,128]{2,1,0:T(8,128)(2,1)S(1)} %collective-permute-done.5.refs_0_.refs_3_, ...), custom_call_target="tpu_custom_call" | custom-call | flops 1 | bytes 1 | tf_op jit(solution)/shard_map/near_attention/pallas_call | solution.py:78
  41.2 2.7 %far_attention_0.1 = (bf16[8,64,128]{2,1,0:T(8,128)(2,1)S(1)}, bf16[8,64,128]{2,1,0:T(8,128)(2,1)S(1)}, bf16[8,64,128]{2,1,0:T(8,128)(2,1)S(1)}) custom-call(s32[1]{0:T(128)} %bitcast.refs_0_, s32[1]{0:T(128)} %bitcast.1.refs_1_, bf16[7,128,128]{2,1,0:T(8,128)(2,1)S(1)} %join_units.1.refs_5_.refs_2_, ...), custom_call_target="tpu_custom_call" | custom-call | flops 1 | bytes 1 | tf_op jit(solution)/shard_map/far_attention_0/pallas_call | solution.py:78
  43.8 1.8 %collective-permute-start.17 = (bf16[8,64,128]{2,1,0:T(8,128)(2,1)S(1)}, bf16[8,64,128]{2,1,0:T(8,128)(2,1)S(1)}, u32[]{:S(2)}, u32[]{:S(2)}) collective-permute-start(bf16[8,64,128]{2,1,0:T(8,128)(2,1)S(1)} %get-tuple-element.47), channel_id=1, source_target_pairs={{0,12},{2,98},{4,0},{6,102},{8,4},{10,106},{12,8},{14,110},{16,28}... | collective-permute-start | bytes 393224 | tf_op jit(solution)/shard_map/ppermute | solution.py:63
  45.6 1.3 %collective-permute-start.19 = (bf16[8,64,128]{2,1,0:T(8,128)(2,1)S(1)}, bf16[8,64,128]{2,1,0:T(8,128)(2,1)S(1)}, u32[]{:S(2)}, u32[]{:S(2)}) collective-permute-start(bf16[8,64,128]{2,1,0:T(8,128)(2,1)S(1)} %get-tuple-element.49), channel_id=1, source_target_pairs={{0,8},{2,66},{4,12},{6,70},{8,0},{10,74},{12,4},{14,78},{16,24},{1... | collective-permute-start | bytes 393224 | tf_op jit(solution)/shard_map/ppermute | solution.py:63
  46.9 4.1 %far_attention_1.1 = (bf16[8,128,128]{2,1,0:T(8,128)(2,1)S(1)}, bf16[8,64,128]{2,1,0:T(8,128)(2,1)S(1)}, bf16[8,64,128]{2,1,0:T(8,128)(2,1)S(1)}, bf16[8,64,128]{2,1,0:T(8,128)(2,1)S(1)}) custom-call(s32[1]{0:T(128)} %bitcast.refs_0_, s32[1]{0:T(128)} %bitcast.1.refs_1_, bf16[7,128,128]{2,1,0:T(8,128)(2,1)S(1)} %join_units.1.refs_5_.refs_2_, ...), custom_call_target="tpu_custom_call" | custom-call | flops 1 | bytes 1 | tf_op jit(solution)/shard_map/far_attention_1/pallas_call | solution.py:78
  51.0 1.1 %collective-permute-done.18.refs_2_ = bf16[8,64,128]{2,1,0:T(8,128)(2,1)S(1)} collective-permute-done((bf16[8,64,128]{2,1,0:T(8,128)(2,1)S(1)}, bf16[8,64,128]{2,1,0:T(8,128)(2,1)S(1)}, u32[]{:S(2)}, u32[]{:S(2)}) %collective-permute-start.18) | collective-permute-done | bytes 131104 | tf_op jit(solution)/shard_map/ppermute | solution.py:63
  52.6 4.4 %collective-permute-start.20 = (bf16[4,64,128]{2,1,0:T(8,128)(2,1)S(1)}, bf16[4,64,128]{2,1,0:T(8,128)(2,1)S(1)}, u32[]{:S(2)}, u32[]{:S(2)}) collective-permute-start(bf16[4,64,128]{2,1,0:T(8,128)(2,1)S(1)} %get-tuple-element.52), channel_id=1, source_target_pairs={{0,2},{2,0},{4,6},{6,4},{8,10},{10,8},{12,14},{14,12},{16,18},{18,... | collective-permute-start | bytes 196616 | tf_op jit(solution)/shard_map/ppermute | solution.py:63
  56.9 0.8 %output_projection_mine.3.refs_2_ = f32[64,3072]{1,0:T(8,128)S(1)} custom-call(s32[1]{0:T(128)} %bitcast.refs_0_, s32[1]{0:T(128)} %bitcast.1.refs_1_, bf16[4,64,128]{2,1,0:T(8,128)(2,1)S(1)} %get-tuple-element.50.refs_2_, f32[64,128]{1,0:T(8,128)S(1)} %get-tuple-element.51.refs_3_, bf16[7,128,128]{2,1,0:T(8,128)(2,1)S(1)} %get-tuple-element.36.refs_10_.refs_4_, ...), custom_call_target="tpu_custom_call" | custom-call | flops 1 | bytes 1 | tf_op jit(solution)/shard_map/output_projection_mine/pallas_call | solution.py:78
  59.1 3.2 %collective-permute-start.13 = (bf16[8,64,128]{2,1,0:T(8,128)(2,1)S(1)}, bf16[8,64,128]{2,1,0:T(8,128)(2,1)S(1)}, u32[]{:S(2)}, u32[]{:S(2)}) collective-permute-start(bf16[8,64,128]{2,1,0:T(8,128)(2,1)S(1)} %get-tuple-element.40), channel_id=1, source_target_pairs={{0,12},{2,98},{4,0},{6,102},{8,4},{10,106},{12,8},{14,110},{16,28}... | collective-permute-start | bytes 393224 | tf_op jit(solution)/shard_map/ppermute | solution.py:63
  62.3 1.5 %collective-permute-start.15 = (bf16[8,64,128]{2,1,0:T(8,128)(2,1)S(1)}, bf16[8,64,128]{2,1,0:T(8,128)(2,1)S(1)}, u32[]{:S(2)}, u32[]{:S(2)}) collective-permute-start(bf16[8,64,128]{2,1,0:T(8,128)(2,1)S(1)} %get-tuple-element.42), channel_id=1, source_target_pairs={{0,8},{2,66},{4,12},{6,70},{8,0},{10,74},{12,4},{14,78},{16,24},{1... | collective-permute-start | bytes 393224 | tf_op jit(solution)/shard_map/ppermute | solution.py:63
  64.2 4.8 %collective-permute-done.14.refs_2_ = bf16[8,64,128]{2,1,0:T(8,128)(2,1)S(1)} collective-permute-done((bf16[8,64,128]{2,1,0:T(8,128)(2,1)S(1)}, bf16[8,64,128]{2,1,0:T(8,128)(2,1)S(1)}, u32[]{:S(2)}, u32[]{:S(2)}) %collective-permute-start.14) | collective-permute-done | bytes 131104 | tf_op jit(solution)/shard_map/ppermute | solution.py:63
  70.0 0.8 %output_projection_mine.2.refs_2_ = f32[64,3072]{1,0:T(8,128)S(1)} custom-call(s32[1]{0:T(128)} %bitcast.refs_0_, s32[1]{0:T(128)} %bitcast.1.refs_1_, bf16[4,64,128]{2,1,0:T(8,128)(2,1)S(1)} %get-tuple-element.43.refs_2_, f32[64,128]{1,0:T(8,128)S(1)} %get-tuple-element.44.refs_3_, bf16[7,128,128]{2,1,0:T(8,128)(2,1)S(1)} %get-tuple-element.36.refs_10_.refs_4_, ...), custom_call_target="tpu_custom_call" | custom-call | flops 1 | bytes 1 | tf_op jit(solution)/shard_map/output_projection_mine/pallas_call | solution.py:78
  70.9 1.5 %output_projection_got.3 = bf16[64,3072]{1,0:T(8,128)(2,1)} custom-call(s32[1]{0:T(128)} %bitcast.refs_0_, s32[1]{0:T(128)} %bitcast.1.refs_1_, f32[64,3072]{1,0:T(8,128)S(1)} %output_projection_mine.2.refs_2_, bf16[4,64,128]{2,1,0:T(8,128)(2,1)S(1)} %collective-permute-done.16.refs_3_, bf16[7,128,128]{2,1,0:T(8,128)(2,1)S(1)} %get-tuple-element.36.refs_10_.refs_4_, ...), custom_call_target="tpu_custom_call" | custom-call | flops 1 | bytes 1 | tf_op jit(solution)/shard_map/output_projection_got/pallas_call | solution.py:78
  (41 shorter events, 4.7 us)
Async XLA Ops:
  1.7 3.6 %collective-permute-start = (bf16[2,128,512]{2,1,0:T(8,128)(2,1)S(1)}, bf16[2,128,512]{2,1,0:T(8,128)(2,1)S(1)}, u32[]{:S(2)}, u32[]{:S(2)}) collective-permute-start(bf16[2,128,512]{2,1,0:T(8,128)(2,1)S(1)} %get-tuple-element.55), channel_id=1, source_target_pairs={{0,2},{2,0},{4,6},{6,4},{8,10},{10,8},{12,14},{14,12},{16,18},{18,... | collective-permute-start | bytes 786440 | tf_op jit(solution)/shard_map/ppermute | solution.py:63
  3.2 13.9 %collective-permute-start.1 = (bf16[64,3072]{1,0:T(8,128)(2,1)}, bf16[64,3072]{1,0:T(8,128)(2,1)S(1)}, u32[]{:S(2)}, u32[]{:S(2)}) collective-permute-start(bf16[64,3072]{1,0:T(8,128)(2,1)} %refs_1_.2), channel_id=1, source_target_pairs={{0,1},{1,0},{2,3},{3,2},{4,5},{5,4},{6,7},{7,6},{8,9},{9,8},{10,11... | collective-permute-start | bytes 1179656 | tf_op jit(solution)/shard_map/ppermute | solution.py:67
  5.3 14.7 %collective-permute-start.3 = (bf16[2,256,512]{2,1,0:T(8,128)(2,1)S(1)}, bf16[2,256,512]{2,1,0:T(8,128)(2,1)S(1)}, u32[]{:S(2)}, u32[]{:S(2)}) collective-permute-start(bf16[2,256,512]{2,1,0:T(8,128)(2,1)S(1)} %pad_maximum_fusion.refs_4_.refs_6_), channel_id=1, source_target_pairs={{0,32},{2,6},{4,36},{6,10},{8,40},{10,14},{12,44},{14,2},{16,48},{... | collective-permute-start | bytes 1572872 | tf_op jit(solution)/shard_map/ppermute | solution.py:63
  7.0 13.9 %collective-permute-start.4 = (bf16[2,256,512]{2,1,0:T(8,128)(2,1)S(1)}, bf16[2,256,512]{2,1,0:T(8,128)(2,1)S(1)}, u32[]{:S(2)}, u32[]{:S(2)}) collective-permute-start(bf16[2,256,512]{2,1,0:T(8,128)(2,1)S(1)} %pad_maximum_fusion.refs_4_.refs_6_), channel_id=1, source_target_pairs={{0,96},{2,14},{4,100},{6,2},{8,104},{10,6},{12,108},{14,10},{16,11... | collective-permute-start | bytes 1572872 | tf_op jit(solution)/shard_map/ppermute | solution.py:63
  9.3 16.0 %collective-permute-start.8 = (bf16[2,256,512]{2,1,0:T(8,128)(2,1)S(1)}, bf16[2,256,512]{2,1,0:T(8,128)(2,1)S(1)}, u32[]{:S(2)}, u32[]{:S(2)}) collective-permute-start(bf16[2,256,512]{2,1,0:T(8,128)(2,1)S(1)} %pad_maximum_fusion.refs_4_.refs_6_), channel_id=1, source_target_pairs={{0,64},{2,10},{4,68},{6,14},{8,72},{10,2},{12,76},{14,6},{16,80},{... | collective-permute-start | bytes 1572872 | tf_op jit(solution)/shard_map/ppermute | solution.py:63
  10.6 20.1 %collective-permute-start.9 = (bf16[2,256,512]{2,1,0:T(8,128)(2,1)S(1)}, bf16[2,256,512]{2,1,0:T(8,128)(2,1)S(1)}, u32[]{:S(2)}, u32[]{:S(2)}) collective-permute-start(bf16[2,256,512]{2,1,0:T(8,128)(2,1)S(1)} %pad_maximum_fusion.refs_4_.refs_6_), channel_id=1, source_target_pairs={{0,16},{2,18},{4,20},{6,22},{8,24},{10,26},{12,28},{14,30},{16,0},... | collective-permute-start | bytes 1572872 | tf_op jit(solution)/shard_map/ppermute | solution.py:63
  14.2 13.7 %copy-start = (bf16[3072,3,896]{2,0,1:T(8,128)(2,1)S(1)}, bf16[3072,3,896]{2,0,1:T(8,128)(2,1)}, u32[]{:S(2)}) copy-start(bf16[3072,3,896]{2,0,1:T(8,128)(2,1)} %param.12) | copy-start | bytes 49545220
  18.4 1.6 %collective-permute-start.2 = (bf16[3,128,128]{2,1,0:T(8,128)(2,1)S(1)}, bf16[3,128,128]{2,1,0:T(8,128)(2,1)S(1)}, u32[]{:S(2)}, u32[]{:S(2)}) collective-permute-start(bf16[3,128,128]{2,1,0:T(8,128)(2,1)S(1)} %get-tuple-element.32), channel_id=1, source_target_pairs={{0,2},{2,0},{4,6},{6,4},{8,10},{10,8},{12,14},{14,12},{16,18},{18,... | collective-permute-start | bytes 294920 | tf_op jit(solution)/shard_map/ppermute | solution.py:63
  21.0 9.6 %collective-permute-start.5 = (bf16[7,128,128]{2,1,0:T(8,128)(2,1)S(1)}, bf16[7,128,128]{2,1,0:T(8,128)(2,1)S(1)}, u32[]{:S(2)}, u32[]{:S(2)}) collective-permute-start(bf16[7,128,128]{2,1,0:T(8,128)(2,1)S(1)} %join_units.1.refs_5_.refs_2_), channel_id=1, source_target_pairs={{0,4},{2,34},{4,8},{6,38},{8,12},{10,42},{12,0},{14,46},{16,20},{1... | collective-permute-start | bytes 688136 | tf_op jit(solution)/shard_map/ppermute | solution.py:63
  22.3 8.3 %collective-permute-start.6 = (bf16[7,128,128]{2,1,0:T(8,128)(2,1)S(1)}, bf16[7,128,128]{2,1,0:T(8,128)(2,1)S(1)}, u32[]{:S(2)}, u32[]{:S(2)}) collective-permute-start(bf16[7,128,128]{2,1,0:T(8,128)(2,1)S(1)} %join_units.1.refs_5_.refs_2_), channel_id=1, source_target_pairs={{0,12},{2,98},{4,0},{6,102},{8,4},{10,106},{12,8},{14,110},{16,28}... | collective-permute-start | bytes 688136 | tf_op jit(solution)/shard_map/ppermute | solution.py:63
  23.7 7.1 %collective-permute-start.7 = (bf16[7,128,128]{2,1,0:T(8,128)(2,1)S(1)}, bf16[7,128,128]{2,1,0:T(8,128)(2,1)S(1)}, u32[]{:S(2)}, u32[]{:S(2)}) collective-permute-start(bf16[7,128,128]{2,1,0:T(8,128)(2,1)S(1)} %join_units.1.refs_5_.refs_2_), channel_id=1, source_target_pairs={{0,8},{2,66},{4,12},{6,70},{8,0},{10,74},{12,4},{14,78},{16,24},{1... | collective-permute-start | bytes 688136 | tf_op jit(solution)/shard_map/ppermute | solution.py:63
  25.3 15.6 %collective-permute-start.12 = (bf16[2,256,512]{2,1,0:T(8,128)(2,1)S(1)}, bf16[2,256,512]{2,1,0:T(8,128)(2,1)S(1)}, u32[]{:S(2)}, u32[]{:S(2)}) collective-permute-start(bf16[2,256,512]{2,1,0:T(8,128)(2,1)S(1)} %collective-permute-done.8.refs_6_.refs_9_), channel_id=1, source_target_pairs={{0,16},{2,18},{4,20},{6,22},{8,24},{10,26},{12,28},{14,30},{16,0},... | collective-permute-start | bytes 1572872 | tf_op jit(solution)/shard_map/ppermute | solution.py:63
  27.9 7.1 %copy-start.1 = (bf16[2,512,896]{2,1,0:T(8,128)(2,1)S(1)}, bf16[2,512,896]{2,1,0:T(8,128)(2,1)}, u32[]{:S(2)}) copy-start(bf16[2,512,896]{2,1,0:T(8,128)(2,1)} %refs_1_.3) | copy-start | bytes 5505028
  30.9 10.3 %collective-permute-start.10 = (bf16[2,256,512]{2,1,0:T(8,128)(2,1)S(1)}, bf16[2,256,512]{2,1,0:T(8,128)(2,1)S(1)}, u32[]{:S(2)}, u32[]{:S(2)}) collective-permute-start(bf16[2,256,512]{2,1,0:T(8,128)(2,1)S(1)} %gate.1.refs_4_.refs_8_), channel_id=1, source_target_pairs={{0,32},{2,6},{4,36},{6,10},{8,40},{10,14},{12,44},{14,2},{16,48},{... | collective-permute-start | bytes 1572872 | tf_op jit(solution)/shard_map/ppermute | solution.py:63
  30.9 10.3 %collective-permute-start.11 = (bf16[2,256,512]{2,1,0:T(8,128)(2,1)S(1)}, bf16[2,256,512]{2,1,0:T(8,128)(2,1)S(1)}, u32[]{:S(2)}, u32[]{:S(2)}) collective-permute-start(bf16[2,256,512]{2,1,0:T(8,128)(2,1)S(1)} %gate.1.refs_4_.refs_8_), channel_id=1, source_target_pairs={{0,96},{2,14},{4,100},{6,2},{8,104},{10,6},{12,108},{14,10},{16,11... | collective-permute-start | bytes 1572872 | tf_op jit(solution)/shard_map/ppermute | solution.py:63
  36.2 20.8 %slice-start = ((s8[5505024]{0:T(1024)(128)(4,1)}), s8[4194304]{0:T(1024)(128)(4,1)S(1)}, s32[]{:S(2)}) async-start(s8[5505024]{0:T(1024)(128)(4,1)} %bitcast.5), calls=%async_computation | async-start | bytes 8388608
  41.2 15.8 %slice-start.1 = ((s8[5505024]{0:T(1024)(128)(4,1)}), s8[1310720]{0:T(1024)(128)(4,1)S(1)}, s32[]{:S(2)}) async-start(s8[5505024]{0:T(1024)(128)(4,1)} %bitcast.5), calls=%async_computation.1 | async-start | bytes 2621440
  43.8 7.1 %collective-permute-start.17 = (bf16[8,64,128]{2,1,0:T(8,128)(2,1)S(1)}, bf16[8,64,128]{2,1,0:T(8,128)(2,1)S(1)}, u32[]{:S(2)}, u32[]{:S(2)}) collective-permute-start(bf16[8,64,128]{2,1,0:T(8,128)(2,1)S(1)} %get-tuple-element.47), channel_id=1, source_target_pairs={{0,12},{2,98},{4,0},{6,102},{8,4},{10,106},{12,8},{14,110},{16,28}... | collective-permute-start | bytes 393224 | tf_op jit(solution)/shard_map/ppermute | solution.py:63
  45.6 6.4 %collective-permute-start.18 = (bf16[8,64,128]{2,1,0:T(8,128)(2,1)S(1)}, bf16[8,64,128]{2,1,0:T(8,128)(2,1)S(1)}, u32[]{:S(2)}, u32[]{:S(2)}) collective-permute-start(bf16[8,64,128]{2,1,0:T(8,128)(2,1)S(1)} %get-tuple-element.48), channel_id=1, source_target_pairs={{0,4},{2,34},{4,8},{6,38},{8,12},{10,42},{12,0},{14,46},{16,20},{1... | collective-permute-start | bytes 393224 | tf_op jit(solution)/shard_map/ppermute | solution.py:63
  45.6 6.4 %collective-permute-start.19 = (bf16[8,64,128]{2,1,0:T(8,128)(2,1)S(1)}, bf16[8,64,128]{2,1,0:T(8,128)(2,1)S(1)}, u32[]{:S(2)}, u32[]{:S(2)}) collective-permute-start(bf16[8,64,128]{2,1,0:T(8,128)(2,1)S(1)} %get-tuple-element.49), channel_id=1, source_target_pairs={{0,8},{2,66},{4,12},{6,70},{8,0},{10,74},{12,4},{14,78},{16,24},{1... | collective-permute-start | bytes 393224 | tf_op jit(solution)/shard_map/ppermute | solution.py:63
  52.6 5.3 %collective-permute-start.20 = (bf16[4,64,128]{2,1,0:T(8,128)(2,1)S(1)}, bf16[4,64,128]{2,1,0:T(8,128)(2,1)S(1)}, u32[]{:S(2)}, u32[]{:S(2)}) collective-permute-start(bf16[4,64,128]{2,1,0:T(8,128)(2,1)S(1)} %get-tuple-element.52), channel_id=1, source_target_pairs={{0,2},{2,0},{4,6},{6,4},{8,10},{10,8},{12,14},{14,12},{16,18},{18,... | collective-permute-start | bytes 196616 | tf_op jit(solution)/shard_map/ppermute | solution.py:63
  58.5 12.4 %collective-permute-start.21 = (bf16[64,3072]{1,0:T(8,128)(2,1)S(1)}, bf16[64,3072]{1,0:T(8,128)(2,1)S(1)}, u32[]{:S(2)}, u32[]{:S(2)}) collective-permute-start(bf16[64,3072]{1,0:T(8,128)(2,1)S(1)} %output_projection_got.2), channel_id=1, source_target_pairs={{0,1},{1,0},{2,3},{3,2},{4,5},{5,4},{6,7},{7,6},{8,9},{9,8},{10,11... | collective-permute-start | bytes 1179656 | tf_op jit(solution)/shard_map/ppermute | solution.py:67
  59.1 5.1 %collective-permute-start.13 = (bf16[8,64,128]{2,1,0:T(8,128)(2,1)S(1)}, bf16[8,64,128]{2,1,0:T(8,128)(2,1)S(1)}, u32[]{:S(2)}, u32[]{:S(2)}) collective-permute-start(bf16[8,64,128]{2,1,0:T(8,128)(2,1)S(1)} %get-tuple-element.40), channel_id=1, source_target_pairs={{0,12},{2,98},{4,0},{6,102},{8,4},{10,106},{12,8},{14,110},{16,28}... | collective-permute-start | bytes 393224 | tf_op jit(solution)/shard_map/ppermute | solution.py:63
  62.3 6.7 %collective-permute-start.14 = (bf16[8,64,128]{2,1,0:T(8,128)(2,1)S(1)}, bf16[8,64,128]{2,1,0:T(8,128)(2,1)S(1)}, u32[]{:S(2)}, u32[]{:S(2)}) collective-permute-start(bf16[8,64,128]{2,1,0:T(8,128)(2,1)S(1)} %get-tuple-element.41), channel_id=1, source_target_pairs={{0,4},{2,34},{4,8},{6,38},{8,12},{10,42},{12,0},{14,46},{16,20},{1... | collective-permute-start | bytes 393224 | tf_op jit(solution)/shard_map/ppermute | solution.py:63
  62.3 6.7 %collective-permute-start.15 = (bf16[8,64,128]{2,1,0:T(8,128)(2,1)S(1)}, bf16[8,64,128]{2,1,0:T(8,128)(2,1)S(1)}, u32[]{:S(2)}, u32[]{:S(2)}) collective-permute-start(bf16[8,64,128]{2,1,0:T(8,128)(2,1)S(1)} %get-tuple-element.42), channel_id=1, source_target_pairs={{0,8},{2,66},{4,12},{6,70},{8,0},{10,74},{12,4},{14,78},{16,24},{1... | collective-permute-start | bytes 393224 | tf_op jit(solution)/shard_map/ppermute | solution.py:63
  69.5 1.4 %collective-permute-start.16 = (bf16[4,64,128]{2,1,0:T(8,128)(2,1)S(1)}, bf16[4,64,128]{2,1,0:T(8,128)(2,1)S(1)}, u32[]{:S(2)}, u32[]{:S(2)}) collective-permute-start(bf16[4,64,128]{2,1,0:T(8,128)(2,1)S(1)} %get-tuple-element.46), channel_id=1, source_target_pairs={{0,2},{2,0},{4,6},{6,4},{8,10},{10,8},{12,14},{14,12},{16,18},{18,... | collective-permute-start | bytes 196616 | tf_op jit(solution)/shard_map/ppermute | solution.py:63

commit v7 on v6

--- a/solution.py
+++ b/solution.py
@@ -503,7 +503,8 @@
 
     first = attend_far(0, place, queries, acc, stat, far, [])
     own, *second = attend_far(1, place, queries, acc, stat, far, [])
-    back = [[own] + [move(p, _query_move(d)) for p, d in zip(parts, (3, 1, 2))] for parts in (first, second)]
+    back = [[own] + [move(p, _query_move(d)) for p, d in zip(first, (3, 1, 2))]]
+    back.append([own] + [move(second[i], _query_move(d)) for i, d in ((2, 2), (0, 3), (1, 1))])
     merged = [merge(g, back[g]) for g in (0, 1)]
     got = [move(merged[g][2], _core_move) for g in (0, 1)]
     sent = project_out(0, place, *merged[0][:2], got[0], home, level, w_out)

time: 72.5 us -> 72.2 us (level)
  waiting for transfers between devices: 8.96 us -> 7.89 us
  starting transfers between devices: 34.9 us -> 35.7 us
    ppermute x20, waiting for transfers between devices: 8.96 us -> 7.89 us  [move(): return lax.ppermute(array, 'patch', _perm(how))]
    ppermute x20, starting transfers between devices: 33 us -> 33.7 us  [move(): return lax.ppermute(array, 'patch', _perm(how))]
  transfers between devices with their start and end apart: 22 -> 22, of which waited for: 9 -> 10; matrix products, arithmetic and copies ran while one was open for 1% -> 1% of each run, Pallas kernels for 26% -> 26%
where the time goes in v7:
time: 72.2 us; the launch traced here: 72.1 us
  starting transfers between devices  35.7 us (49%)
  Pallas kernels  24.2 us (34%)
  waiting for transfers between devices  7.89 us (11%)
  between operations  2.14 us (3%)
  local copies, waits for them, and re-layouts  1.09 us (2%)
  other arithmetic  1.07 us (1%)
    ppermute x20, starting transfers between devices, move(): return lax.ppermute(array, 'patch', _perm(how))  33.7 us
    pallas_call x14, Pallas kernels, kernel_call(): pl.pallas_call(run, in_specs=[SMEM] * len(scalars) + [ANY] * len(outside)...  24.2 us
    ppermute x20, waiting for transfers between devices, move(): return lax.ppermute(array, 'patch', _perm(how))  7.89 us
    ppermute x2, starting transfers between devices, swap_heads(): return lax.ppermute(array, 'head', [(0, 1), (1, 0)])  1.97 us
  transfers between devices with their start and end apart: 22, of which 10 were waited for; matrix products, arithmetic and copies ran while one was open for 1% of the time, Pallas kernels for 26%

profile of v7, /device:TPU:1, one launch (start us, length us, event | category | flops | bytes accessed | tf_op | source)
XLA Modules:
  0.0 72.1 jit_solution(2874099411537675056)
XLA Ops:
  0.7 1.1 %constant_dynamic-slice_fusion.1 = (bf16[2,128,512]{2,1,0:T(8,128)(2,1)S(1)}, bf16[2,128,512]{2,1,0:T(8,128)(2,1)S(1)}) fusion(bf16[2,128,896]{2,1,0:T(8,128)(2,1)} %param.14, s32[]{:T(128)S(6)} %select_n.46, s32[]{:T(128)S(6)} %select_n.47), kind=kLoop, calls=%fused_computation.14 | loop fusion | bytes 1048584 | tf_op jit(solution)/shard_map/dynamic_slice | solution.py:479
  1.7 1.5 %collective-permute-start = (bf16[2,128,512]{2,1,0:T(8,128)(2,1)S(1)}, bf16[2,128,512]{2,1,0:T(8,128)(2,1)S(1)}, u32[]{:S(2)}, u32[]{:S(2)}) collective-permute-start(bf16[2,128,512]{2,1,0:T(8,128)(2,1)S(1)} %get-tuple-element.55), channel_id=1, source_target_pairs={{0,2},{2,0},{4,6},{6,4},{8,10},{10,8},{12,14},{14,12},{16,18},{18,... | collective-permute-start | bytes 786440 | tf_op jit(solution)/shard_map/ppermute | solution.py:63
  3.2 1.4 %collective-permute-start.1 = (bf16[64,3072]{1,0:T(8,128)(2,1)}, bf16[64,3072]{1,0:T(8,128)(2,1)S(1)}, u32[]{:S(2)}, u32[]{:S(2)}) collective-permute-start(bf16[64,3072]{1,0:T(8,128)(2,1)} %refs_1_.2), channel_id=1, source_target_pairs={{0,1},{1,0},{2,3},{3,2},{4,5},{5,4},{6,7},{7,6},{8,9},{9,8},{10,11... | collective-permute-start | bytes 1179656 | tf_op jit(solution)/shard_map/ppermute | solution.py:67
  5.3 1.7 %collective-permute-start.3 = (bf16[2,256,512]{2,1,0:T(8,128)(2,1)S(1)}, bf16[2,256,512]{2,1,0:T(8,128)(2,1)S(1)}, u32[]{:S(2)}, u32[]{:S(2)}) collective-permute-start(bf16[2,256,512]{2,1,0:T(8,128)(2,1)S(1)} %pad_maximum_fusion.refs_4_.refs_6_), channel_id=1, source_target_pairs={{0,32},{2,6},{4,36},{6,10},{8,40},{10,14},{12,44},{14,2},{16,48},{... | collective-permute-start | bytes 1572872 | tf_op jit(solution)/shard_map/ppermute | solution.py:63
  7.0 2.2 %collective-permute-start.4 = (bf16[2,256,512]{2,1,0:T(8,128)(2,1)S(1)}, bf16[2,256,512]{2,1,0:T(8,128)(2,1)S(1)}, u32[]{:S(2)}, u32[]{:S(2)}) collective-permute-start(bf16[2,256,512]{2,1,0:T(8,128)(2,1)S(1)} %pad_maximum_fusion.refs_4_.refs_6_), channel_id=1, source_target_pairs={{0,96},{2,14},{4,100},{6,2},{8,104},{10,6},{12,108},{14,10},{16,11... | collective-permute-start | bytes 1572872 | tf_op jit(solution)/shard_map/ppermute | solution.py:63
  9.3 1.3 %collective-permute-start.8 = (bf16[2,256,512]{2,1,0:T(8,128)(2,1)S(1)}, bf16[2,256,512]{2,1,0:T(8,128)(2,1)S(1)}, u32[]{:S(2)}, u32[]{:S(2)}) collective-permute-start(bf16[2,256,512]{2,1,0:T(8,128)(2,1)S(1)} %pad_maximum_fusion.refs_4_.refs_6_), channel_id=1, source_target_pairs={{0,64},{2,10},{4,68},{6,14},{8,72},{10,2},{12,76},{14,6},{16,80},{... | collective-permute-start | bytes 1572872 | tf_op jit(solution)/shard_map/ppermute | solution.py:63
  10.6 2.6 %collective-permute-start.9 = (bf16[2,256,512]{2,1,0:T(8,128)(2,1)S(1)}, bf16[2,256,512]{2,1,0:T(8,128)(2,1)S(1)}, u32[]{:S(2)}, u32[]{:S(2)}) collective-permute-start(bf16[2,256,512]{2,1,0:T(8,128)(2,1)S(1)} %pad_maximum_fusion.refs_4_.refs_6_), channel_id=1, source_target_pairs={{0,16},{2,18},{4,20},{6,22},{8,24},{10,26},{12,28},{14,30},{16,0},... | collective-permute-start | bytes 1572872 | tf_op jit(solution)/shard_map/ppermute | solution.py:63
  13.2 1.0 %fusion = (f32[1,128,128]{2,1,0:T(8,128)S(1)}, f32[1,128,128]{2,1,0:T(8,128)S(1)}) fusion(f32[128]{0:T(128)} %constant.65.clone, f32[128]{0:T(128)S(1)} %get-tuple-element.58, f32[128]{0:T(128)} %constant.64.clone, f32[128]{0:T(128)S(1)} %get-tuple-element.59, f32[128]{0:T(128)} %constant.66.clone), kind=kLoop, calls=%fused_computation.4 | loop fusion | flops 65536 | bytes 133632 | tf_op jit(solution)/shard_map/cos | solution.py:490
  14.2 2.9 %stage.1 = (bf16[1,3072,896]{2,1,0:T(8,128)(2,1)S(1)}, bf16[64,3072]{1,0:T(8,128)(2,1)S(1)}, f32[4,128,128]{2,1,0:T(8,128)S(1)}) custom-call(bf16[3,3072,896]{2,1,0:T(8,128)(2,1)} %bitcast.7, bf16[64,3072]{1,0:T(8,128)(2,1)} %refs_1_.2, f32[2,128]{1,0:T(2,128)} %refs_2_.1, f32[2,128,128]{2,1,0:T(8,128)S(1)} %pad_maximum_fusion.1.refs_3_, ...), custom_call_target="tpu_custom_call" | custom-call | flops 1 | bytes 1 | tf_op jit(solution)/shard_map/stage/pallas_call | solution.py:78
  17.1 1.3 %query_projection.1 = (bf16[4,128,128]{2,1,0:T(8,128)(2,1)S(1)}, bf16[3,128,128]{2,1,0:T(8,128)(2,1)S(1)}, bf16[7,128,128]{2,1,0:T(8,128)(2,1)S(1)}, bf16[128,3072]{1,0:T(8,128)(2,1)S(1)}) custom-call(s32[1]{0:T(128)} %bitcast.refs_0_, s32[1]{0:T(128)} %bitcast.1.refs_1_, bf16[1,3072,896]{2,1,0:T(8,128)(2,1)S(1)} %get-tuple-element.28.refs_2_, ...), custom_call_target="tpu_custom_call" | custom-call | flops 1 | bytes 1 | tf_op jit(solution)/shard_map/query_projection/pallas_call | solution.py:78
  19.1 0.9 %collective-permute-done.2.refs_1_ = bf16[3,128,128]{2,1,0:T(8,128)(2,1)S(1)} collective-permute-done((bf16[3,128,128]{2,1,0:T(8,128)(2,1)S(1)}, bf16[3,128,128]{2,1,0:T(8,128)(2,1)S(1)}, u32[]{:S(2)}, u32[]{:S(2)}) %collective-permute-start.2) | collective-permute-done | bytes 98336 | tf_op jit(solution)/shard_map/ppermute | solution.py:63
  21.0 1.3 %collective-permute-start.5 = (bf16[7,128,128]{2,1,0:T(8,128)(2,1)S(1)}, bf16[7,128,128]{2,1,0:T(8,128)(2,1)S(1)}, u32[]{:S(2)}, u32[]{:S(2)}) collective-permute-start(bf16[7,128,128]{2,1,0:T(8,128)(2,1)S(1)} %join_units.1.refs_5_.refs_2_), channel_id=1, source_target_pairs={{0,4},{2,34},{4,8},{6,38},{8,12},{10,42},{12,0},{14,46},{16,20},{1... | collective-permute-start | bytes 688136 | tf_op jit(solution)/shard_map/ppermute | solution.py:63
  22.3 1.5 %collective-permute-start.6 = (bf16[7,128,128]{2,1,0:T(8,128)(2,1)S(1)}, bf16[7,128,128]{2,1,0:T(8,128)(2,1)S(1)}, u32[]{:S(2)}, u32[]{:S(2)}) collective-permute-start(bf16[7,128,128]{2,1,0:T(8,128)(2,1)S(1)} %join_units.1.refs_5_.refs_2_), channel_id=1, source_target_pairs={{0,12},{2,98},{4,0},{6,102},{8,4},{10,106},{12,8},{14,110},{16,28}... | collective-permute-start | bytes 688136 | tf_op jit(solution)/shard_map/ppermute | solution.py:63
  23.7 1.5 %collective-permute-start.7 = (bf16[7,128,128]{2,1,0:T(8,128)(2,1)S(1)}, bf16[7,128,128]{2,1,0:T(8,128)(2,1)S(1)}, u32[]{:S(2)}, u32[]{:S(2)}) collective-permute-start(bf16[7,128,128]{2,1,0:T(8,128)(2,1)S(1)} %join_units.1.refs_5_.refs_2_), channel_id=1, source_target_pairs={{0,8},{2,66},{4,12},{6,70},{8,0},{10,74},{12,4},{14,78},{16,24},{1... | collective-permute-start | bytes 688136 | tf_op jit(solution)/shard_map/ppermute | solution.py:63
  25.3 2.6 %collective-permute-start.12 = (bf16[2,256,512]{2,1,0:T(8,128)(2,1)S(1)}, bf16[2,256,512]{2,1,0:T(8,128)(2,1)S(1)}, u32[]{:S(2)}, u32[]{:S(2)}) collective-permute-start(bf16[2,256,512]{2,1,0:T(8,128)(2,1)S(1)} %collective-permute-done.8.refs_6_.refs_9_), channel_id=1, source_target_pairs={{0,16},{2,18},{4,20},{6,22},{8,24},{10,26},{12,28},{14,30},{16,0},... | collective-permute-start | bytes 1572872 | tf_op jit(solution)/shard_map/ppermute | solution.py:63
  27.9 2.7 %key_value_projection.1 = (bf16[2,128,896]{2,1,0:T(8,128)(2,1)}, bf16[2,128,896]{2,1,0:T(8,128)(2,1)S(1)}) custom-call(s32[1]{0:T(128)} %bitcast.refs_0_, s32[1]{0:T(128)} %bitcast.1.refs_1_, bf16[3,3072,896]{2,1,0:T(8,128)(2,1)S(1)} %bitcast.8, bf16[128,3072]{1,0:T(8,128)(2,1)S(1)} %get-tuple-element.34.refs_3_, ...), custom_call_target="tpu_custom_call" | custom-call | flops 1 | bytes 1 | tf_op jit(solution)/shard_map/key_value_projection/pallas_call | solution.py:78
  30.9 3.4 %collective-permute-start.11 = (bf16[2,256,512]{2,1,0:T(8,128)(2,1)S(1)}, bf16[2,256,512]{2,1,0:T(8,128)(2,1)S(1)}, u32[]{:S(2)}, u32[]{:S(2)}) collective-permute-start(bf16[2,256,512]{2,1,0:T(8,128)(2,1)S(1)} %gate.1.refs_4_.refs_8_), channel_id=1, source_target_pairs={{0,96},{2,14},{4,100},{6,2},{8,104},{10,6},{12,108},{14,10},{16,11... | collective-permute-start | bytes 1572872 | tf_op jit(solution)/shard_map/ppermute | solution.py:63
  35.0 1.2 %home_attention.1 = (bf16[7,128,128]{2,1,0:T(8,128)(2,1)S(1)}, f32[128,128]{1,0:T(8,128)S(1)}) custom-call(s32[1]{0:T(128)S(6)} %copy.15.refs_0_, bf16[2,512,896]{2,1,0:T(8,128)(2,1)S(1)} %copy-done.1, bf16[7,128,128]{2,1,0:T(8,128)(2,1)S(1)} %get-tuple-element.33.refs_2_, bf16[2,128,896]{2,1,0:T(8,128)(2,1)S(1)} %get-tuple-element.35.refs_3_, ...), custom_call_target="tpu_custom_call" | custom-call | flops 1 | bytes 1 | tf_op jit(solution)/shard_map/home_attention/pallas_call | solution.py:78
  36.2 4.7 %near_attention.1 = (f32[7,512,128]{2,1,0:T(8,128)S(1)}, f32[512,128]{1,0:T(8,128)S(1)}) custom-call(s32[1]{0:T(128)} %bitcast.refs_0_, s32[1]{0:T(128)} %bitcast.1.refs_1_, bf16[7,128,128]{2,1,0:T(8,128)(2,1)S(1)} %join_units.1.refs_5_.refs_2_, bf16[7,128,128]{2,1,0:T(8,128)(2,1)S(1)} %collective-permute-done.5.refs_0_.refs_3_, ...), custom_call_target="tpu_custom_call" | custom-call | flops 1 | bytes 1 | tf_op jit(solution)/shard_map/near_attention/pallas_call | solution.py:78
  41.2 2.7 %far_attention_0.1 = (bf16[8,64,128]{2,1,0:T(8,128)(2,1)S(1)}, bf16[8,64,128]{2,1,0:T(8,128)(2,1)S(1)}, bf16[8,64,128]{2,1,0:T(8,128)(2,1)S(1)}) custom-call(s32[1]{0:T(128)} %bitcast.refs_0_, s32[1]{0:T(128)} %bitcast.1.refs_1_, bf16[7,128,128]{2,1,0:T(8,128)(2,1)S(1)} %join_units.1.refs_5_.refs_2_, ...), custom_call_target="tpu_custom_call" | custom-call | flops 1 | bytes 1 | tf_op jit(solution)/shard_map/far_attention_0/pallas_call | solution.py:78
  43.8 1.8 %collective-permute-start.17 = (bf16[8,64,128]{2,1,0:T(8,128)(2,1)S(1)}, bf16[8,64,128]{2,1,0:T(8,128)(2,1)S(1)}, u32[]{:S(2)}, u32[]{:S(2)}) collective-permute-start(bf16[8,64,128]{2,1,0:T(8,128)(2,1)S(1)} %get-tuple-element.47), channel_id=1, source_target_pairs={{0,12},{2,98},{4,0},{6,102},{8,4},{10,106},{12,8},{14,110},{16,28}... | collective-permute-start | bytes 393224 | tf_op jit(solution)/shard_map/ppermute | solution.py:63
  45.6 1.3 %collective-permute-start.19 = (bf16[8,64,128]{2,1,0:T(8,128)(2,1)S(1)}, bf16[8,64,128]{2,1,0:T(8,128)(2,1)S(1)}, u32[]{:S(2)}, u32[]{:S(2)}) collective-permute-start(bf16[8,64,128]{2,1,0:T(8,128)(2,1)S(1)} %get-tuple-element.49), channel_id=1, source_target_pairs={{0,8},{2,66},{4,12},{6,70},{8,0},{10,74},{12,4},{14,78},{16,24},{1... | collective-permute-start | bytes 393224 | tf_op jit(solution)/shard_map/ppermute | solution.py:63
  46.9 4.1 %far_attention_1.1 = (bf16[8,128,128]{2,1,0:T(8,128)(2,1)S(1)}, bf16[8,64,128]{2,1,0:T(8,128)(2,1)S(1)}, bf16[8,64,128]{2,1,0:T(8,128)(2,1)S(1)}, bf16[8,64,128]{2,1,0:T(8,128)(2,1)S(1)}) custom-call(s32[1]{0:T(128)} %bitcast.refs_0_, s32[1]{0:T(128)} %bitcast.1.refs_1_, bf16[7,128,128]{2,1,0:T(8,128)(2,1)S(1)} %join_units.1.refs_5_.refs_2_, ...), custom_call_target="tpu_custom_call" | custom-call | flops 1 | bytes 1 | tf_op jit(solution)/shard_map/far_attention_1/pallas_call | solution.py:78
  51.0 1.1 %collective-permute-done.18.refs_2_ = bf16[8,64,128]{2,1,0:T(8,128)(2,1)S(1)} collective-permute-done((bf16[8,64,128]{2,1,0:T(8,128)(2,1)S(1)}, bf16[8,64,128]{2,1,0:T(8,128)(2,1)S(1)}, u32[]{:S(2)}, u32[]{:S(2)}) %collective-permute-start.18) | collective-permute-done | bytes 131104 | tf_op jit(solution)/shard_map/ppermute | solution.py:63
  52.6 4.4 %collective-permute-start.20 = (bf16[4,64,128]{2,1,0:T(8,128)(2,1)S(1)}, bf16[4,64,128]{2,1,0:T(8,128)(2,1)S(1)}, u32[]{:S(2)}, u32[]{:S(2)}) collective-permute-start(bf16[4,64,128]{2,1,0:T(8,128)(2,1)S(1)} %get-tuple-element.52), channel_id=1, source_target_pairs={{0,2},{2,0},{4,6},{6,4},{8,10},{10,8},{12,14},{14,12},{16,18},{18,... | collective-permute-start | bytes 196616 | tf_op jit(solution)/shard_map/ppermute | solution.py:63
  59.1 3.2 %collective-permute-start.13 = (bf16[8,64,128]{2,1,0:T(8,128)(2,1)S(1)}, bf16[8,64,128]{2,1,0:T(8,128)(2,1)S(1)}, u32[]{:S(2)}, u32[]{:S(2)}) collective-permute-start(bf16[8,64,128]{2,1,0:T(8,128)(2,1)S(1)} %get-tuple-element.40), channel_id=1, source_target_pairs={{0,8},{2,66},{4,12},{6,70},{8,0},{10,74},{12,4},{14,78},{16,24},{1... | collective-permute-start | bytes 393224 | tf_op jit(solution)/shard_map/ppermute | solution.py:63
  62.6 1.1 %collective-permute-start.15 = (bf16[8,64,128]{2,1,0:T(8,128)(2,1)S(1)}, bf16[8,64,128]{2,1,0:T(8,128)(2,1)S(1)}, u32[]{:S(2)}, u32[]{:S(2)}) collective-permute-start(bf16[8,64,128]{2,1,0:T(8,128)(2,1)S(1)} %get-tuple-element.42), channel_id=1, source_target_pairs={{0,4},{2,34},{4,8},{6,38},{8,12},{10,42},{12,0},{14,46},{16,20},{1... | collective-permute-start | bytes 393224 | tf_op jit(solution)/shard_map/ppermute | solution.py:63
  63.8 1.2 %collective-permute-done.13.refs_1_ = bf16[8,64,128]{2,1,0:T(8,128)(2,1)S(1)} collective-permute-done((bf16[8,64,128]{2,1,0:T(8,128)(2,1)S(1)}, bf16[8,64,128]{2,1,0:T(8,128)(2,1)S(1)}, u32[]{:S(2)}, u32[]{:S(2)}) %collective-permute-start.13) | collective-permute-done | bytes 131104 | tf_op jit(solution)/shard_map/ppermute | solution.py:63
  65.0 2.0 %collective-permute-done.14.refs_2_ = bf16[8,64,128]{2,1,0:T(8,128)(2,1)S(1)} collective-permute-done((bf16[8,64,128]{2,1,0:T(8,128)(2,1)S(1)}, bf16[8,64,128]{2,1,0:T(8,128)(2,1)S(1)}, u32[]{:S(2)}, u32[]{:S(2)}) %collective-permute-start.14) | collective-permute-done | bytes 131104 | tf_op jit(solution)/shard_map/ppermute | solution.py:63
  66.9 1.0 %collective-permute-done.15.refs_3_ = bf16[8,64,128]{2,1,0:T(8,128)(2,1)S(1)} collective-permute-done((bf16[8,64,128]{2,1,0:T(8,128)(2,1)S(1)}, bf16[8,64,128]{2,1,0:T(8,128)(2,1)S(1)}, u32[]{:S(2)}, u32[]{:S(2)}) %collective-permute-start.15) | collective-permute-done | bytes 131104 | tf_op jit(solution)/shard_map/ppermute | solution.py:63
  68.4 1.3 %collective-permute-start.16 = (bf16[4,64,128]{2,1,0:T(8,128)(2,1)S(1)}, bf16[4,64,128]{2,1,0:T(8,128)(2,1)S(1)}, u32[]{:S(2)}, u32[]{:S(2)}) collective-permute-start(bf16[4,64,128]{2,1,0:T(8,128)(2,1)S(1)} %get-tuple-element.46), channel_id=1, source_target_pairs={{0,2},{2,0},{4,6},{6,4},{8,10},{10,8},{12,14},{14,12},{16,18},{18,... | collective-permute-start | bytes 196616 | tf_op jit(solution)/shard_map/ppermute | solution.py:63
  70.6 1.5 %output_projection_got.3 = bf16[64,3072]{1,0:T(8,128)(2,1)} custom-call(s32[1]{0:T(128)} %bitcast.refs_0_, s32[1]{0:T(128)} %bitcast.1.refs_1_, f32[64,3072]{1,0:T(8,128)S(1)} %output_projection_mine.2.refs_2_, bf16[4,64,128]{2,1,0:T(8,128)(2,1)S(1)} %collective-permute-done.16.refs_3_, bf16[7,128,128]{2,1,0:T(8,128)(2,1)S(1)} %get-tuple-element.36.refs_10_.refs_4_, ...), custom_call_target="tpu_custom_call" | custom-call | flops 1 | bytes 1 | tf_op jit(solution)/shard_map/output_projection_got/pallas_call | solution.py:78
  (41 shorter events, 6.6 us)
Async XLA Ops:
  1.7 3.6 %collective-permute-start = (bf16[2,128,512]{2,1,0:T(8,128)(2,1)S(1)}, bf16[2,128,512]{2,1,0:T(8,128)(2,1)S(1)}, u32[]{:S(2)}, u32[]{:S(2)}) collective-permute-start(bf16[2,128,512]{2,1,0:T(8,128)(2,1)S(1)} %get-tuple-element.55), channel_id=1, source_target_pairs={{0,2},{2,0},{4,6},{6,4},{8,10},{10,8},{12,14},{14,12},{16,18},{18,... | collective-permute-start | bytes 786440 | tf_op jit(solution)/shard_map/ppermute | solution.py:63
  3.2 13.9 %collective-permute-start.1 = (bf16[64,3072]{1,0:T(8,128)(2,1)}, bf16[64,3072]{1,0:T(8,128)(2,1)S(1)}, u32[]{:S(2)}, u32[]{:S(2)}) collective-permute-start(bf16[64,3072]{1,0:T(8,128)(2,1)} %refs_1_.2), channel_id=1, source_target_pairs={{0,1},{1,0},{2,3},{3,2},{4,5},{5,4},{6,7},{7,6},{8,9},{9,8},{10,11... | collective-permute-start | bytes 1179656 | tf_op jit(solution)/shard_map/ppermute | solution.py:67
  5.3 14.7 %collective-permute-start.3 = (bf16[2,256,512]{2,1,0:T(8,128)(2,1)S(1)}, bf16[2,256,512]{2,1,0:T(8,128)(2,1)S(1)}, u32[]{:S(2)}, u32[]{:S(2)}) collective-permute-start(bf16[2,256,512]{2,1,0:T(8,128)(2,1)S(1)} %pad_maximum_fusion.refs_4_.refs_6_), channel_id=1, source_target_pairs={{0,32},{2,6},{4,36},{6,10},{8,40},{10,14},{12,44},{14,2},{16,48},{... | collective-permute-start | bytes 1572872 | tf_op jit(solution)/shard_map/ppermute | solution.py:63
  7.0 13.9 %collective-permute-start.4 = (bf16[2,256,512]{2,1,0:T(8,128)(2,1)S(1)}, bf16[2,256,512]{2,1,0:T(8,128)(2,1)S(1)}, u32[]{:S(2)}, u32[]{:S(2)}) collective-permute-start(bf16[2,256,512]{2,1,0:T(8,128)(2,1)S(1)} %pad_maximum_fusion.refs_4_.refs_6_), channel_id=1, source_target_pairs={{0,96},{2,14},{4,100},{6,2},{8,104},{10,6},{12,108},{14,10},{16,11... | collective-permute-start | bytes 1572872 | tf_op jit(solution)/shard_map/ppermute | solution.py:63
  9.3 16.0 %collective-permute-start.8 = (bf16[2,256,512]{2,1,0:T(8,128)(2,1)S(1)}, bf16[2,256,512]{2,1,0:T(8,128)(2,1)S(1)}, u32[]{:S(2)}, u32[]{:S(2)}) collective-permute-start(bf16[2,256,512]{2,1,0:T(8,128)(2,1)S(1)} %pad_maximum_fusion.refs_4_.refs_6_), channel_id=1, source_target_pairs={{0,64},{2,10},{4,68},{6,14},{8,72},{10,2},{12,76},{14,6},{16,80},{... | collective-permute-start | bytes 1572872 | tf_op jit(solution)/shard_map/ppermute | solution.py:63
  10.6 20.1 %collective-permute-start.9 = (bf16[2,256,512]{2,1,0:T(8,128)(2,1)S(1)}, bf16[2,256,512]{2,1,0:T(8,128)(2,1)S(1)}, u32[]{:S(2)}, u32[]{:S(2)}) collective-permute-start(bf16[2,256,512]{2,1,0:T(8,128)(2,1)S(1)} %pad_maximum_fusion.refs_4_.refs_6_), channel_id=1, source_target_pairs={{0,16},{2,18},{4,20},{6,22},{8,24},{10,26},{12,28},{14,30},{16,0},... | collective-permute-start | bytes 1572872 | tf_op jit(solution)/shard_map/ppermute | solution.py:63
  14.2 13.7 %copy-start = (bf16[3072,3,896]{2,0,1:T(8,128)(2,1)S(1)}, bf16[3072,3,896]{2,0,1:T(8,128)(2,1)}, u32[]{:S(2)}) copy-start(bf16[3072,3,896]{2,0,1:T(8,128)(2,1)} %param.12) | copy-start | bytes 49545220
  18.4 1.6 %collective-permute-start.2 = (bf16[3,128,128]{2,1,0:T(8,128)(2,1)S(1)}, bf16[3,128,128]{2,1,0:T(8,128)(2,1)S(1)}, u32[]{:S(2)}, u32[]{:S(2)}) collective-permute-start(bf16[3,128,128]{2,1,0:T(8,128)(2,1)S(1)} %get-tuple-element.32), channel_id=1, source_target_pairs={{0,2},{2,0},{4,6},{6,4},{8,10},{10,8},{12,14},{14,12},{16,18},{18,... | collective-permute-start | bytes 294920 | tf_op jit(solution)/shard_map/ppermute | solution.py:63
  21.0 9.6 %collective-permute-start.5 = (bf16[7,128,128]{2,1,0:T(8,128)(2,1)S(1)}, bf16[7,128,128]{2,1,0:T(8,128)(2,1)S(1)}, u32[]{:S(2)}, u32[]{:S(2)}) collective-permute-start(bf16[7,128,128]{2,1,0:T(8,128)(2,1)S(1)} %join_units.1.refs_5_.refs_2_), channel_id=1, source_target_pairs={{0,4},{2,34},{4,8},{6,38},{8,12},{10,42},{12,0},{14,46},{16,20},{1... | collective-permute-start | bytes 688136 | tf_op jit(solution)/shard_map/ppermute | solution.py:63
  22.3 8.3 %collective-permute-start.6 = (bf16[7,128,128]{2,1,0:T(8,128)(2,1)S(1)}, bf16[7,128,128]{2,1,0:T(8,128)(2,1)S(1)}, u32[]{:S(2)}, u32[]{:S(2)}) collective-permute-start(bf16[7,128,128]{2,1,0:T(8,128)(2,1)S(1)} %join_units.1.refs_5_.refs_2_), channel_id=1, source_target_pairs={{0,12},{2,98},{4,0},{6,102},{8,4},{10,106},{12,8},{14,110},{16,28}... | collective-permute-start | bytes 688136 | tf_op jit(solution)/shard_map/ppermute | solution.py:63
  23.7 7.1 %collective-permute-start.7 = (bf16[7,128,128]{2,1,0:T(8,128)(2,1)S(1)}, bf16[7,128,128]{2,1,0:T(8,128)(2,1)S(1)}, u32[]{:S(2)}, u32[]{:S(2)}) collective-permute-start(bf16[7,128,128]{2,1,0:T(8,128)(2,1)S(1)} %join_units.1.refs_5_.refs_2_), channel_id=1, source_target_pairs={{0,8},{2,66},{4,12},{6,70},{8,0},{10,74},{12,4},{14,78},{16,24},{1... | collective-permute-start | bytes 688136 | tf_op jit(solution)/shard_map/ppermute | solution.py:63
  25.3 15.6 %collective-permute-start.12 = (bf16[2,256,512]{2,1,0:T(8,128)(2,1)S(1)}, bf16[2,256,512]{2,1,0:T(8,128)(2,1)S(1)}, u32[]{:S(2)}, u32[]{:S(2)}) collective-permute-start(bf16[2,256,512]{2,1,0:T(8,128)(2,1)S(1)} %collective-permute-done.8.refs_6_.refs_9_), channel_id=1, source_target_pairs={{0,16},{2,18},{4,20},{6,22},{8,24},{10,26},{12,28},{14,30},{16,0},... | collective-permute-start | bytes 1572872 | tf_op jit(solution)/shard_map/ppermute | solution.py:63
  27.9 7.1 %copy-start.1 = (bf16[2,512,896]{2,1,0:T(8,128)(2,1)S(1)}, bf16[2,512,896]{2,1,0:T(8,128)(2,1)}, u32[]{:S(2)}) copy-start(bf16[2,512,896]{2,1,0:T(8,128)(2,1)} %refs_1_.3) | copy-start | bytes 5505028
  30.9 10.3 %collective-permute-start.10 = (bf16[2,256,512]{2,1,0:T(8,128)(2,1)S(1)}, bf16[2,256,512]{2,1,0:T(8,128)(2,1)S(1)}, u32[]{:S(2)}, u32[]{:S(2)}) collective-permute-start(bf16[2,256,512]{2,1,0:T(8,128)(2,1)S(1)} %gate.1.refs_4_.refs_8_), channel_id=1, source_target_pairs={{0,32},{2,6},{4,36},{6,10},{8,40},{10,14},{12,44},{14,2},{16,48},{... | collective-permute-start | bytes 1572872 | tf_op jit(solution)/shard_map/ppermute | solution.py:63
  30.9 10.3 %collective-permute-start.11 = (bf16[2,256,512]{2,1,0:T(8,128)(2,1)S(1)}, bf16[2,256,512]{2,1,0:T(8,128)(2,1)S(1)}, u32[]{:S(2)}, u32[]{:S(2)}) collective-permute-start(bf16[2,256,512]{2,1,0:T(8,128)(2,1)S(1)} %gate.1.refs_4_.refs_8_), channel_id=1, source_target_pairs={{0,96},{2,14},{4,100},{6,2},{8,104},{10,6},{12,108},{14,10},{16,11... | collective-permute-start | bytes 1572872 | tf_op jit(solution)/shard_map/ppermute | solution.py:63
  36.2 20.8 %slice-start = ((s8[5505024]{0:T(1024)(128)(4,1)}), s8[4194304]{0:T(1024)(128)(4,1)S(1)}, s32[]{:S(2)}) async-start(s8[5505024]{0:T(1024)(128)(4,1)} %bitcast.5), calls=%async_computation | async-start | bytes 8388608
  41.2 15.8 %slice-start.1 = ((s8[5505024]{0:T(1024)(128)(4,1)}), s8[1310720]{0:T(1024)(128)(4,1)S(1)}, s32[]{:S(2)}) async-start(s8[5505024]{0:T(1024)(128)(4,1)} %bitcast.5), calls=%async_computation.1 | async-start | bytes 2621440
  43.8 7.1 %collective-permute-start.17 = (bf16[8,64,128]{2,1,0:T(8,128)(2,1)S(1)}, bf16[8,64,128]{2,1,0:T(8,128)(2,1)S(1)}, u32[]{:S(2)}, u32[]{:S(2)}) collective-permute-start(bf16[8,64,128]{2,1,0:T(8,128)(2,1)S(1)} %get-tuple-element.47), channel_id=1, source_target_pairs={{0,12},{2,98},{4,0},{6,102},{8,4},{10,106},{12,8},{14,110},{16,28}... | collective-permute-start | bytes 393224 | tf_op jit(solution)/shard_map/ppermute | solution.py:63
  45.6 6.4 %collective-permute-start.18 = (bf16[8,64,128]{2,1,0:T(8,128)(2,1)S(1)}, bf16[8,64,128]{2,1,0:T(8,128)(2,1)S(1)}, u32[]{:S(2)}, u32[]{:S(2)}) collective-permute-start(bf16[8,64,128]{2,1,0:T(8,128)(2,1)S(1)} %get-tuple-element.48), channel_id=1, source_target_pairs={{0,4},{2,34},{4,8},{6,38},{8,12},{10,42},{12,0},{14,46},{16,20},{1... | collective-permute-start | bytes 393224 | tf_op jit(solution)/shard_map/ppermute | solution.py:63
  45.6 6.4 %collective-permute-start.19 = (bf16[8,64,128]{2,1,0:T(8,128)(2,1)S(1)}, bf16[8,64,128]{2,1,0:T(8,128)(2,1)S(1)}, u32[]{:S(2)}, u32[]{:S(2)}) collective-permute-start(bf16[8,64,128]{2,1,0:T(8,128)(2,1)S(1)} %get-tuple-element.49), channel_id=1, source_target_pairs={{0,8},{2,66},{4,12},{6,70},{8,0},{10,74},{12,4},{14,78},{16,24},{1... | collective-permute-start | bytes 393224 | tf_op jit(solution)/shard_map/ppermute | solution.py:63
  52.6 5.3 %collective-permute-start.20 = (bf16[4,64,128]{2,1,0:T(8,128)(2,1)S(1)}, bf16[4,64,128]{2,1,0:T(8,128)(2,1)S(1)}, u32[]{:S(2)}, u32[]{:S(2)}) collective-permute-start(bf16[4,64,128]{2,1,0:T(8,128)(2,1)S(1)} %get-tuple-element.52), channel_id=1, source_target_pairs={{0,2},{2,0},{4,6},{6,4},{8,10},{10,8},{12,14},{14,12},{16,18},{18,... | collective-permute-start | bytes 196616 | tf_op jit(solution)/shard_map/ppermute | solution.py:63
  58.5 12.1 %collective-permute-start.21 = (bf16[64,3072]{1,0:T(8,128)(2,1)S(1)}, bf16[64,3072]{1,0:T(8,128)(2,1)S(1)}, u32[]{:S(2)}, u32[]{:S(2)}) collective-permute-start(bf16[64,3072]{1,0:T(8,128)(2,1)S(1)} %output_projection_got.2), channel_id=1, source_target_pairs={{0,1},{1,0},{2,3},{3,2},{4,5},{5,4},{6,7},{7,6},{8,9},{9,8},{10,11... | collective-permute-start | bytes 1179656 | tf_op jit(solution)/shard_map/ppermute | solution.py:67
  59.1 5.9 %collective-permute-start.13 = (bf16[8,64,128]{2,1,0:T(8,128)(2,1)S(1)}, bf16[8,64,128]{2,1,0:T(8,128)(2,1)S(1)}, u32[]{:S(2)}, u32[]{:S(2)}) collective-permute-start(bf16[8,64,128]{2,1,0:T(8,128)(2,1)S(1)} %get-tuple-element.40), channel_id=1, source_target_pairs={{0,8},{2,66},{4,12},{6,70},{8,0},{10,74},{12,4},{14,78},{16,24},{1... | collective-permute-start | bytes 393224 | tf_op jit(solution)/shard_map/ppermute | solution.py:63
  62.3 4.6 %collective-permute-start.14 = (bf16[8,64,128]{2,1,0:T(8,128)(2,1)S(1)}, bf16[8,64,128]{2,1,0:T(8,128)(2,1)S(1)}, u32[]{:S(2)}, u32[]{:S(2)}) collective-permute-start(bf16[8,64,128]{2,1,0:T(8,128)(2,1)S(1)} %get-tuple-element.41), channel_id=1, source_target_pairs={{0,12},{2,98},{4,0},{6,102},{8,4},{10,106},{12,8},{14,110},{16,28}... | collective-permute-start | bytes 393224 | tf_op jit(solution)/shard_map/ppermute | solution.py:63
  62.6 5.3 %collective-permute-start.15 = (bf16[8,64,128]{2,1,0:T(8,128)(2,1)S(1)}, bf16[8,64,128]{2,1,0:T(8,128)(2,1)S(1)}, u32[]{:S(2)}, u32[]{:S(2)}) collective-permute-start(bf16[8,64,128]{2,1,0:T(8,128)(2,1)S(1)} %get-tuple-element.42), channel_id=1, source_target_pairs={{0,4},{2,34},{4,8},{6,38},{8,12},{10,42},{12,0},{14,46},{16,20},{1... | collective-permute-start | bytes 393224 | tf_op jit(solution)/shard_map/ppermute | solution.py:63
  68.4 2.2 %collective-permute-start.16 = (bf16[4,64,128]{2,1,0:T(8,128)(2,1)S(1)}, bf16[4,64,128]{2,1,0:T(8,128)(2,1)S(1)}, u32[]{:S(2)}, u32[]{:S(2)}) collective-permute-start(bf16[4,64,128]{2,1,0:T(8,128)(2,1)S(1)} %get-tuple-element.46), channel_id=1, source_target_pairs={{0,2},{2,0},{4,6},{6,4},{8,10},{10,8},{12,14},{14,12},{16,18},{18,... | collective-permute-start | bytes 196616 | tf_op jit(solution)/shard_map/ppermute | solution.py:63

commit v8 on v7

--- a/solution.py
+++ b/solution.py
@@ -450,7 +450,7 @@
     arrays = (mine, stat, home, level, w_out)
     kernel = functools.partial(_mine_kernel, g)
     part = kernel_call(kernel, "output_projection_mine", outs, [], place, [], *arrays)[0]
-    outs = [((HALF, D), BF16, HBM)]
+    outs = [((HALF, D), BF16, HBM) if g == 1 else ((HALF, D), BF16)]
     arrays = (part, got, home, level, w_out, *other)
     kernel = functools.partial(_got_kernel, g)
     return kernel_call(kernel, "output_projection_got", outs, [], place, [], *arrays)[0]

time: 72.2 us -> 72.2 us (level)
  no operation moved by 1% of the time
where the time goes in v8:
time: 72.2 us; the launch traced here: 72.1 us
  starting transfers between devices  35.7 us (49%)
  Pallas kernels  24.2 us (34%)
  waiting for transfers between devices  7.89 us (11%)
  between operations  2.14 us (3%)
  local copies, waits for them, and re-layouts  1.09 us (2%)
  other arithmetic  1.07 us (1%)
    ppermute x20, starting transfers between devices, move(): return lax.ppermute(array, 'patch', _perm(how))  33.7 us
    pallas_call x14, Pallas kernels, kernel_call(): pl.pallas_call(run, in_specs=[SMEM] * len(scalars) + [ANY] * len(outside)...  24.2 us
    ppermute x20, waiting for transfers between devices, move(): return lax.ppermute(array, 'patch', _perm(how))  7.89 us
    ppermute x2, starting transfers between devices, swap_heads(): return lax.ppermute(array, 'head', [(0, 1), (1, 0)])  1.97 us
  transfers between devices with their start and end apart: 22, of which 10 were waited for; matrix products, arithmetic and copies ran while one was open for 1% of the time, Pallas kernels for 26%

profile of v8, /device:TPU:1, one launch (start us, length us, event | category | flops | bytes accessed | tf_op | source)
XLA Modules:
  0.0 72.1 jit_solution(2874099411537675056)
XLA Ops:
  0.7 1.1 %constant_dynamic-slice_fusion.1 = (bf16[2,128,512]{2,1,0:T(8,128)(2,1)S(1)}, bf16[2,128,512]{2,1,0:T(8,128)(2,1)S(1)}) fusion(bf16[2,128,896]{2,1,0:T(8,128)(2,1)} %param.14, s32[]{:T(128)S(6)} %select_n.46, s32[]{:T(128)S(6)} %select_n.47), kind=kLoop, calls=%fused_computation.14 | loop fusion | bytes 1048584 | tf_op jit(solution)/shard_map/dynamic_slice | solution.py:479
  1.7 1.5 %collective-permute-start = (bf16[2,128,512]{2,1,0:T(8,128)(2,1)S(1)}, bf16[2,128,512]{2,1,0:T(8,128)(2,1)S(1)}, u32[]{:S(2)}, u32[]{:S(2)}) collective-permute-start(bf16[2,128,512]{2,1,0:T(8,128)(2,1)S(1)} %get-tuple-element.55), channel_id=1, source_target_pairs={{0,2},{2,0},{4,6},{6,4},{8,10},{10,8},{12,14},{14,12},{16,18},{18,... | collective-permute-start | bytes 786440 | tf_op jit(solution)/shard_map/ppermute | solution.py:63
  3.2 1.4 %collective-permute-start.1 = (bf16[64,3072]{1,0:T(8,128)(2,1)}, bf16[64,3072]{1,0:T(8,128)(2,1)S(1)}, u32[]{:S(2)}, u32[]{:S(2)}) collective-permute-start(bf16[64,3072]{1,0:T(8,128)(2,1)} %refs_1_.2), channel_id=1, source_target_pairs={{0,1},{1,0},{2,3},{3,2},{4,5},{5,4},{6,7},{7,6},{8,9},{9,8},{10,11... | collective-permute-start | bytes 1179656 | tf_op jit(solution)/shard_map/ppermute | solution.py:67
  5.3 1.7 %collective-permute-start.3 = (bf16[2,256,512]{2,1,0:T(8,128)(2,1)S(1)}, bf16[2,256,512]{2,1,0:T(8,128)(2,1)S(1)}, u32[]{:S(2)}, u32[]{:S(2)}) collective-permute-start(bf16[2,256,512]{2,1,0:T(8,128)(2,1)S(1)} %pad_maximum_fusion.refs_4_.refs_6_), channel_id=1, source_target_pairs={{0,32},{2,6},{4,36},{6,10},{8,40},{10,14},{12,44},{14,2},{16,48},{... | collective-permute-start | bytes 1572872 | tf_op jit(solution)/shard_map/ppermute | solution.py:63
  7.0 2.2 %collective-permute-start.4 = (bf16[2,256,512]{2,1,0:T(8,128)(2,1)S(1)}, bf16[2,256,512]{2,1,0:T(8,128)(2,1)S(1)}, u32[]{:S(2)}, u32[]{:S(2)}) collective-permute-start(bf16[2,256,512]{2,1,0:T(8,128)(2,1)S(1)} %pad_maximum_fusion.refs_4_.refs_6_), channel_id=1, source_target_pairs={{0,96},{2,14},{4,100},{6,2},{8,104},{10,6},{12,108},{14,10},{16,11... | collective-permute-start | bytes 1572872 | tf_op jit(solution)/shard_map/ppermute | solution.py:63
  9.3 1.3 %collective-permute-start.8 = (bf16[2,256,512]{2,1,0:T(8,128)(2,1)S(1)}, bf16[2,256,512]{2,1,0:T(8,128)(2,1)S(1)}, u32[]{:S(2)}, u32[]{:S(2)}) collective-permute-start(bf16[2,256,512]{2,1,0:T(8,128)(2,1)S(1)} %pad_maximum_fusion.refs_4_.refs_6_), channel_id=1, source_target_pairs={{0,64},{2,10},{4,68},{6,14},{8,72},{10,2},{12,76},{14,6},{16,80},{... | collective-permute-start | bytes 1572872 | tf_op jit(solution)/shard_map/ppermute | solution.py:63
  10.6 2.6 %collective-permute-start.9 = (bf16[2,256,512]{2,1,0:T(8,128)(2,1)S(1)}, bf16[2,256,512]{2,1,0:T(8,128)(2,1)S(1)}, u32[]{:S(2)}, u32[]{:S(2)}) collective-permute-start(bf16[2,256,512]{2,1,0:T(8,128)(2,1)S(1)} %pad_maximum_fusion.refs_4_.refs_6_), channel_id=1, source_target_pairs={{0,16},{2,18},{4,20},{6,22},{8,24},{10,26},{12,28},{14,30},{16,0},... | collective-permute-start | bytes 1572872 | tf_op jit(solution)/shard_map/ppermute | solution.py:63
  13.2 1.0 %fusion = (f32[1,128,128]{2,1,0:T(8,128)S(1)}, f32[1,128,128]{2,1,0:T(8,128)S(1)}) fusion(f32[128]{0:T(128)} %constant.65.clone, f32[128]{0:T(128)S(1)} %get-tuple-element.58, f32[128]{0:T(128)} %constant.64.clone, f32[128]{0:T(128)S(1)} %get-tuple-element.59, f32[128]{0:T(128)} %constant.66.clone), kind=kLoop, calls=%fused_computation.4 | loop fusion | flops 65536 | bytes 133632 | tf_op jit(solution)/shard_map/cos | solution.py:490
  14.2 2.9 %stage.1 = (bf16[1,3072,896]{2,1,0:T(8,128)(2,1)S(1)}, bf16[64,3072]{1,0:T(8,128)(2,1)S(1)}, f32[4,128,128]{2,1,0:T(8,128)S(1)}) custom-call(bf16[3,3072,896]{2,1,0:T(8,128)(2,1)} %bitcast.7, bf16[64,3072]{1,0:T(8,128)(2,1)} %refs_1_.2, f32[2,128]{1,0:T(2,128)} %refs_2_.1, f32[2,128,128]{2,1,0:T(8,128)S(1)} %pad_maximum_fusion.1.refs_3_, ...), custom_call_target="tpu_custom_call" | custom-call | flops 1 | bytes 1 | tf_op jit(solution)/shard_map/stage/pallas_call | solution.py:78
  17.1 1.3 %query_projection.1 = (bf16[4,128,128]{2,1,0:T(8,128)(2,1)S(1)}, bf16[3,128,128]{2,1,0:T(8,128)(2,1)S(1)}, bf16[7,128,128]{2,1,0:T(8,128)(2,1)S(1)}, bf16[128,3072]{1,0:T(8,128)(2,1)S(1)}) custom-call(s32[1]{0:T(128)} %bitcast.refs_0_, s32[1]{0:T(128)} %bitcast.1.refs_1_, bf16[1,3072,896]{2,1,0:T(8,128)(2,1)S(1)} %get-tuple-element.28.refs_2_, ...), custom_call_target="tpu_custom_call" | custom-call | flops 1 | bytes 1 | tf_op jit(solution)/shard_map/query_projection/pallas_call | solution.py:78
  19.1 0.9 %collective-permute-done.2.refs_1_ = bf16[3,128,128]{2,1,0:T(8,128)(2,1)S(1)} collective-permute-done((bf16[3,128,128]{2,1,0:T(8,128)(2,1)S(1)}, bf16[3,128,128]{2,1,0:T(8,128)(2,1)S(1)}, u32[]{:S(2)}, u32[]{:S(2)}) %collective-permute-start.2) | collective-permute-done | bytes 98336 | tf_op jit(solution)/shard_map/ppermute | solution.py:63
  21.0 1.3 %collective-permute-start.5 = (bf16[7,128,128]{2,1,0:T(8,128)(2,1)S(1)}, bf16[7,128,128]{2,1,0:T(8,128)(2,1)S(1)}, u32[]{:S(2)}, u32[]{:S(2)}) collective-permute-start(bf16[7,128,128]{2,1,0:T(8,128)(2,1)S(1)} %join_units.1.refs_5_.refs_2_), channel_id=1, source_target_pairs={{0,4},{2,34},{4,8},{6,38},{8,12},{10,42},{12,0},{14,46},{16,20},{1... | collective-permute-start | bytes 688136 | tf_op jit(solution)/shard_map/ppermute | solution.py:63
  22.3 1.5 %collective-permute-start.6 = (bf16[7,128,128]{2,1,0:T(8,128)(2,1)S(1)}, bf16[7,128,128]{2,1,0:T(8,128)(2,1)S(1)}, u32[]{:S(2)}, u32[]{:S(2)}) collective-permute-start(bf16[7,128,128]{2,1,0:T(8,128)(2,1)S(1)} %join_units.1.refs_5_.refs_2_), channel_id=1, source_target_pairs={{0,12},{2,98},{4,0},{6,102},{8,4},{10,106},{12,8},{14,110},{16,28}... | collective-permute-start | bytes 688136 | tf_op jit(solution)/shard_map/ppermute | solution.py:63
  23.7 1.5 %collective-permute-start.7 = (bf16[7,128,128]{2,1,0:T(8,128)(2,1)S(1)}, bf16[7,128,128]{2,1,0:T(8,128)(2,1)S(1)}, u32[]{:S(2)}, u32[]{:S(2)}) collective-permute-start(bf16[7,128,128]{2,1,0:T(8,128)(2,1)S(1)} %join_units.1.refs_5_.refs_2_), channel_id=1, source_target_pairs={{0,8},{2,66},{4,12},{6,70},{8,0},{10,74},{12,4},{14,78},{16,24},{1... | collective-permute-start | bytes 688136 | tf_op jit(solution)/shard_map/ppermute | solution.py:63
  25.3 2.6 %collective-permute-start.12 = (bf16[2,256,512]{2,1,0:T(8,128)(2,1)S(1)}, bf16[2,256,512]{2,1,0:T(8,128)(2,1)S(1)}, u32[]{:S(2)}, u32[]{:S(2)}) collective-permute-start(bf16[2,256,512]{2,1,0:T(8,128)(2,1)S(1)} %collective-permute-done.8.refs_6_.refs_9_), channel_id=1, source_target_pairs={{0,16},{2,18},{4,20},{6,22},{8,24},{10,26},{12,28},{14,30},{16,0},... | collective-permute-start | bytes 1572872 | tf_op jit(solution)/shard_map/ppermute | solution.py:63
  27.9 2.7 %key_value_projection.1 = (bf16[2,128,896]{2,1,0:T(8,128)(2,1)}, bf16[2,128,896]{2,1,0:T(8,128)(2,1)S(1)}) custom-call(s32[1]{0:T(128)} %bitcast.refs_0_, s32[1]{0:T(128)} %bitcast.1.refs_1_, bf16[3,3072,896]{2,1,0:T(8,128)(2,1)S(1)} %bitcast.8, bf16[128,3072]{1,0:T(8,128)(2,1)S(1)} %get-tuple-element.34.refs_3_, ...), custom_call_target="tpu_custom_call" | custom-call | flops 1 | bytes 1 | tf_op jit(solution)/shard_map/key_value_projection/pallas_call | solution.py:78
  30.9 3.4 %collective-permute-start.11 = (bf16[2,256,512]{2,1,0:T(8,128)(2,1)S(1)}, bf16[2,256,512]{2,1,0:T(8,128)(2,1)S(1)}, u32[]{:S(2)}, u32[]{:S(2)}) collective-permute-start(bf16[2,256,512]{2,1,0:T(8,128)(2,1)S(1)} %gate.1.refs_4_.refs_8_), channel_id=1, source_target_pairs={{0,96},{2,14},{4,100},{6,2},{8,104},{10,6},{12,108},{14,10},{16,11... | collective-permute-start | bytes 1572872 | tf_op jit(solution)/shard_map/ppermute | solution.py:63
  35.0 1.2 %home_attention.1 = (bf16[7,128,128]{2,1,0:T(8,128)(2,1)S(1)}, f32[128,128]{1,0:T(8,128)S(1)}) custom-call(s32[1]{0:T(128)S(6)} %copy.15.refs_0_, bf16[2,512,896]{2,1,0:T(8,128)(2,1)S(1)} %copy-done.1, bf16[7,128,128]{2,1,0:T(8,128)(2,1)S(1)} %get-tuple-element.33.refs_2_, bf16[2,128,896]{2,1,0:T(8,128)(2,1)S(1)} %get-tuple-element.35.refs_3_, ...), custom_call_target="tpu_custom_call" | custom-call | flops 1 | bytes 1 | tf_op jit(solution)/shard_map/home_attention/pallas_call | solution.py:78
  36.2 4.7 %near_attention.1 = (f32[7,512,128]{2,1,0:T(8,128)S(1)}, f32[512,128]{1,0:T(8,128)S(1)}) custom-call(s32[1]{0:T(128)} %bitcast.refs_0_, s32[1]{0:T(128)} %bitcast.1.refs_1_, bf16[7,128,128]{2,1,0:T(8,128)(2,1)S(1)} %join_units.1.refs_5_.refs_2_, bf16[7,128,128]{2,1,0:T(8,128)(2,1)S(1)} %collective-permute-done.5.refs_0_.refs_3_, ...), custom_call_target="tpu_custom_call" | custom-call | flops 1 | bytes 1 | tf_op jit(solution)/shard_map/near_attention/pallas_call | solution.py:78
  41.2 2.7 %far_attention_0.1 = (bf16[8,64,128]{2,1,0:T(8,128)(2,1)S(1)}, bf16[8,64,128]{2,1,0:T(8,128)(2,1)S(1)}, bf16[8,64,128]{2,1,0:T(8,128)(2,1)S(1)}) custom-call(s32[1]{0:T(128)} %bitcast.refs_0_, s32[1]{0:T(128)} %bitcast.1.refs_1_, bf16[7,128,128]{2,1,0:T(8,128)(2,1)S(1)} %join_units.1.refs_5_.refs_2_, ...), custom_call_target="tpu_custom_call" | custom-call | flops 1 | bytes 1 | tf_op jit(solution)/shard_map/far_attention_0/pallas_call | solution.py:78
  43.8 1.8 %collective-permute-start.17 = (bf16[8,64,128]{2,1,0:T(8,128)(2,1)S(1)}, bf16[8,64,128]{2,1,0:T(8,128)(2,1)S(1)}, u32[]{:S(2)}, u32[]{:S(2)}) collective-permute-start(bf16[8,64,128]{2,1,0:T(8,128)(2,1)S(1)} %get-tuple-element.47), channel_id=1, source_target_pairs={{0,12},{2,98},{4,0},{6,102},{8,4},{10,106},{12,8},{14,110},{16,28}... | collective-permute-start | bytes 393224 | tf_op jit(solution)/shard_map/ppermute | solution.py:63
  45.6 1.3 %collective-permute-start.19 = (bf16[8,64,128]{2,1,0:T(8,128)(2,1)S(1)}, bf16[8,64,128]{2,1,0:T(8,128)(2,1)S(1)}, u32[]{:S(2)}, u32[]{:S(2)}) collective-permute-start(bf16[8,64,128]{2,1,0:T(8,128)(2,1)S(1)} %get-tuple-element.49), channel_id=1, source_target_pairs={{0,8},{2,66},{4,12},{6,70},{8,0},{10,74},{12,4},{14,78},{16,24},{1... | collective-permute-start | bytes 393224 | tf_op jit(solution)/shard_map/ppermute | solution.py:63
  46.9 4.1 %far_attention_1.1 = (bf16[8,128,128]{2,1,0:T(8,128)(2,1)S(1)}, bf16[8,64,128]{2,1,0:T(8,128)(2,1)S(1)}, bf16[8,64,128]{2,1,0:T(8,128)(2,1)S(1)}, bf16[8,64,128]{2,1,0:T(8,128)(2,1)S(1)}) custom-call(s32[1]{0:T(128)} %bitcast.refs_0_, s32[1]{0:T(128)} %bitcast.1.refs_1_, bf16[7,128,128]{2,1,0:T(8,128)(2,1)S(1)} %join_units.1.refs_5_.refs_2_, ...), custom_call_target="tpu_custom_call" | custom-call | flops 1 | bytes 1 | tf_op jit(solution)/shard_map/far_attention_1/pallas_call | solution.py:78
  51.0 1.1 %collective-permute-done.18.refs_2_ = bf16[8,64,128]{2,1,0:T(8,128)(2,1)S(1)} collective-permute-done((bf16[8,64,128]{2,1,0:T(8,128)(2,1)S(1)}, bf16[8,64,128]{2,1,0:T(8,128)(2,1)S(1)}, u32[]{:S(2)}, u32[]{:S(2)}) %collective-permute-start.18) | collective-permute-done | bytes 131104 | tf_op jit(solution)/shard_map/ppermute | solution.py:63
  52.6 4.4 %collective-permute-start.20 = (bf16[4,64,128]{2,1,0:T(8,128)(2,1)S(1)}, bf16[4,64,128]{2,1,0:T(8,128)(2,1)S(1)}, u32[]{:S(2)}, u32[]{:S(2)}) collective-permute-start(bf16[4,64,128]{2,1,0:T(8,128)(2,1)S(1)} %get-tuple-element.52), channel_id=1, source_target_pairs={{0,2},{2,0},{4,6},{6,4},{8,10},{10,8},{12,14},{14,12},{16,18},{18,... | collective-permute-start | bytes 196616 | tf_op jit(solution)/shard_map/ppermute | solution.py:63
  59.1 3.2 %collective-permute-start.13 = (bf16[8,64,128]{2,1,0:T(8,128)(2,1)S(1)}, bf16[8,64,128]{2,1,0:T(8,128)(2,1)S(1)}, u32[]{:S(2)}, u32[]{:S(2)}) collective-permute-start(bf16[8,64,128]{2,1,0:T(8,128)(2,1)S(1)} %get-tuple-element.40), channel_id=1, source_target_pairs={{0,8},{2,66},{4,12},{6,70},{8,0},{10,74},{12,4},{14,78},{16,24},{1... | collective-permute-start | bytes 393224 | tf_op jit(solution)/shard_map/ppermute | solution.py:63
  62.6 1.1 %collective-permute-start.15 = (bf16[8,64,128]{2,1,0:T(8,128)(2,1)S(1)}, bf16[8,64,128]{2,1,0:T(8,128)(2,1)S(1)}, u32[]{:S(2)}, u32[]{:S(2)}) collective-permute-start(bf16[8,64,128]{2,1,0:T(8,128)(2,1)S(1)} %get-tuple-element.42), channel_id=1, source_target_pairs={{0,4},{2,34},{4,8},{6,38},{8,12},{10,42},{12,0},{14,46},{16,20},{1... | collective-permute-start | bytes 393224 | tf_op jit(solution)/shard_map/ppermute | solution.py:63
  63.8 1.2 %collective-permute-done.13.refs_1_ = bf16[8,64,128]{2,1,0:T(8,128)(2,1)S(1)} collective-permute-done((bf16[8,64,128]{2,1,0:T(8,128)(2,1)S(1)}, bf16[8,64,128]{2,1,0:T(8,128)(2,1)S(1)}, u32[]{:S(2)}, u32[]{:S(2)}) %collective-permute-start.13) | collective-permute-done | bytes 131104 | tf_op jit(solution)/shard_map/ppermute | solution.py:63
  65.0 2.0 %collective-permute-done.14.refs_2_ = bf16[8,64,128]{2,1,0:T(8,128)(2,1)S(1)} collective-permute-done((bf16[8,64,128]{2,1,0:T(8,128)(2,1)S(1)}, bf16[8,64,128]{2,1,0:T(8,128)(2,1)S(1)}, u32[]{:S(2)}, u32[]{:S(2)}) %collective-permute-start.14) | collective-permute-done | bytes 131104 | tf_op jit(solution)/shard_map/ppermute | solution.py:63
  66.9 1.0 %collective-permute-done.15.refs_3_ = bf16[8,64,128]{2,1,0:T(8,128)(2,1)S(1)} collective-permute-done((bf16[8,64,128]{2,1,0:T(8,128)(2,1)S(1)}, bf16[8,64,128]{2,1,0:T(8,128)(2,1)S(1)}, u32[]{:S(2)}, u32[]{:S(2)}) %collective-permute-start.15) | collective-permute-done | bytes 131104 | tf_op jit(solution)/shard_map/ppermute | solution.py:63
  68.4 1.3 %collective-permute-start.16 = (bf16[4,64,128]{2,1,0:T(8,128)(2,1)S(1)}, bf16[4,64,128]{2,1,0:T(8,128)(2,1)S(1)}, u32[]{:S(2)}, u32[]{:S(2)}) collective-permute-start(bf16[4,64,128]{2,1,0:T(8,128)(2,1)S(1)} %get-tuple-element.46), channel_id=1, source_target_pairs={{0,2},{2,0},{4,6},{6,4},{8,10},{10,8},{12,14},{14,12},{16,18},{18,... | collective-permute-start | bytes 196616 | tf_op jit(solution)/shard_map/ppermute | solution.py:63
  70.6 1.5 %output_projection_got.3 = bf16[64,3072]{1,0:T(8,128)(2,1)} custom-call(s32[1]{0:T(128)} %bitcast.refs_0_, s32[1]{0:T(128)} %bitcast.1.refs_1_, f32[64,3072]{1,0:T(8,128)S(1)} %output_projection_mine.2.refs_2_, bf16[4,64,128]{2,1,0:T(8,128)(2,1)S(1)} %collective-permute-done.16.refs_3_, bf16[7,128,128]{2,1,0:T(8,128)(2,1)S(1)} %get-tuple-element.36.refs_10_.refs_4_, ...), custom_call_target="tpu_custom_call" | custom-call | flops 1 | bytes 1 | tf_op jit(solution)/shard_map/output_projection_got/pallas_call | solution.py:78
  (41 shorter events, 6.6 us)
Async XLA Ops:
  1.7 3.6 %collective-permute-start = (bf16[2,128,512]{2,1,0:T(8,128)(2,1)S(1)}, bf16[2,128,512]{2,1,0:T(8,128)(2,1)S(1)}, u32[]{:S(2)}, u32[]{:S(2)}) collective-permute-start(bf16[2,128,512]{2,1,0:T(8,128)(2,1)S(1)} %get-tuple-element.55), channel_id=1, source_target_pairs={{0,2},{2,0},{4,6},{6,4},{8,10},{10,8},{12,14},{14,12},{16,18},{18,... | collective-permute-start | bytes 786440 | tf_op jit(solution)/shard_map/ppermute | solution.py:63
  3.2 13.9 %collective-permute-start.1 = (bf16[64,3072]{1,0:T(8,128)(2,1)}, bf16[64,3072]{1,0:T(8,128)(2,1)S(1)}, u32[]{:S(2)}, u32[]{:S(2)}) collective-permute-start(bf16[64,3072]{1,0:T(8,128)(2,1)} %refs_1_.2), channel_id=1, source_target_pairs={{0,1},{1,0},{2,3},{3,2},{4,5},{5,4},{6,7},{7,6},{8,9},{9,8},{10,11... | collective-permute-start | bytes 1179656 | tf_op jit(solution)/shard_map/ppermute | solution.py:67
  5.3 14.7 %collective-permute-start.3 = (bf16[2,256,512]{2,1,0:T(8,128)(2,1)S(1)}, bf16[2,256,512]{2,1,0:T(8,128)(2,1)S(1)}, u32[]{:S(2)}, u32[]{:S(2)}) collective-permute-start(bf16[2,256,512]{2,1,0:T(8,128)(2,1)S(1)} %pad_maximum_fusion.refs_4_.refs_6_), channel_id=1, source_target_pairs={{0,32},{2,6},{4,36},{6,10},{8,40},{10,14},{12,44},{14,2},{16,48},{... | collective-permute-start | bytes 1572872 | tf_op jit(solution)/shard_map/ppermute | solution.py:63
  7.0 13.9 %collective-permute-start.4 = (bf16[2,256,512]{2,1,0:T(8,128)(2,1)S(1)}, bf16[2,256,512]{2,1,0:T(8,128)(2,1)S(1)}, u32[]{:S(2)}, u32[]{:S(2)}) collective-permute-start(bf16[2,256,512]{2,1,0:T(8,128)(2,1)S(1)} %pad_maximum_fusion.refs_4_.refs_6_), channel_id=1, source_target_pairs={{0,96},{2,14},{4,100},{6,2},{8,104},{10,6},{12,108},{14,10},{16,11... | collective-permute-start | bytes 1572872 | tf_op jit(solution)/shard_map/ppermute | solution.py:63
  9.3 16.0 %collective-permute-start.8 = (bf16[2,256,512]{2,1,0:T(8,128)(2,1)S(1)}, bf16[2,256,512]{2,1,0:T(8,128)(2,1)S(1)}, u32[]{:S(2)}, u32[]{:S(2)}) collective-permute-start(bf16[2,256,512]{2,1,0:T(8,128)(2,1)S(1)} %pad_maximum_fusion.refs_4_.refs_6_), channel_id=1, source_target_pairs={{0,64},{2,10},{4,68},{6,14},{8,72},{10,2},{12,76},{14,6},{16,80},{... | collective-permute-start | bytes 1572872 | tf_op jit(solution)/shard_map/ppermute | solution.py:63
  10.6 20.1 %collective-permute-start.9 = (bf16[2,256,512]{2,1,0:T(8,128)(2,1)S(1)}, bf16[2,256,512]{2,1,0:T(8,128)(2,1)S(1)}, u32[]{:S(2)}, u32[]{:S(2)}) collective-permute-start(bf16[2,256,512]{2,1,0:T(8,128)(2,1)S(1)} %pad_maximum_fusion.refs_4_.refs_6_), channel_id=1, source_target_pairs={{0,16},{2,18},{4,20},{6,22},{8,24},{10,26},{12,28},{14,30},{16,0},... | collective-permute-start | bytes 1572872 | tf_op jit(solution)/shard_map/ppermute | solution.py:63
  14.2 13.7 %copy-start = (bf16[3072,3,896]{2,0,1:T(8,128)(2,1)S(1)}, bf16[3072,3,896]{2,0,1:T(8,128)(2,1)}, u32[]{:S(2)}) copy-start(bf16[3072,3,896]{2,0,1:T(8,128)(2,1)} %param.12) | copy-start | bytes 49545220
  18.4 1.6 %collective-permute-start.2 = (bf16[3,128,128]{2,1,0:T(8,128)(2,1)S(1)}, bf16[3,128,128]{2,1,0:T(8,128)(2,1)S(1)}, u32[]{:S(2)}, u32[]{:S(2)}) collective-permute-start(bf16[3,128,128]{2,1,0:T(8,128)(2,1)S(1)} %get-tuple-element.32), channel_id=1, source_target_pairs={{0,2},{2,0},{4,6},{6,4},{8,10},{10,8},{12,14},{14,12},{16,18},{18,... | collective-permute-start | bytes 294920 | tf_op jit(solution)/shard_map/ppermute | solution.py:63
  21.0 9.6 %collective-permute-start.5 = (bf16[7,128,128]{2,1,0:T(8,128)(2,1)S(1)}, bf16[7,128,128]{2,1,0:T(8,128)(2,1)S(1)}, u32[]{:S(2)}, u32[]{:S(2)}) collective-permute-start(bf16[7,128,128]{2,1,0:T(8,128)(2,1)S(1)} %join_units.1.refs_5_.refs_2_), channel_id=1, source_target_pairs={{0,4},{2,34},{4,8},{6,38},{8,12},{10,42},{12,0},{14,46},{16,20},{1... | collective-permute-start | bytes 688136 | tf_op jit(solution)/shard_map/ppermute | solution.py:63
  22.3 8.3 %collective-permute-start.6 = (bf16[7,128,128]{2,1,0:T(8,128)(2,1)S(1)}, bf16[7,128,128]{2,1,0:T(8,128)(2,1)S(1)}, u32[]{:S(2)}, u32[]{:S(2)}) collective-permute-start(bf16[7,128,128]{2,1,0:T(8,128)(2,1)S(1)} %join_units.1.refs_5_.refs_2_), channel_id=1, source_target_pairs={{0,12},{2,98},{4,0},{6,102},{8,4},{10,106},{12,8},{14,110},{16,28}... | collective-permute-start | bytes 688136 | tf_op jit(solution)/shard_map/ppermute | solution.py:63
  23.7 7.1 %collective-permute-start.7 = (bf16[7,128,128]{2,1,0:T(8,128)(2,1)S(1)}, bf16[7,128,128]{2,1,0:T(8,128)(2,1)S(1)}, u32[]{:S(2)}, u32[]{:S(2)}) collective-permute-start(bf16[7,128,128]{2,1,0:T(8,128)(2,1)S(1)} %join_units.1.refs_5_.refs_2_), channel_id=1, source_target_pairs={{0,8},{2,66},{4,12},{6,70},{8,0},{10,74},{12,4},{14,78},{16,24},{1... | collective-permute-start | bytes 688136 | tf_op jit(solution)/shard_map/ppermute | solution.py:63
  25.3 15.6 %collective-permute-start.12 = (bf16[2,256,512]{2,1,0:T(8,128)(2,1)S(1)}, bf16[2,256,512]{2,1,0:T(8,128)(2,1)S(1)}, u32[]{:S(2)}, u32[]{:S(2)}) collective-permute-start(bf16[2,256,512]{2,1,0:T(8,128)(2,1)S(1)} %collective-permute-done.8.refs_6_.refs_9_), channel_id=1, source_target_pairs={{0,16},{2,18},{4,20},{6,22},{8,24},{10,26},{12,28},{14,30},{16,0},... | collective-permute-start | bytes 1572872 | tf_op jit(solution)/shard_map/ppermute | solution.py:63
  27.9 7.1 %copy-start.1 = (bf16[2,512,896]{2,1,0:T(8,128)(2,1)S(1)}, bf16[2,512,896]{2,1,0:T(8,128)(2,1)}, u32[]{:S(2)}) copy-start(bf16[2,512,896]{2,1,0:T(8,128)(2,1)} %refs_1_.3) | copy-start | bytes 5505028
  30.9 10.3 %collective-permute-start.10 = (bf16[2,256,512]{2,1,0:T(8,128)(2,1)S(1)}, bf16[2,256,512]{2,1,0:T(8,128)(2,1)S(1)}, u32[]{:S(2)}, u32[]{:S(2)}) collective-permute-start(bf16[2,256,512]{2,1,0:T(8,128)(2,1)S(1)} %gate.1.refs_4_.refs_8_), channel_id=1, source_target_pairs={{0,32},{2,6},{4,36},{6,10},{8,40},{10,14},{12,44},{14,2},{16,48},{... | collective-permute-start | bytes 1572872 | tf_op jit(solution)/shard_map/ppermute | solution.py:63
  30.9 10.3 %collective-permute-start.11 = (bf16[2,256,512]{2,1,0:T(8,128)(2,1)S(1)}, bf16[2,256,512]{2,1,0:T(8,128)(2,1)S(1)}, u32[]{:S(2)}, u32[]{:S(2)}) collective-permute-start(bf16[2,256,512]{2,1,0:T(8,128)(2,1)S(1)} %gate.1.refs_4_.refs_8_), channel_id=1, source_target_pairs={{0,96},{2,14},{4,100},{6,2},{8,104},{10,6},{12,108},{14,10},{16,11... | collective-permute-start | bytes 1572872 | tf_op jit(solution)/shard_map/ppermute | solution.py:63
  36.2 20.8 %slice-start = ((s8[5505024]{0:T(1024)(128)(4,1)}), s8[4194304]{0:T(1024)(128)(4,1)S(1)}, s32[]{:S(2)}) async-start(s8[5505024]{0:T(1024)(128)(4,1)} %bitcast.5), calls=%async_computation | async-start | bytes 8388608
  41.2 15.8 %slice-start.1 = ((s8[5505024]{0:T(1024)(128)(4,1)}), s8[1310720]{0:T(1024)(128)(4,1)S(1)}, s32[]{:S(2)}) async-start(s8[5505024]{0:T(1024)(128)(4,1)} %bitcast.5), calls=%async_computation.1 | async-start | bytes 2621440
  43.8 7.1 %collective-permute-start.17 = (bf16[8,64,128]{2,1,0:T(8,128)(2,1)S(1)}, bf16[8,64,128]{2,1,0:T(8,128)(2,1)S(1)}, u32[]{:S(2)}, u32[]{:S(2)}) collective-permute-start(bf16[8,64,128]{2,1,0:T(8,128)(2,1)S(1)} %get-tuple-element.47), channel_id=1, source_target_pairs={{0,12},{2,98},{4,0},{6,102},{8,4},{10,106},{12,8},{14,110},{16,28}... | collective-permute-start | bytes 393224 | tf_op jit(solution)/shard_map/ppermute | solution.py:63
  45.6 6.4 %collective-permute-start.18 = (bf16[8,64,128]{2,1,0:T(8,128)(2,1)S(1)}, bf16[8,64,128]{2,1,0:T(8,128)(2,1)S(1)}, u32[]{:S(2)}, u32[]{:S(2)}) collective-permute-start(bf16[8,64,128]{2,1,0:T(8,128)(2,1)S(1)} %get-tuple-element.48), channel_id=1, source_target_pairs={{0,4},{2,34},{4,8},{6,38},{8,12},{10,42},{12,0},{14,46},{16,20},{1... | collective-permute-start | bytes 393224 | tf_op jit(solution)/shard_map/ppermute | solution.py:63
  45.6 6.4 %collective-permute-start.19 = (bf16[8,64,128]{2,1,0:T(8,128)(2,1)S(1)}, bf16[8,64,128]{2,1,0:T(8,128)(2,1)S(1)}, u32[]{:S(2)}, u32[]{:S(2)}) collective-permute-start(bf16[8,64,128]{2,1,0:T(8,128)(2,1)S(1)} %get-tuple-element.49), channel_id=1, source_target_pairs={{0,8},{2,66},{4,12},{6,70},{8,0},{10,74},{12,4},{14,78},{16,24},{1... | collective-permute-start | bytes 393224 | tf_op jit(solution)/shard_map/ppermute | solution.py:63
  52.6 5.3 %collective-permute-start.20 = (bf16[4,64,128]{2,1,0:T(8,128)(2,1)S(1)}, bf16[4,64,128]{2,1,0:T(8,128)(2,1)S(1)}, u32[]{:S(2)}, u32[]{:S(2)}) collective-permute-start(bf16[4,64,128]{2,1,0:T(8,128)(2,1)S(1)} %get-tuple-element.52), channel_id=1, source_target_pairs={{0,2},{2,0},{4,6},{6,4},{8,10},{10,8},{12,14},{14,12},{16,18},{18,... | collective-permute-start | bytes 196616 | tf_op jit(solution)/shard_map/ppermute | solution.py:63
  58.5 12.1 %collective-permute-start.21 = (bf16[64,3072]{1,0:T(8,128)(2,1)S(1)}, bf16[64,3072]{1,0:T(8,128)(2,1)S(1)}, u32[]{:S(2)}, u32[]{:S(2)}) collective-permute-start(bf16[64,3072]{1,0:T(8,128)(2,1)S(1)} %output_projection_got.2), channel_id=1, source_target_pairs={{0,1},{1,0},{2,3},{3,2},{4,5},{5,4},{6,7},{7,6},{8,9},{9,8},{10,11... | collective-permute-start | bytes 1179656 | tf_op jit(solution)/shard_map/ppermute | solution.py:67
  59.1 5.9 %collective-permute-start.13 = (bf16[8,64,128]{2,1,0:T(8,128)(2,1)S(1)}, bf16[8,64,128]{2,1,0:T(8,128)(2,1)S(1)}, u32[]{:S(2)}, u32[]{:S(2)}) collective-permute-start(bf16[8,64,128]{2,1,0:T(8,128)(2,1)S(1)} %get-tuple-element.40), channel_id=1, source_target_pairs={{0,8},{2,66},{4,12},{6,70},{8,0},{10,74},{12,4},{14,78},{16,24},{1... | collective-permute-start | bytes 393224 | tf_op jit(solution)/shard_map/ppermute | solution.py:63
  62.3 4.6 %collective-permute-start.14 = (bf16[8,64,128]{2,1,0:T(8,128)(2,1)S(1)}, bf16[8,64,128]{2,1,0:T(8,128)(2,1)S(1)}, u32[]{:S(2)}, u32[]{:S(2)}) collective-permute-start(bf16[8,64,128]{2,1,0:T(8,128)(2,1)S(1)} %get-tuple-element.41), channel_id=1, source_target_pairs={{0,12},{2,98},{4,0},{6,102},{8,4},{10,106},{12,8},{14,110},{16,28}... | collective-permute-start | bytes 393224 | tf_op jit(solution)/shard_map/ppermute | solution.py:63
  62.6 5.3 %collective-permute-start.15 = (bf16[8,64,128]{2,1,0:T(8,128)(2,1)S(1)}, bf16[8,64,128]{2,1,0:T(8,128)(2,1)S(1)}, u32[]{:S(2)}, u32[]{:S(2)}) collective-permute-start(bf16[8,64,128]{2,1,0:T(8,128)(2,1)S(1)} %get-tuple-element.42), channel_id=1, source_target_pairs={{0,4},{2,34},{4,8},{6,38},{8,12},{10,42},{12,0},{14,46},{16,20},{1... | collective-permute-start | bytes 393224 | tf_op jit(solution)/shard_map/ppermute | solution.py:63
  68.4 2.2 %collective-permute-start.16 = (bf16[4,64,128]{2,1,0:T(8,128)(2,1)S(1)}, bf16[4,64,128]{2,1,0:T(8,128)(2,1)S(1)}, u32[]{:S(2)}, u32[]{:S(2)}) collective-permute-start(bf16[4,64,128]{2,1,0:T(8,128)(2,1)S(1)} %get-tuple-element.46), channel_id=1, source_target_pairs={{0,2},{2,0},{4,6},{6,4},{8,10},{10,8},{12,14},{14,12},{16,18},{18,... | collective-permute-start | bytes 196616 | tf_op jit(solution)/shard_map/ppermute | solution.py:63
